TPU v7x, 32 devices: a whole 2x2x4 slice. The times are simulated.
32 devices in a mesh: tensor: 4 (over x, core), dp: 8 (over z, y).
Axes of the slice: x: 2, y: 2, z: 4, core: 2. Of those that a mesh axis runs over, the one named last changes fastest.
Arguments:
- inputs: bfloat16 [16384, 768], P('dp'), may hold values from -6 to 6
- gain_attn: bfloat16 [768], replicated, may hold values from 0.25 to 1.75
- w_qkv: bfloat16 [3, 768, 768], P(None, None, 'tensor'), may hold values from -0.21875 to 0.21875
- w_out: bfloat16 [768, 768], P('tensor'), may hold values from -0.875 to 0.875
- gain_ffn: bfloat16 [768], replicated, may hold values from 0.25 to 1.75
- w_in: bfloat16 [768, 3072], P(None, 'tensor'), may hold values from -0.21875 to 0.21875
- w_back: bfloat16 [3072, 768], P('tensor'), may hold values from -0.109375 to 0.109375
- bias_table: bfloat16 [32, 12], P(None, 'tensor'), may hold values from -4 to 4
- lengths: int32 [32], P('dp'), may hold values from 51 to 512, as said below
- buckets: int32 [512, 512], replicated, may hold values from 0 to 31, as said below
- cotangent: bfloat16 [16384, 768], P('dp'), may hold values from -6 to 6
Outputs:
- mixed: bfloat16 [16384, 768], P('dp')
- grad_input: float32 [16384, 768], P('dp')
- grad_gain_attn: float32 [768], replicated
- grad_w_qkv: float32 [3, 768, 768], P(None, None, 'tensor')
- grad_w_out: float32 [768, 768], P('tensor')
- grad_gain_ffn: float32 [768], replicated
- grad_w_in: float32 [768, 3072], P(None, 'tensor')
- grad_w_back: float32 [3072, 768], P('tensor')
- grad_bias_table: float32 [32, 12], P(None, 'tensor')
Inputs may be any that keep to these rules, and one draw needn't show every extreme that they name: `lengths`: every group of 4 consecutive documents holds one of 512 tokens. `buckets`: a function of j - i alone, never falling as |j - i| grows on either side of zero; larger when j > i than for the same |j - i| with j < i.
All inputs are finite; a program needn't handle non-finite values.
Results may differ from a plain program's by a relative error of at most 0.012.
Values may be sent and summed in bfloat16 or wider, within the bound.
No kernel may reach another device: no remote copies, remote signals or barrier semaphores. Data moves between devices by JAX's collectives and lax.ppermute only.
A program may use at most 192 MiB of HBM per device.

v0:
```python
import math

import jax
import jax.numpy as jnp
from jax import lax
from jax.sharding import PartitionSpec as P

HD = 64


epsilon = 1e-06
masked_score = -1000000000.0
gelu_coeff = 0.7978845608028654


def rms_norm(values, gain_vec):
    return (
        values * lax.rsqrt(jnp.mean(values * values, axis=-1, keepdims=True) + epsilon) * gain_vec
    )


def gelu_tanh(values):
    return (
        0.5 * values * (1.0 + jnp.tanh(gelu_coeff * (values + 0.044715 * values * values * values)))
    )


def across(left, right):
    return lax.dot_general(
        left, right, (((0,), (0,)), ((), ())), preferred_element_type=jnp.float32
    )


def against(left, right):
    return lax.dot_general(
        left, right, (((1,), (1,)), ((), ())), preferred_element_type=jnp.float32
    )


def per_device(
    inputs, gain_attn, w_qkv, w_out, gain_ffn, w_in, w_back, bias_table, lengths, buckets, cotangent
):
    row_count = inputs.shape[0]
    seq_len = buckets.shape[0]
    doc_count = lengths.shape[0]
    bucket_count = bias_table.shape[0]
    heads_here = bias_table.shape[1]
    local_width = heads_here * HD
    score_scale = 1.0 / math.sqrt(HD)
    gain_one = gain_attn.astype(jnp.float32)
    gain_two = gain_ffn.astype(jnp.float32)
    source = inputs.astype(jnp.float32)
    normed = rms_norm(source, gain_one)
    normed_low = normed.astype(jnp.bfloat16)
    packed = jnp.einsum(
        "td,cde->cte", normed_low, w_qkv, preferred_element_type=jnp.float32
    ).astype(jnp.bfloat16)
    head_split = packed.reshape(3, doc_count, seq_len, heads_here, HD).transpose(0, 1, 3, 2, 4)
    one_hot = (buckets.reshape(1, -1) == jnp.arange(bucket_count)[:, None]).astype(jnp.bfloat16)
    relative = jnp.einsum(
        "bh,bn->hn", bias_table, one_hot, preferred_element_type=jnp.float32
    ).reshape(heads_here, seq_len, seq_len)
    positions = jnp.arange(seq_len)

    def masked_scores(doc_queries, doc_keys, doc_length):
        scores = (
            jnp.einsum("hqe,hke->hqk", doc_queries, doc_keys, preferred_element_type=jnp.float32)
            * score_scale
            + relative
        )
        return jnp.where(positions[None, None, :] < doc_length, scores, masked_score)

    mixed_list = []
    logsum_list = []
    for doc_index in range(doc_count):
        scores = masked_scores(
            head_split[0, doc_index], head_split[1, doc_index], lengths[doc_index]
        )
        top_score = jnp.max(scores, axis=-1, keepdims=True)
        shifted = jnp.exp(scores - top_score)
        row_total = jnp.sum(shifted, axis=-1, keepdims=True)
        weights = (shifted / row_total).astype(jnp.bfloat16)
        mixed_list.append(
            jnp.einsum(
                "hqk,hke->hqe",
                weights,
                head_split[2, doc_index],
                preferred_element_type=jnp.float32,
            )
        )
        logsum_list.append(top_score + jnp.log(row_total))
    attended = (
        jnp.stack(mixed_list)
        .transpose(0, 2, 1, 3)
        .reshape(row_count, local_width)
        .astype(jnp.bfloat16)
    )
    attn_terms = jnp.dot(attended, w_out, preferred_element_type=jnp.float32)
    middle = source + lax.psum(attn_terms, "tensor")
    normed_two, pull_ffn_norm = jax.vjp(rms_norm, middle, gain_two)
    normed_second = normed_two.astype(jnp.bfloat16)
    hidden_full, pull_gelu = jax.vjp(
        gelu_tanh, jnp.dot(normed_second, w_in, preferred_element_type=jnp.float32)
    )
    hidden_low = hidden_full.astype(jnp.bfloat16)
    ffn_terms = jnp.dot(hidden_low, w_back, preferred_element_type=jnp.float32)
    output = (middle + lax.psum(ffn_terms, "tensor")).astype(jnp.bfloat16)
    grad_w_back = across(hidden_low, cotangent)
    grad_pre = pull_gelu(against(cotangent, w_back))[0].astype(jnp.bfloat16)
    grad_w_in = across(normed_second, grad_pre)
    grad_norm_terms = against(grad_pre, w_in)
    grad_middle_norm, grad_gain_ffn = pull_ffn_norm(lax.psum(grad_norm_terms, "tensor"))
    grad_middle = cotangent.astype(jnp.float32) + grad_middle_norm
    middle_low = grad_middle.astype(jnp.bfloat16)
    grad_w_out = across(attended, middle_low)
    grad_attended = against(middle_low, w_out).astype(jnp.bfloat16)
    grad_heads = grad_attended.reshape(doc_count, seq_len, heads_here, HD).transpose(0, 2, 1, 3)
    grad_table = jnp.zeros((bucket_count, heads_here), jnp.float32)
    grad_list = []
    for doc_index in range(doc_count):
        doc_queries = head_split[0, doc_index]
        doc_keys = head_split[1, doc_index]
        doc_values = head_split[2, doc_index]
        scores = masked_scores(doc_queries, doc_keys, lengths[doc_index])
        softmax_probs = jnp.exp(scores - logsum_list[doc_index])
        grad_out = grad_heads[doc_index]
        grad_probs = jnp.einsum(
            "hqe,hke->hqk", grad_out, doc_values, preferred_element_type=jnp.float32
        )
        grad_scores = (
            softmax_probs
            * (grad_probs - jnp.sum(grad_probs * softmax_probs, axis=-1, keepdims=True))
        ).astype(jnp.bfloat16)
        grad_table = grad_table + jnp.einsum(
            "bn,hn->bh",
            one_hot,
            grad_scores.reshape(heads_here, seq_len * seq_len),
            preferred_element_type=jnp.float32,
        )
        grad_query = (
            jnp.einsum("hqk,hke->hqe", grad_scores, doc_keys, preferred_element_type=jnp.float32)
            * score_scale
        )
        grad_key = (
            jnp.einsum("hqk,hqe->hke", grad_scores, doc_queries, preferred_element_type=jnp.float32)
            * score_scale
        )
        grad_value = jnp.einsum(
            "hqk,hqe->hke",
            softmax_probs.astype(jnp.bfloat16),
            grad_out,
            preferred_element_type=jnp.float32,
        )
        grad_list.append(jnp.stack([grad_query, grad_key, grad_value]))
    grad_packed = (
        jnp.stack(grad_list, axis=1)
        .transpose(0, 1, 3, 2, 4)
        .reshape(3, row_count, local_width)
        .astype(jnp.bfloat16)
    )
    grad_w_qkv = jnp.einsum(
        "td,cte->cde", normed_low, grad_packed, preferred_element_type=jnp.float32
    )
    attn_back_terms = jnp.einsum(
        "cte,cde->td", grad_packed, w_qkv, preferred_element_type=jnp.float32
    )
    normed_again, pull_attn_norm = jax.vjp(rms_norm, source, gain_one)
    grad_source_norm, grad_gain_attn = pull_attn_norm(lax.psum(attn_back_terms, "tensor"))
    grad_input = grad_middle + grad_source_norm
    grad_gain_attn, grad_w_qkv, grad_w_out, grad_gain_ffn, grad_w_in, grad_w_back, grad_table = (
        lax.psum(
            (
                grad_gain_attn,
                grad_w_qkv,
                grad_w_out,
                grad_gain_ffn,
                grad_w_in,
                grad_w_back,
                grad_table,
            ),
            "dp",
        )
    )
    return (
        output,
        grad_input,
        grad_gain_attn,
        grad_w_qkv,
        grad_w_out,
        grad_gain_ffn,
        grad_w_in,
        grad_w_back,
        grad_table,
    )


def solution(mesh):
    return jax.shard_map(
        per_device,
        mesh=mesh,
        in_specs=(
            P("dp", None),
            P(),
            P(None, None, "tensor"),
            P("tensor", None),
            P(),
            P(None, "tensor"),
            P("tensor", None),
            P(None, "tensor"),
            P("dp"),
            P(),
            P("dp", None),
        ),
        out_specs=(
            P("dp", None),
            P("dp", None),
            P(),
            P(None, None, "tensor"),
            P("tensor", None),
            P(),
            P(None, "tensor"),
            P("tensor", None),
            P(None, "tensor"),
        ),
        check_vma=False,
    )
```

profile of v0, /device:TPU:0, one launch (start us, length us, event | category | flops | bytes accessed | tf_op | source)
XLA Modules:
  0.0 844.8 jit_solution(12696225435505745363)
XLA Ops:
  7.3 2.7 fusion.22
  10.1 3.3 fusion.108
  13.8 3.0 reshape.149
  16.8 2.3 copy.93
  19.4 5.1 fusion.4
  24.5 2.6 copy.92
  27.2 3.7 copy.39
  32.2 2.7 fusion.124
  36.6 1.0 iota_compare_fusion.14
  37.9 0.9 fusion.123
  41.1 0.9 fusion.122
  44.3 0.9 fusion.121
  47.9 0.9 copy-done.24
  48.8 3.7 fusion.125
  53.0 1.3 convert_element_type.101
  54.3 8.1 fusion.126
  62.4 112.6 %all-reduce.8.cloned.1.call-done = f32[2048,768]{1,0:T(8,128)} async-done(((f32[2048,768]{1,0:T(8,128)}), f32[2048,768]{1,0:T(8,128)}) %all-reduce.8.cloned.1.call-update) | async-done | bytes 6291472 | tf_op jit(solution)/shard_map/psum | solution.py:99
  175.0 4.7 multiply_reduce_fusion.2
  180.5 8.6 %fusion.17 = (bf16[2048,768]{1,0:T(8,128)(2,1)S(1)}, f32[2048,768]{1,0:T(8,128)}) fusion(f32[2048,768]{1,0:T(8,128)S(1)} %copy-done.74, bf16[768,768]{1,0:T(8,128)(2,1)S(1)} %copy-done, f32[2048,768]{1,0:T(8,128)S(1)} %get-tuple-element.23, f32[768]{0:T(1024)S(1)} %copy-done.58, f32[2048]{0:T(1024)S(1)} %fusion.115), kind=kOutput, calls=%fused_computation.29 | convolution fusion | flops 2458386432 | bytes 23211008 | tf_op jit(solution)/shard_map/dot_general | solution.py:103
  189.1 1.6 copy-done.75
  190.7 4.5 fusion.127
  196.0 9.6 %fusion.119 = f32[2048,768]{1,0:T(8,128)} fusion(bf16[768,768]{1,0:T(8,128)(2,1)} %param.17, f32[2048,768]{1,0:T(8,128)} %get-tuple-element.37), kind=kOutput, calls=%fused_computation.185 | convolution fusion | flops 2430074880 | bytes 13762560 | tf_op jit(solution)/shard_map/dot_general | solution.py:106
  205.6 109.6 %all-reduce.10.cloned.1.call-done = f32[2048,768]{1,0:T(8,128)} async-done(((f32[2048,768]{1,0:T(8,128)}), f32[2048,768]{1,0:T(8,128)}) %all-reduce.10.cloned.1.call-update) | async-done | bytes 6291472 | tf_op jit(solution)/shard_map/psum | solution.py:112
  315.2 6.2 multiply_reduce_fusion
  321.6 0.9 copy-done.30
  322.6 3.9 fusion.20
  326.5 2.7 copy-done.3
  329.1 1.2 convolution_convert_fusion
  330.4 1.5 reshape.151
  331.8 1.3 copy.94
  333.1 2.8 multiply_reduce_fusion.5
  335.9 0.9 multiply_convert_fusion.4
  340.6 0.9 multiply_convert_fusion.5
  344.6 0.9 multiply_convert_fusion.2
  348.7 0.8 multiply_convert_fusion.3
  351.7 3.6 copy.61
  355.4 5.9 convert_element_type.118
  361.3 7.0 convolution_bitcast_fusion
  369.0 8.1 fusion.116
  377.1 7.6 fusion.118
  384.8 1.7 fusion.45
  387.7 3.4 fusion.53
  391.1 1.6 copy.63
  392.7 2.7 copy.62
  395.5 1.6 copy.65
  397.0 2.9 copy.64
  399.9 2.7 copy.86
  402.7 1.4 copy.85
  404.0 2.7 copy.88
  406.7 2.7 copy.87
  409.4 6.8 fusion.2
  416.2 7.1 fusion
  423.3 7.2 fusion.1
  430.4 5.6 fusion.106
  436.1 153.7 %all-reduce.14.cloned.1.call-done = (f32[2048,768]{1,0:T(8,128)}, f32[2048,768]{1,0:T(8,128)}) async-done(((f32[2048,768]{1,0:T(8,128)}, f32[2048,768]{1,0:T(8,128)}), (f32[2048,768]{1,0:T(8,128)}, f32[2048,768]{1,0:T(8,128)})) %all-reduce.14.cloned.1.call-update) | async-done | bytes 12582928 | tf_op jit(solution)/shard_map/psum | solution.py:107
  589.7 5.0 fusion.13
  594.7 39.1 %all-reduce = (f32[768]{0:T(1024)}, f32[768]{0:T(1024)}, f32[32,3]{0,1:T(4,128)}) all-reduce(f32[768]{0:T(1024)S(1)} %get-tuple-element.11, f32[768]{0:T(1024)S(1)} %copy-done.69, f32[32,3]{0,1:T(4,128)S(1)} %fusion.106), channel_id=1, replica_groups=mesh['tensor'=4,'dp'=8] {'dp'}, use_global_device_ids=true, to_apply=%region_21.22 | all-reduce | flops 1632 | bytes 13056 | tf_op jit(solution)/shard_map/psum | solution.py:171
  633.8 7.4 add_convert_fusion
  642.0 1.9 copy-done.20
  644.0 3.5 fusion.21
  647.5 183.8 %all-reduce.12.cloned.1.call-done = (f32[3,768,192]{1,2,0:T(8,128)}, f32[192,768]{1,0:T(8,128)}, f32[768,768]{1,0:T(8,128)}, f32[768,768]{1,0:T(8,128)}) async-done(((f32[3,768,192]{1,2,0:T(8,128)}, f32[192,768]{1,0:T(8,128)}, f32[768,768]{1,0:T(8,128)}, f32[768,768]{1,0:T(8,128)}), (f32[3,768,192]{1,2,0:T(8,128)}, f32[192,768]{1,0:T(8,128)}, f32[768,768]{1,0:T(8,128)}, ...) | async-done | bytes 7077904 | tf_op jit(solution)/shard_map/psum | solution.py:171
  831.2 2.9 copy.103
  835.0 1.4 copy.105
  836.4 1.4 copy.106
  (210 shorter events, 29.2 us)
Async XLA Ops:
  7.2 172.6 %copy-start = (bf16[768,768]{1,0:T(8,128)(2,1)S(1)}, bf16[768,768]{1,0:T(8,128)(2,1)}, u32[]{:S(2)}) copy-start(bf16[768,768]{1,0:T(8,128)(2,1)} %param.16) | copy-start | bytes 3538948
  7.2 2.8 copy-start.71
  7.2 167.8 %all-reduce.8.cloned.1.call-start = ((), (), s32[]{:S(2)}) async-start(), calls=%async_computation | async-start | bytes 12582912 | tf_op jit(solution)/shard_map/psum | solution.py:99
  7.2 2.9 copy-start.13
  10.0 3.5 copy-start.49
  10.0 3.4 copy-start.51
  10.0 3.4 copy-start.56
  16.8 2.3 copy-start.37
  16.8 2.6 copy-start.73
  19.1 314.0 %copy-start.22 = (bf16[3,4,512,3,64]{2,4,3,1,0:T(8,128)(2,1)}, bf16[3,4,512,3,64]{2,4,3,1,0:T(8,128)(2,1)S(1)}, u32[]{:S(2)}) copy-start(bf16[3,4,512,3,64]{2,4,3,1,0:T(8,128)(2,1)S(1)} %copy.93) | copy-start | bytes 7077892
  19.4 5.1 copy-start.38
  27.2 3.8 copy-start.70
  34.9 1.7 copy-start.6
  35.4 2.5 copy-start.12
  42.0 1.7 copy-start.4
  45.2 1.7 copy-start.8
  45.2 1.7 copy-start.47
  46.9 1.8 copy-start.35
  52.5 262.6 %all-reduce.10.cloned.1.call-start = ((), (), s32[]{:S(2)}) async-start(), calls=%async_computation.1 | async-start | bytes 12582912 | tf_op jit(solution)/shard_map/psum | solution.py:112
  175.0 4.8 copy-start.58
  175.0 5.5 copy-start.74
  179.7 9.3 %copy-start.2 = (f32[2048,768]{1,0:T(8,128)}, f32[2048,768]{1,0:T(8,128)S(1)}, u32[]{:S(2)}) copy-start(f32[2048,768]{1,0:T(8,128)S(1)} %get-tuple-element.23) | copy-start | bytes 18874372
  179.7 9.3 %copy-start.43 = (f32[2048]{0:T(1024)}, f32[2048]{0:T(1024)S(1)}, u32[]{:S(2)}) copy-start(f32[2048]{0:T(1024)S(1)} %get-tuple-element.22) | copy-start | bytes 24580
  179.8 9.3 %copy-start.53 = (f32[2048]{0:T(1024)}, f32[2048]{0:T(1024)S(1)}, u32[]{:S(2)}) copy-start(f32[2048]{0:T(1024)S(1)} %fusion.115) | copy-start | bytes 24580
  195.2 394.5 %all-reduce.14.cloned.1.call-start = ((), (), s32[]{:S(2)}) async-start(), calls=%async_computation.3 | async-start | bytes 25165824 | tf_op jit(solution)/shard_map/psum | solution.py:107
  195.9 144.7 %copy-start.41 = (f32[3,512]{1,0:T(4,128)}, f32[3,512]{1,0:T(4,128)S(1)}, u32[]{:S(2)}) copy-start(f32[3,512]{1,0:T(4,128)S(1)} %log_add_fusion.3) | copy-start | bytes 18436
  196.0 119.2 %copy-start.54 = (f32[2048]{0:T(1024)S(1)}, f32[2048]{0:T(1024)}, u32[]{:S(2)}) copy-start(f32[2048]{0:T(1024)} %copy-done.53) | copy-start | bytes 24580
  196.0 119.2 %copy-start.59 = (f32[768]{0:T(1024)S(1)}, f32[768]{0:T(1024)}, u32[]{:S(2)}) copy-start(f32[768]{0:T(1024)} %convert_element_type.101) | copy-start | bytes 9220
  205.6 115.7 %copy-start.44 = (f32[2048]{0:T(1024)S(1)}, f32[2048]{0:T(1024)}, u32[]{:S(2)}) copy-start(f32[2048]{0:T(1024)} %copy-done.43) | copy-start | bytes 24580
  315.2 6.4 copy-start.21
  315.2 7.4 copy-start.30
  322.6 6.6 copy-start.36
  326.5 2.7 copy-start.3
  333.1 2.8 copy-start.11
  335.9 1.7 copy-start.23
  338.0 1.9 copy-start.7
  341.9 2.0 copy-start.9
  345.9 2.0 copy-start.5
  355.3 5.9 copy-start.72
  368.3 462.9 %all-reduce.12.cloned.1.call-start = ((), (), s32[]{:S(2)}) async-start(), calls=%async_computation.2 | async-start | bytes 14155776 | tf_op jit(solution)/shard_map/psum | solution.py:171
  369.0 8.1 copy-start.31
  369.0 15.7 %slice-start = ((s8[6291456]{0:T(1024)(128)(4,1)}), s8[2097152]{0:T(1024)(128)(4,1)S(1)}, s32[]{:S(2)}) async-start(s8[6291456]{0:T(1024)(128)(4,1)} %bitcast.220), calls=%async_computation.4 | async-start | bytes 4194304
  377.1 7.6 slice-start.1
  377.1 7.7 copy-start.25
  384.7 2.1 copy-start.14
  384.8 2.9 copy-start.34
  384.8 2.9 copy-start.52
  384.8 2.9 copy-start.57
  392.7 2.7 copy-start.18
  397.0 2.9 copy-start.26
  399.9 2.7 copy-start.27
  399.9 4.1 copy-start.28
  402.6 4.0 copy-start.29
  404.0 5.4 copy-start.39
  589.7 5.0 copy-start.69
  589.7 44.1 %copy-start.50 = (f32[2048]{0:T(1024)S(1)}, f32[2048]{0:T(1024)}, u32[]{:S(2)}) copy-start(f32[2048]{0:T(1024)} %copy-done.49) | copy-start | bytes 24580
  589.7 51.5 %slice-start.2 = ((s8[6291456]{0:T(1024)(128)(4,1)}), s8[2097152]{0:T(1024)(128)(4,1)S(1)}, s32[]{:S(2)}) async-start(s8[6291456]{0:T(1024)(128)(4,1)} %bitcast.222), calls=%async_computation.6 | async-start | bytes 4194304
  633.8 7.4 slice-start.3
  633.8 8.2 copy-start.15
  633.8 10.1 %copy-start.20 = (f32[2048,768]{1,0:T(8,128)S(1)}, f32[2048,768]{1,0:T(8,128)}, u32[]{:S(2)}) copy-start(f32[2048,768]{1,0:T(8,128)} %get-tuple-element.21) | copy-start | bytes 18874372
  831.2 3.0 copy-start.40
  831.2 3.8 copy-start.33
  834.2 2.2 copy-start.32
  835.0 2.8 copy-start.1
  (20 other events, 22.4 us)
Sparse Core Ops, SparseCore 0:
  52.7 122.2 all-reduce.7
  195.4 119.7 all-reduce.9
  368.5 221.2 all-reduce.13
  594.6 236.6 all-reduce.11
where the time goes:
time: 852 us; the launch traced here: 845 us
  waiting for transfers between devices  560 us (66%)
  matrix products  118 us (14%)
  local copies, waits for them, and re-layouts  68.5 us (8%)
  other arithmetic  43.9 us (5%)
  blocking collectives  39.1 us (5%)
  between operations  15.2 us (2%)
    psum x1, waiting for transfers between devices, per_device(): lax.psum((grad_gain_attn, grad_w_qkv, grad_w_out, grad_gain_ffn, grad_w_i...  184 us
    psum x1, waiting for transfers between devices, per_device(): output = (middle + lax.psum(ffn_terms, 'tensor')).astype(jnp.bfloat16)  154 us
    psum x1, waiting for transfers between devices, per_device(): middle = source + lax.psum(attn_terms, 'tensor')  113 us
    psum x1, waiting for transfers between devices, per_device(): lax.psum(grad_norm_terms, 'tensor')  110 us
    psum x1, blocking collectives, per_device(): lax.psum((grad_gain_attn, grad_w_qkv, grad_w_out, grad_gain_ffn, grad_w_i...  39.1 us
    unnamed x171, local copies, waits for them, and re-layouts  37.2 us
    dot_general x4, matrix products, per_device(): jnp.einsum('bn,hn->bh', one_hot, grad_scores.reshape(heads_here, seq_len...  26.7 us
    dot_general x3, matrix products, across(): lax.dot_general(left, right, (((0,), (0,)), ((), ())), preferred_element_...  17.4 us
  transfers between devices with their start and end apart: 4, of which 4 were waited for; matrix products, arithmetic and copies ran while one was open for 12% of the time, Pallas kernels for 0%

commit v1 on v0

v1 whole, which is shorter than its diff:
```python
import functools
import math

import jax
import jax.numpy as jnp
from jax import lax
from jax.experimental import pallas as pl
from jax.experimental.pallas import tpu as pltpu
from jax.sharding import PartitionSpec as P

HD = 64
PAIR = 2 * HD
EPS = 1e-06
MASKED = -1000000000.0
GELU_C = 0.7978845608028654
GELU_A = 0.044715
VMEM_BYTES = 60 * 1024 * 1024

F32 = jnp.float32
BF16 = jnp.bfloat16


def dot_nn(a, b):
    return lax.dot_general(a, b, (((1,), (0,)), ((), ())), preferred_element_type=F32)


def dot_nt(a, b):
    return lax.dot_general(a, b, (((1,), (1,)), ((), ())), preferred_element_type=F32)


def dot_tn(a, b):
    return lax.dot_general(a, b, (((0,), (0,)), ((), ())), preferred_element_type=F32)


def params():
    return pltpu.CompilerParams(vmem_limit_bytes=VMEM_BYTES)


def whole(shape):
    return pl.BlockSpec(shape, lambda *_: (0,) * len(shape))


def norm_kernel(src_ref, gain_ref, out_ref):
    v = src_ref[...].astype(F32)
    r = lax.rsqrt(jnp.mean(v * v, axis=-1, keepdims=True) + EPS)
    out_ref[...] = (v * r * gain_ref[...]).astype(BF16)


def norm_rows(src, gain):
    rows, width = src.shape
    return pl.pallas_call(
        norm_kernel,
        grid=(4,),
        in_specs=[pl.BlockSpec((rows // 4, width), lambda i: (i, 0)), whole((1, width))],
        out_specs=pl.BlockSpec((rows // 4, width), lambda i: (i, 0)),
        out_shape=jax.ShapeDtypeStruct((rows, width), BF16),
        compiler_params=params(),
        name="norm_rows",
    )(src, gain)


def attn_fwd_kernel(docs, seq, len_ref, normed_ref, w_ref, u_ref, packed_ref, probs_ref, att_ref):
    packed = dot_nn(normed_ref[...], w_ref[:, : 3 * PAIR])
    lane = lax.broadcasted_iota(jnp.int32, (seq, PAIR), 1)
    scale = 1.0 / math.sqrt(HD)
    packed_ref[:, :PAIR] = (packed[:, :PAIR].astype(BF16).astype(F32) * scale).astype(BF16)
    packed_ref[:, PAIR:] = packed[:, PAIR:].astype(BF16)
    key_pos = lax.broadcasted_iota(jnp.int32, (seq, 1), 0)
    for head in range(2):
        row = jnp.broadcast_to(u_ref[0, head : head + 1, :], (seq, 2 * seq))
        rel = pltpu.roll(row, 0, 1, stride=1, stride_axis=0)[:, :seq]
        mine = (lane >= HD) if head else (lane < HD)
        for doc in range(docs):
            rows = slice(doc * seq, (doc + 1) * seq)
            q = packed_ref[rows, :PAIR]
            k = packed_ref[rows, PAIR : 2 * PAIR]
            v = packed_ref[rows, 2 * PAIR :]
            k = jnp.where(mine, k, jnp.zeros_like(k))
            scores = dot_nt(k, q) + rel
            scores = jnp.where(key_pos < len_ref[doc], scores, MASKED)
            top = jnp.max(scores, axis=0, keepdims=True)
            e = jnp.exp(scores - top)
            total = jnp.sum(e, axis=0, keepdims=True)
            p = (e * (1.0 / total)).astype(BF16)
            probs_ref[doc, head] = p
            vt = v.T[head * HD : (head + 1) * HD, :]
            o = dot_nn(vt, p)
            att_ref[rows, head * HD : (head + 1) * HD] = o.T.astype(BF16)


def attn_fwd(normed, w_half, u_half, lengths, docs, seq):
    rows, width = normed.shape
    pairs = u_half.shape[0]
    return pl.pallas_call(
        functools.partial(attn_fwd_kernel, docs, seq),
        grid=(pairs,),
        in_specs=[
            pl.BlockSpec(memory_space=pltpu.SMEM),
            whole((rows, width)),
            pl.BlockSpec((width, 4 * PAIR), lambda p: (0, p)),
            pl.BlockSpec((1, 2, 2 * seq), lambda p: (p, 0, 0)),
        ],
        out_specs=[
            pl.BlockSpec((rows, 3 * PAIR), lambda p: (0, p)),
            pl.BlockSpec((docs, 2, seq, seq), lambda p: (0, p, 0, 0)),
            pl.BlockSpec((rows, PAIR), lambda p: (0, p)),
        ],
        out_shape=[
            jax.ShapeDtypeStruct((rows, pairs * 3 * PAIR), BF16),
            jax.ShapeDtypeStruct((docs, 2 * pairs, seq, seq), BF16),
            jax.ShapeDtypeStruct((rows, pairs * PAIR), BF16),
        ],
        compiler_params=params(),
        name="attn_fwd",
    )(lengths, normed, w_half, u_half)


def fold_diagonals(g, seq):
    g = jnp.concatenate([g, jnp.zeros_like(g)], axis=1)
    n = seq
    while n > 8:
        n //= 2
        g = g[:n] + pltpu.roll(g[n:], 2 * seq - n, 1)
    while n > 1:
        n //= 2
        g = g[:n] + jnp.concatenate([g[n:, n:], g[n:, :n]], axis=1)
    return g


def attn_bwd_kernel(docs, seq, packed_ref, probs_ref, dout_ref, gp_ref, diag_ref):
    lane = lax.broadcasted_iota(jnp.int32, (seq, PAIR), 1)
    scale = 1.0 / math.sqrt(HD)
    sums = [None, None]
    for doc in range(docs):
        rows = slice(doc * seq, (doc + 1) * seq)
        q = packed_ref[rows, :PAIR]
        k = packed_ref[rows, PAIR : 2 * PAIR]
        v = packed_ref[rows, 2 * PAIR :]
        do = dout_ref[rows, :]
        kt = k.T
        dqs, dks, dvs = [], [], []
        for head in range(2):
            mine = (lane >= HD) if head else (lane < HD)
            vm = jnp.where(mine, v, jnp.zeros_like(v))
            dp = dot_nt(vm, do)
            p_low = probs_ref[doc, head]
            p = p_low.astype(F32)
            mean = jnp.sum(dp * p, axis=0, keepdims=True)
            ds = (p * (dp - mean)).astype(BF16)
            ds32 = ds.astype(F32)
            sums[head] = ds32 if sums[head] is None else sums[head] + ds32
            dvs.append(dot_nn(p_low, do))
            dks.append(dot_nn(ds, q))
            dqs.append(dot_nn(kt[head * HD : (head + 1) * HD, :], ds))
        dq = jnp.concatenate(dqs, axis=0).T * scale
        first = lane < HD
        gp_ref[rows, :PAIR] = dq.astype(BF16)
        gp_ref[rows, PAIR : 2 * PAIR] = jnp.where(first, dks[0], dks[1]).astype(BF16)
        gp_ref[rows, 2 * PAIR :] = jnp.where(first, dvs[0], dvs[1]).astype(BF16)
    for head in range(2):
        diag_ref[0, head : head + 1, :] = fold_diagonals(sums[head], seq)


def attn_bwd(packed, probs, dout, docs, seq):
    rows = packed.shape[0]
    pairs = packed.shape[1] // (3 * PAIR)
    return pl.pallas_call(
        functools.partial(attn_bwd_kernel, docs, seq),
        grid=(pairs,),
        in_specs=[
            pl.BlockSpec((rows, 3 * PAIR), lambda p: (0, p)),
            pl.BlockSpec((docs, 2, seq, seq), lambda p: (0, p, 0, 0)),
            pl.BlockSpec((rows, PAIR), lambda p: (0, p)),
        ],
        out_specs=[
            pl.BlockSpec((rows, 3 * PAIR), lambda p: (0, p)),
            pl.BlockSpec((1, 2, 2 * seq), lambda p: (p, 0, 0)),
        ],
        out_shape=[
            jax.ShapeDtypeStruct((rows, pairs * 3 * PAIR), BF16),
            jax.ShapeDtypeStruct((pairs, 2, 2 * seq), F32),
        ],
        compiler_params=params(),
        name="attn_bwd",
    )(packed, probs, dout)


CHUNK = 256


def out_proj_weight(w_ref):
    pairs = w_ref.shape[1] // (4 * PAIR)
    return jnp.concatenate(
        [w_ref[:, (4 * p + 3) * PAIR : (4 * p + 4) * PAIR] for p in range(pairs)], axis=1
    )


def ffn_half(step, normed_ref, cot_ref, w_in, w_back, acc_ref, gacc_ref, hid_ref, gpre_ref):
    rows = normed_ref.shape[0]
    for start in range(0, rows, CHUNK):
        at = slice(start, start + CHUNK)
        pre = dot_nn(normed_ref[at, :], w_in)
        ghid = dot_nt(cot_ref[at, :], w_back)
        sq = pre * pre
        t = jnp.tanh(GELU_C * (pre + GELU_A * sq * pre))
        half_t = 0.5 * (1.0 + t)
        hidden = (pre * half_t).astype(BF16)
        slope = half_t + 0.5 * pre * (1.0 - t * t) * (GELU_C * (1.0 + 3.0 * GELU_A * sq))
        gpre = (ghid * slope).astype(BF16)
        out = dot_nn(hidden, w_back)
        gnorm = dot_nt(gpre, w_in)
        if hid_ref is not None:
            hid_ref[at, :] = hidden
            gpre_ref[at, :] = gpre

        @pl.when(step == 0)
        def _():
            acc_ref[at, :] = out
            gacc_ref[at, :] = gnorm

        @pl.when(step != 0)
        def _():
            acc_ref[at, :] += out
            gacc_ref[at, :] += gnorm


def ffn_a_kernel(
    src_ref,
    att_own_ref,
    att_oth_ref,
    wa_own_ref,
    wa_oth_ref,
    gain_ref,
    cot_ref,
    in_a_ref,
    in_b_ref,
    back_a_ref,
    back_b_ref,
    middle_ref,
    normed_ref,
    acc_ref,
    gacc_ref,
    gback_ref,
    gin_ref,
    hid_ref,
    gpre_ref,
):
    step = pl.program_id(0)
    rows = src_ref.shape[0]

    @pl.when(step == 0)
    def _():
        wo_own = out_proj_weight(wa_own_ref)
        wo_oth = out_proj_weight(wa_oth_ref)
        for start in range(0, rows, CHUNK):
            at = slice(start, start + CHUNK)
            terms = dot_nt(att_own_ref[at, :], wo_own) + dot_nt(att_oth_ref[at, :], wo_oth)
            m = src_ref[at, :].astype(F32) + terms
            r = lax.rsqrt(jnp.mean(m * m, axis=-1, keepdims=True) + EPS)
            middle_ref[at, :] = m
            normed_ref[at, :] = (m * r * gain_ref[...]).astype(BF16)

    w_in = jnp.where(step == 0, in_a_ref[...], in_b_ref[...])
    w_back = jnp.where(step == 0, back_a_ref[...], back_b_ref[...])
    ffn_half(step, normed_ref, cot_ref, w_in, w_back, acc_ref, gacc_ref, hid_ref, gpre_ref)
    gback_ref[0] = dot_tn(hid_ref[...], cot_ref[...]).astype(BF16)
    gin_ref[0] = dot_tn(normed_ref[...], gpre_ref[...]).astype(BF16)


def ffn_a(src, att_own, att_oth, wa_own, wa_oth, gain, cot, in_a, in_b, back_a, back_b):
    rows, width = src.shape
    units = in_a.shape[1]
    args = (src, att_own, att_oth, wa_own, wa_oth, gain, cot, in_a, in_b, back_a, back_b)
    return pl.pallas_call(
        ffn_a_kernel,
        grid=(2,),
        in_specs=[whole(a.shape) for a in args],
        out_specs=[
            whole((rows, width)),
            whole((rows, width)),
            whole((rows, width)),
            whole((rows, width)),
            pl.BlockSpec((1, units, width), lambda i: (i, 0, 0)),
            pl.BlockSpec((1, width, units), lambda i: (i, 0, 0)),
        ],
        out_shape=[
            jax.ShapeDtypeStruct((rows, width), F32),
            jax.ShapeDtypeStruct((rows, width), BF16),
            jax.ShapeDtypeStruct((rows, width), F32),
            jax.ShapeDtypeStruct((rows, width), F32),
            jax.ShapeDtypeStruct((2, units, width), BF16),
            jax.ShapeDtypeStruct((2, width, units), BF16),
        ],
        scratch_shapes=[pltpu.VMEM((rows, units), BF16), pltpu.VMEM((rows, units), BF16)],
        compiler_params=params(),
        name="ffn_a",
    )(*args)


def ffn_b_kernel(
    middle_ref,
    normed_ref,
    acc_a_ref,
    gacc_a_ref,
    att_own_ref,
    wa_own_ref,
    wa_oth_ref,
    gain_ref,
    cot_ref,
    in_a_ref,
    in_b_ref,
    back_a_ref,
    back_b_ref,
    mixed_ref,
    gmid_ref,
    ggain_ref,
    gwout_ref,
    do_own_ref,
    do_oth_ref,
    acc_ref,
    gacc_ref,
    low_ref,
):
    step = pl.program_id(0)
    rows = middle_ref.shape[0]
    w_in = jnp.where(step == 0, in_a_ref[...], in_b_ref[...])
    w_back = jnp.where(step == 0, back_a_ref[...], back_b_ref[...])
    ffn_half(step, normed_ref, cot_ref, w_in, w_back, acc_ref, gacc_ref, None, None)

    @pl.when(step == 1)
    def _():
        wo_own = out_proj_weight(wa_own_ref)
        wo_oth = out_proj_weight(wa_oth_ref)
        ggain = jnp.zeros(ggain_ref.shape, F32)
        for start in range(0, rows, CHUNK):
            at = slice(start, start + CHUNK)
            m = middle_ref[at, :]
            mixed_ref[at, :] = (m + (acc_a_ref[at, :] + acc_ref[at, :])).astype(BF16)
            gnorm = gacc_a_ref[at, :] + gacc_ref[at, :]
            r = lax.rsqrt(jnp.mean(m * m, axis=-1, keepdims=True) + EPS)
            ggain = ggain + jnp.sum(gnorm * m * r, axis=0, keepdims=True)
            back = gain_ref[...] * gnorm
            inner = jnp.mean(back * m, axis=-1, keepdims=True)
            gm = cot_ref[at, :].astype(F32) + r * back - m * (r * r * r * inner)
            gmid_ref[at, :] = gm
            low = gm.astype(BF16)
            low_ref[at, :] = low
            do_own_ref[at, :] = dot_nn(low, wo_own).astype(BF16)
            do_oth_ref[at, :] = dot_nn(low, wo_oth).astype(BF16)
        ggain_ref[...] = ggain
        gwout_ref[...] = dot_tn(att_own_ref[...], low_ref[...]).astype(BF16)


def ffn_b(middle, normed, acc_a, gacc_a, att_own, wa_own, wa_oth, gain, cot, in_a, in_b, back_a, back_b):
    rows, width = middle.shape
    half = att_own.shape[1]
    args = (middle, normed, acc_a, gacc_a, att_own, wa_own, wa_oth, gain, cot, in_a, in_b, back_a, back_b)
    outs = [
        jax.ShapeDtypeStruct((rows, width), BF16),
        jax.ShapeDtypeStruct((rows, width), F32),
        jax.ShapeDtypeStruct((1, width), F32),
        jax.ShapeDtypeStruct((half, width), BF16),
        jax.ShapeDtypeStruct((rows, half), BF16),
        jax.ShapeDtypeStruct((rows, half), BF16),
    ]
    return pl.pallas_call(
        ffn_b_kernel,
        grid=(2,),
        in_specs=[whole(a.shape) for a in args],
        out_specs=[whole(o.shape) for o in outs],
        out_shape=outs,
        scratch_shapes=[
            pltpu.VMEM((rows, width), F32),
            pltpu.VMEM((rows, width), F32),
            pltpu.VMEM((rows, width), BF16),
        ],
        compiler_params=params(),
        name="ffn_b",
    )(*args)


def grad_qkv_kernel(normed_ref, gp_ref, out_ref):
    out_ref[...] = dot_tn(normed_ref[...], gp_ref[...]).astype(BF16)


def grad_qkv(normed, gp):
    rows, width = normed.shape
    pairs = gp.shape[1] // (3 * PAIR)
    return pl.pallas_call(
        grad_qkv_kernel,
        grid=(pairs,),
        in_specs=[whole((rows, width)), pl.BlockSpec((rows, 3 * PAIR), lambda p: (0, p))],
        out_specs=pl.BlockSpec((width, 3 * PAIR), lambda p: (0, p)),
        out_shape=jax.ShapeDtypeStruct((width, gp.shape[1]), BF16),
        compiler_params=params(),
        name="grad_qkv",
    )(normed, gp)


def grad_input_kernel(src_ref, gmid_ref, gain_ref, gp_own_ref, gp_oth_ref, wa_own_ref, wa_oth_ref, out_ref, ggain_ref):
    rows = src_ref.shape[0]
    pairs = wa_own_ref.shape[1] // (4 * PAIR)

    def weight(ref):
        return jnp.concatenate(
            [ref[:, 4 * p * PAIR : (4 * p + 3) * PAIR] for p in range(pairs)], axis=1
        )

    w_own, w_oth = weight(wa_own_ref), weight(wa_oth_ref)
    ggain = jnp.zeros(ggain_ref.shape, F32)
    for start in range(0, rows, CHUNK):
        at = slice(start, start + CHUNK)
        gnorm = dot_nt(gp_own_ref[at, :], w_own) + dot_nt(gp_oth_ref[at, :], w_oth)
        v = src_ref[at, :].astype(F32)
        r = lax.rsqrt(jnp.mean(v * v, axis=-1, keepdims=True) + EPS)
        ggain = ggain + jnp.sum(gnorm * v * r, axis=0, keepdims=True)
        back = gain_ref[...] * gnorm
        inner = jnp.mean(back * v, axis=-1, keepdims=True)
        out_ref[at, :] = gmid_ref[at, :] + r * back - v * (r * r * r * inner)
    ggain_ref[...] = ggain


def grad_input(src, gmid, gain, gp_own, gp_oth, wa_own, wa_oth):
    rows, width = src.shape
    args = (src, gmid, gain, gp_own, gp_oth, wa_own, wa_oth)
    return pl.pallas_call(
        grad_input_kernel,
        grid=(1,),
        in_specs=[whole(a.shape) for a in args],
        out_specs=[whole((rows, width)), whole((1, width))],
        out_shape=[
            jax.ShapeDtypeStruct((rows, width), F32),
            jax.ShapeDtypeStruct((1, width), F32),
        ],
        compiler_params=params(),
        name="grad_input",
    )(*args)


def swap(v, axis, size, bit):
    return lax.ppermute(v, axis, [(i, i ^ bit) for i in range(size)])


def ordered(flag, mine, other):
    return jnp.where(
        flag == 0,
        jnp.concatenate([mine, other], axis=0),
        jnp.concatenate([other, mine], axis=0),
    )


def sum_over_dp(cur, dp, me):
    stages = [1 << s for s in range(dp.bit_length() - 1)]
    for bit in stages:
        flag = (me // bit) % 2
        half = cur.shape[0] // 2
        send = lax.dynamic_slice_in_dim(cur, (1 - flag) * half, half, 0)
        keep = lax.dynamic_slice_in_dim(cur, flag * half, half, 0)
        got = swap(send, "dp", dp, bit)
        cur = (keep.astype(F32) + got.astype(F32)).astype(BF16)
    for bit in reversed(stages):
        flag = (me // bit) % 2
        cur = ordered(flag, cur, swap(cur, "dp", dp, bit))
    return cur.astype(F32)


def per_device(dp, inputs, gain_attn, w_qkv, w_out, gain_ffn, w_in, w_back, bias_table, lengths, buckets, cotangent):
    t = lax.axis_index("tensor")
    me = lax.axis_index("dp")
    core = t % 2
    width = inputs.shape[1]
    rows = inputs.shape[0] // 2
    seq = buckets.shape[0]
    docs = lengths.shape[0] // 2
    heads = bias_table.shape[1]
    table_rows = bias_table.shape[0]
    cols = heads * HD
    pairs = heads

    src = lax.dynamic_slice_in_dim(inputs, core * rows, rows, 0)
    cot = lax.dynamic_slice_in_dim(cotangent, core * rows, rows, 0)
    lens = lax.dynamic_slice_in_dim(lengths, core * docs, docs, 0)
    gain_one = gain_attn.astype(F32).reshape(1, width)
    gain_two = gain_ffn.astype(F32).reshape(1, width)

    attn_w = jnp.concatenate([w_qkv[0], w_qkv[1], w_qkv[2], w_out.T], axis=1)

    def from_core(v):
        return swap(v, "tensor", 4, 1)

    def from_x(v):
        flag = me % 2
        half = v.shape[0] // 2
        part = lax.dynamic_slice_in_dim(v, flag * half, half, 0)
        part = swap(part, "tensor", 4, 2)
        return ordered(flag, part, swap(part, "dp", dp, 1))

    attn_c = from_core(attn_w)
    in_c = from_core(w_in)
    back_c = from_core(w_back)
    attn_x = from_x(attn_w)
    attn_xc = from_core(attn_x)
    in_x = from_x(w_in)
    in_xc = from_core(in_x)
    back_x = from_x(w_back)
    back_xc = from_core(back_x)

    def by_pair(a, b):
        both = jnp.stack([a.reshape(width, 4, heads, HD), b.reshape(width, 4, heads, HD)], axis=2)
        both = both.reshape(width, 4, pairs, PAIR).transpose(0, 2, 1, 3)
        return both.reshape(width, pairs * 4 * PAIR)

    wa_own = by_pair(attn_w, attn_c)
    wa_oth = by_pair(attn_x, attn_xc)

    diag_bucket = jnp.concatenate([buckets[:, 0], buckets[0, :1], buckets[0, 1:][::-1]])
    one_hot = diag_bucket[:, None] == jnp.arange(table_rows)[None, :]
    table_all = lax.all_gather(bias_table.T.astype(F32), "tensor", tiled=False)
    along = jnp.sum(
        jnp.where(one_hot[None, None], table_all[:, :, None, :], 0.0), axis=-1
    )

    def along_of(first, second):
        picked = jnp.stack(
            [
                lax.dynamic_index_in_dim(along, first, 0, keepdims=False),
                lax.dynamic_index_in_dim(along, second, 0, keepdims=False),
            ]
        )
        return picked.reshape(pairs, 2, 2 * seq)

    chip = t // 2
    u_own = along_of(2 * chip + core, 2 * chip + 1 - core)
    u_oth = along_of(2 * (1 - chip) + core, 2 * (1 - chip) + 1 - core)

    normed = norm_rows(src, gain_one)
    packed_own, probs_own, att_own = attn_fwd(normed, wa_own, u_own, lens, docs, seq)
    packed_oth, probs_oth, att_oth = attn_fwd(normed, wa_oth, u_oth, lens, docs, seq)
    middle, normed2, acc_a, gacc_a, gback, gin = ffn_a(
        src, att_own, att_oth, wa_own, wa_oth, gain_two, cot, w_in, in_c, w_back, back_c
    )

    def sum_core(mine, other):
        return (mine.astype(F32) + from_core(other).astype(F32)).astype(BF16)

    grad_w_back = sum_over_dp(sum_core(gback[0], gback[1]), dp, me)
    grad_w_in = sum_over_dp(sum_core(gin[0], gin[1]), dp, me)
    mixed, gmid, ggain_two, gwout, do_own, do_oth = ffn_b(
        middle, normed2, acc_a, gacc_a, att_own, wa_own, wa_oth, gain_two, cot, in_x, in_xc, back_x, back_xc
    )
    grad_w_out = sum_over_dp(sum_core(gwout[:cols], gwout[cols:]), dp, me)
    gp_own, diag_own = attn_bwd(packed_own, probs_own, do_own, docs, seq)
    gqkv = grad_qkv(normed, gp_own)
    gqkv = gqkv.reshape(width, pairs, 3, PAIR).transpose(0, 2, 1, 3).reshape(width, 3, 2 * cols)
    gq_mine = gqkv[:, :, :cols].reshape(width, 3 * cols)
    gq_other = gqkv[:, :, cols:].reshape(width, 3 * cols)
    grad_w_qkv = sum_over_dp(sum_core(gq_mine, gq_other), dp, me)
    grad_w_qkv = grad_w_qkv.reshape(width, 3, cols).transpose(1, 0, 2)
    gp_oth, _ = attn_bwd(packed_oth, probs_oth, do_oth, docs, seq)
    gsrc, ggain_one = grad_input(src, gmid, gain_one, gp_own, gp_oth, wa_own, wa_oth)

    diag = diag_own.reshape(2 * heads, 2 * seq)
    table = jnp.sum(jnp.where(one_hot[None], diag[:, :, None], 0.0), axis=1)
    table = ordered(0, table[:heads], table[heads:])
    table_sum = table[:heads] + from_core(table[heads:])
    small = jnp.concatenate([ggain_one, ggain_two], axis=1)
    small = small + from_core(small)
    small = jnp.concatenate([small.reshape(-1), table_sum.reshape(-1)])
    for s in range(dp.bit_length() - 1):
        small = small + swap(small, "dp", dp, 1 << s)
    grad_gain_attn = small[:width]
    grad_gain_ffn = small[width : 2 * width]
    grad_table = small[2 * width :].reshape(heads, table_rows).T

    mixed_all = ordered(core, mixed, from_core(mixed))
    grad_in_all = ordered(core, gsrc, from_core(gsrc))
    return (
        mixed_all,
        grad_in_all,
        grad_gain_attn,
        grad_w_qkv,
        grad_w_out,
        grad_gain_ffn,
        grad_w_in,
        grad_w_back,
        grad_table,
    )


def solution(mesh):
    return jax.shard_map(
        functools.partial(per_device, mesh.shape["dp"]),
        mesh=mesh,
        in_specs=(
            P("dp", None),
            P(),
            P(None, None, "tensor"),
            P("tensor", None),
            P(),
            P(None, "tensor"),
            P("tensor", None),
            P(None, "tensor"),
            P("dp"),
            P(),
            P("dp", None),
        ),
        out_specs=(
            P("dp", None),
            P("dp", None),
            P(),
            P(None, None, "tensor"),
            P("tensor", None),
            P(),
            P(None, "tensor"),
            P("tensor", None),
            P(None, "tensor"),
        ),
        check_vma=False,
    )
```

time: 852 us -> 405 us (0.48)
  waiting for transfers between devices: 560 us -> 98.7 us
  Pallas kernels: 0 us -> 129 us
  matrix products: 118 us -> 0 us
  starting transfers between devices: 0.57 us -> 50.2 us
  blocking collectives: 39.1 us -> 23.2 us
  between operations: 15.2 us -> 1.64 us
  local copies, waits for them, and re-layouts: 68.5 us -> 56.9 us
    psum x4 -> x0, waiting for transfers between devices: 560 us -> none  [the longest x1 184 us: per_device(): lax.psum((grad_gain_attn, grad_w_qkv, grad_w_out, grad_gain_ffn, grad_w_i...]
    pallas_call x0 -> x9, Pallas kernels: none -> 129 us  [the longest x2 28.6 us: attn_fwd(): pl.pallas_call(functools.partial(attn_fwd_kernel, docs, seq), grid=(pairs...]
    dot_general x40 -> x0, matrix products: 115 us -> none  [the longest x4 26.7 us: per_device(): jnp.einsum('bn,hn->bh', one_hot, grad_scores.reshape(heads_here, seq_len...]
    ppermute x0 -> x47, waiting for transfers between devices: none -> 98.7 us  [swap(): return lax.ppermute(v, axis, [(i, i ^ bit) for i in range(size)])]
    ppermute x0 -> x47, starting transfers between devices: none -> 50.2 us  [swap(): return lax.ppermute(v, axis, [(i, i ^ bit) for i in range(size)])]
    psum x1 -> x0, blocking collectives: 39.1 us -> none  [per_device(): lax.psum((grad_gain_attn, grad_w_qkv, grad_w_out, grad_gain_ffn, grad_w_i...]
    unnamed x171 -> x47, local copies, waits for them, and re-layouts: 37.2 us -> 7.65 us
    all_gather x0 -> x1, blocking collectives: none -> 23.2 us  [per_device(): table_all = lax.all_gather(bias_table.T.astype(F32), 'tensor', tiled=False)]
  transfers between devices with their start and end apart: 4 -> 47, of which waited for: 4 -> 24; matrix products, arithmetic and copies ran while one was open for 12% -> 20% of each run, Pallas kernels for 0% -> 26%
where the time goes in v1:
time: 405 us; the launch traced here: 400 us
  Pallas kernels  129 us (32%)
  waiting for transfers between devices  98.7 us (24%)
  local copies, waits for them, and re-layouts  56.9 us (14%)
  starting transfers between devices  50.2 us (12%)
  other arithmetic  40.3 us (10%)
  blocking collectives  23.2 us (6%)
    ppermute x47, waiting for transfers between devices, swap(): return lax.ppermute(v, axis, [(i, i ^ bit) for i in range(size)])  98.7 us
    ppermute x47, starting transfers between devices, swap(): return lax.ppermute(v, axis, [(i, i ^ bit) for i in range(size)])  50.2 us
    pallas_call x2, Pallas kernels, attn_fwd(): pl.pallas_call(functools.partial(attn_fwd_kernel, docs, seq), grid=(pairs...  28.6 us
    pallas_call x1, Pallas kernels, ffn_a(): pl.pallas_call(ffn_a_kernel, grid=(2,), in_specs=[whole(a.shape) for a in...  27.7 us
    pallas_call x1, Pallas kernels, ffn_b(): pl.pallas_call(ffn_b_kernel, grid=(2,), in_specs=[whole(a.shape) for a in...  27.1 us
    pallas_call x2, Pallas kernels, attn_bwd(): pl.pallas_call(functools.partial(attn_bwd_kernel, docs, seq), grid=(pairs...  24.1 us
    all_gather x1, blocking collectives, per_device(): table_all = lax.all_gather(bias_table.T.astype(F32), 'tensor', tiled=False)  23.2 us
    select_n x16, other arithmetic, ordered(): jnp.where(flag == 0, jnp.concatenate([mine, other], axis=0), jnp.concaten...  21.9 us
  transfers between devices with their start and end apart: 47, of which 24 were waited for; matrix products, arithmetic and copies ran while one was open for 20% of the time, Pallas kernels for 26%

profile of v1, /device:TPU:0, one launch (start us, length us, event | category | flops | bytes accessed | tf_op | source)
XLA Modules:
  0.0 400.2 jit_solution(10995770385398167143)
XLA Ops:
  0.7 2.0 copy.70
  2.7 2.0 fusion.7
  4.7 1.9 copy.85
  6.6 1.9 copy.84
  9.4 2.9 pad_maximum_fusion.2
  12.2 2.0 constant_dynamic-slice_fusion.17
  14.2 2.9 collective-permute-start.1
  17.2 1.9 constant_dynamic-slice_fusion.13
  20.0 2.0 collective-permute-start.9
  24.7 7.0 %collective-permute-done.1 = bf16[384,768]{1,0:T(8,128)(2,1)} collective-permute-done((bf16[384,768]{1,0:T(8,128)(2,1)}, bf16[384,768]{1,0:T(8,128)(2,1)}, u32[]{:S(2)}, u32[]{:S(2)}) %collective-permute-start.1) | collective-permute-done | bytes 589856 | tf_op jit(solution)/shard_map/ppermute | solution.py:441
  31.7 2.1 collective-permute-start.2
  33.7 23.2 %all-gather.1 = f32[4,3,32]{2,1,0:T(4,128)S(1)} all-gather(f32[1,3,32]{2,1,0:T(4,128)S(1)} %convert_bitcast_fusion.1), channel_id=2, replica_groups=mesh['tensor'=4,'dp'=8] {'tensor'}, dimensions={0}, use_global_device_ids=true | all-gather | bytes 1920 | tf_op jit(solution)/shard_map/all_gather | solution.py:518
  57.0 1.8 collective-permute-start.7
  61.0 2.8 maximum_select_fusion.3
  63.8 9.5 %collective-permute-done.7 = bf16[384,768]{1,0:T(8,128)(2,1)S(1)} collective-permute-done((bf16[384,768]{1,0:T(8,128)(2,1)}, bf16[384,768]{1,0:T(8,128)(2,1)S(1)}, u32[]{:S(2)}, u32[]{:S(2)}) %collective-permute-start.7) | collective-permute-done | bytes 589856 | tf_op jit(solution)/shard_map/ppermute | solution.py:441
  73.3 2.7 maximum_select_fusion.4.in_a_ref
  76.0 9.4 %collective-permute-done.10 = bf16[384,768]{1,0:T(8,128)(2,1)S(1)} collective-permute-done((bf16[384,768]{1,0:T(8,128)(2,1)}, bf16[384,768]{1,0:T(8,128)(2,1)S(1)}, u32[]{:S(2)}, u32[]{:S(2)}) %collective-permute-start.10) | collective-permute-done | bytes 589856 | tf_op jit(solution)/shard_map/ppermute | solution.py:441
  85.5 2.6 maximum_select_fusion.5.back_a_ref
  93.4 4.3 %norm_rows.1.normed_ref = bf16[1024,768]{1,0:T(8,128)(2,1)} custom-call(bf16[1024,768]{1,0:T(8,128)(2,1)} %constant_dynamic-slice_fusion.20.src_ref, f32[1,768]{1,0:T(1,128)} %reshape.204.gain_ref), custom_call_target="tpu_custom_call" | custom-call | tf_op jit(solution)/shard_map/norm_rows/pallas_call | solution.py:51
  99.0 2.2 copy.75
  101.2 2.4 copy.72
  105.0 3.4 copy.74
  108.4 5.0 %reshape.191.w_ref.wa_own_ref = bf16[768,1536]{1,0:T(8,128)(2,1)} reshape(bf16[768,3,4,128]{3,2,1,0:T(4,128)(2,1)} %copy.74) | data formatting | bytes 4718592 | tf_op jit(solution)/shard_map/reshape | solution.py:511
  113.4 14.4 %attn_fwd.2 = (bf16[1024,1152]{1,0:T(8,128)(2,1)}, bf16[2,6,512,512]{3,2,1,0:T(8,128)(2,1)}, bf16[1024,384]{1,0:T(8,128)(2,1)}) custom-call(s32[2]{0:T(128)} %dynamic_slice.104.len_ref, bf16[1024,768]{1,0:T(8,128)(2,1)} %norm_rows.1.normed_ref, bf16[768,1536]{1,0:T(8,128)(2,1)} %reshape.191.w_ref.wa_own_ref, f32[3,2,1024]{2,1,0:T(2,128)} %reshape.192.u_ref), custom_call_target="tpu_custom_call" | custom-call | tf_op jit(solution)/shard_map/attn_fwd/pallas_call | solution.py:94
  129.5 2.4 copy.77
  131.8 1.8 pad_maximum_fusion.1
  133.7 1.6 copy.78
  135.3 4.0 copy.79
  139.3 2.4 reshape.194.w_ref.wa_oth_ref
  141.6 14.3 %attn_fwd.3 = (bf16[1024,1152]{1,0:T(8,128)(2,1)}, bf16[2,6,512,512]{3,2,1,0:T(8,128)(2,1)}, bf16[1024,384]{1,0:T(8,128)(2,1)}) custom-call(s32[2]{0:T(128)} %dynamic_slice.104.len_ref, bf16[1024,768]{1,0:T(8,128)(2,1)} %norm_rows.1.normed_ref, bf16[768,1536]{1,0:T(8,128)(2,1)} %reshape.194.w_ref.wa_oth_ref, f32[3,2,1024]{2,1,0:T(2,128)} %reshape.195.u_ref), custom_call_target="tpu_custom_call" | custom-call | tf_op jit(solution)/shard_map/attn_fwd/pallas_call | solution.py:94
  155.9 27.7 %ffn_a.1 = (f32[1024,768]{1,0:T(8,128)}, bf16[1024,768]{1,0:T(8,128)(2,1)}, f32[1024,768]{1,0:T(8,128)}, f32[1024,768]{1,0:T(8,128)}, bf16[2,768,768]{2,1,0:T(8,128)(2,1)}, /*index=5*/bf16[2,768,768]{2,1,0:T(8,128)(2,1)}) custom-call(bf16[1024,768]{1,0:T(8,128)(2,1)} %constant_dynamic-slice_fusion.20.src_ref, ...), custom_call_target="tpu_custom_call" | custom-call | tf_op jit(solution)/shard_map/ffn_a/pallas_call | solution.py:274
  183.6 27.1 %ffn_b.1 = (bf16[1024,768]{1,0:T(8,128)(2,1)}, f32[1024,768]{1,0:T(8,128)}, f32[1,768]{1,0:T(1,128)}, bf16[384,768]{1,0:T(8,128)(2,1)}, bf16[1024,384]{1,0:T(8,128)(2,1)}, /*index=5*/bf16[1024,384]{1,0:T(8,128)(2,1)}) custom-call(f32[1024,768]{1,0:T(8,128)} %get-tuple-element.34.middle_ref, bf16[1024,768]{1,0:T(8,128)(2,1)} %get-tuple-element.35.normed_ref, ...), custom_call_target="tpu_custom_call" | custom-call | tf_op jit(solution)/shard_map/ffn_b/pallas_call | solution.py:366
  210.7 12.2 %attn_bwd.2 = (bf16[1024,1152]{1,0:T(8,128)(2,1)}, f32[3,2,1024]{2,1,0:T(2,128)}) custom-call(bf16[1024,1152]{1,0:T(8,128)(2,1)} %get-tuple-element.40.packed_ref, bf16[2,6,512,512]{3,2,1,0:T(8,128)(2,1)} %get-tuple-element.41.probs_ref, bf16[1024,384]{1,0:T(8,128)(2,1)} %get-tuple-element.42.dout_ref), custom_call_target="tpu_custom_call" | custom-call | tf_op jit(solution)/shard_map/attn_bwd/pallas_call | solution.py:167
  224.3 5.8 %grad_qkv.1 = bf16[768,1152]{1,0:T(8,128)(2,1)} custom-call(bf16[1024,768]{1,0:T(8,128)(2,1)} %norm_rows.1.normed_ref, bf16[1024,1152]{1,0:T(8,128)(2,1)} %get-tuple-element.43.gp_own_ref.gp_ref), custom_call_target="tpu_custom_call" | custom-call | tf_op jit(solution)/shard_map/grad_qkv/pallas_call | solution.py:389
  230.2 12.0 %attn_bwd.3 = (bf16[1024,1152]{1,0:T(8,128)(2,1)}, f32[3,2,1024]{2,1,0:T(2,128)}) custom-call(bf16[1024,1152]{1,0:T(8,128)(2,1)} %get-tuple-element.44.packed_ref, bf16[2,6,512,512]{3,2,1,0:T(8,128)(2,1)} %get-tuple-element.45.probs_ref, bf16[1024,384]{1,0:T(8,128)(2,1)} %get-tuple-element.46.dout_ref), custom_call_target="tpu_custom_call" | custom-call | tf_op jit(solution)/shard_map/attn_bwd/pallas_call | solution.py:167
  242.1 11.6 %grad_input.1 = (f32[1024,768]{1,0:T(8,128)}, f32[1,768]{1,0:T(1,128)}) custom-call(bf16[1024,768]{1,0:T(8,128)(2,1)} %constant_dynamic-slice_fusion.20.src_ref, f32[1024,768]{1,0:T(8,128)} %get-tuple-element.39.gmid_ref, f32[1,768]{1,0:T(1,128)} %reshape.204.gain_ref, bf16[1024,1152]{1,0:T(8,128)(2,1)} %get-tuple-element.43.gp_own_ref.gp_ref, ...), custom_call_target="tpu_custom_call" | custom-call | tf_op jit(solution)/shard_map/grad_input/pallas_call | solution.py:426
  254.5 2.5 copy.80
  257.0 1.7 copy.81
  261.5 1.8 collective-permute-start.27
  263.7 4.1 %collective-permute-done.27 = bf16[96,768]{1,0:T(8,128)(2,1)S(1)} collective-permute-done((bf16[96,768]{1,0:T(8,128)(2,1)S(1)}, bf16[96,768]{1,0:T(8,128)(2,1)S(1)}, u32[]{:S(2)}, u32[]{:S(2)}) %collective-permute-start.27) | collective-permute-done | bytes 147488 | tf_op jit(solution)/shard_map/ppermute | solution.py:441
  267.9 1.9 collective-permute-start.28
  270.1 2.3 collective-permute-done.28
  272.5 2.9 collective-permute-start.29
  277.4 2.9 collective-permute-start.30
  285.4 1.8 collective-permute-done.31
  290.4 3.1 collective-permute-done.32
  298.2 8.4 %collective-permute-done.20 = bf16[384,576]{0,1:T(8,128)(2,1)S(1)} collective-permute-done((bf16[384,576]{0,1:T(8,128)(2,1)S(1)}, bf16[384,576]{0,1:T(8,128)(2,1)S(1)}, u32[]{:S(2)}, u32[]{:S(2)}) %collective-permute-start.20) | collective-permute-done | bytes 442400 | tf_op jit(solution)/shard_map/ppermute | solution.py:441
  310.2 3.4 collective-permute-done.21
  314.0 2.6 collective-permute-start.22
  316.6 3.6 maximum_select_fusion.1
  320.2 3.8 collective-permute-done.22
  324.4 4.9 %collective-permute-start.35 = (bf16[192,768]{1,0:T(8,128)(2,1)S(1)}, bf16[192,768]{1,0:T(8,128)(2,1)S(1)}, u32[]{:S(2)}, u32[]{:S(2)}) collective-permute-start(bf16[192,768]{1,0:T(8,128)(2,1)S(1)} %constant_dynamic-slice_fusion.4), channel_id=1, source_target_pairs={{0,2},{1,3},{2,0},{3,1},{4,6},{5,7},{6,4},{7,5},{8,10},{9,11},{10,... | collective-permute-start | bytes 884744 | tf_op jit(solution)/shard_map/ppermute | solution.py:441
  333.2 4.1 %collective-permute-done.35 = bf16[192,768]{1,0:T(8,128)(2,1)S(1)} collective-permute-done((bf16[192,768]{1,0:T(8,128)(2,1)S(1)}, bf16[192,768]{1,0:T(8,128)(2,1)S(1)}, u32[]{:S(2)}, u32[]{:S(2)}) %collective-permute-start.35) | collective-permute-done | bytes 294944 | tf_op jit(solution)/shard_map/ppermute | solution.py:441
  337.6 9.3 %collective-permute-done.42 = bf16[192,768]{1,0:T(8,128)(2,1)S(1)} collective-permute-done((bf16[192,768]{1,0:T(8,128)(2,1)S(1)}, bf16[192,768]{1,0:T(8,128)(2,1)S(1)}, u32[]{:S(2)}, u32[]{:S(2)}) %collective-permute-start.42) | collective-permute-done | bytes 294944 | tf_op jit(solution)/shard_map/ppermute | solution.py:441
  347.0 4.5 %collective-permute-done.36 = bf16[96,768]{1,0:T(8,128)(2,1)S(1)} collective-permute-done((bf16[96,768]{1,0:T(8,128)(2,1)S(1)}, bf16[96,768]{1,0:T(8,128)(2,1)S(1)}, u32[]{:S(2)}, u32[]{:S(2)}) %collective-permute-start.36) | collective-permute-done | bytes 147488 | tf_op jit(solution)/shard_map/ppermute | solution.py:441
  351.6 3.5 collective-permute-start.37
  355.1 6.6 %collective-permute-done.43 = bf16[96,768]{1,0:T(8,128)(2,1)S(1)} collective-permute-done((bf16[96,768]{1,0:T(8,128)(2,1)S(1)}, bf16[96,768]{1,0:T(8,128)(2,1)S(1)}, u32[]{:S(2)}, u32[]{:S(2)}) %collective-permute-start.43) | collective-permute-done | bytes 147488 | tf_op jit(solution)/shard_map/ppermute | solution.py:441
  364.9 1.9 collective-permute-start.38
  366.8 2.4 collective-permute-done.44
  370.1 5.3 %collective-permute-done.38 = bf16[192,768]{1,0:T(8,128)(2,1)S(1)} collective-permute-done((bf16[192,768]{1,0:T(8,128)(2,1)S(1)}, bf16[192,768]{1,0:T(8,128)(2,1)S(1)}, u32[]{:S(2)}, u32[]{:S(2)}) %collective-permute-start.38) | collective-permute-done | bytes 294944 | tf_op jit(solution)/shard_map/ppermute | solution.py:441
  377.1 1.9 collective-permute-done.45
  382.2 7.1 %maximum_select_fusion = f32[2048,768]{1,0:T(8,128)} fusion(f32[1024,768]{1,0:T(8,128)} %collective-permute-done.13, f32[1024,768]{1,0:T(8,128)} %get-tuple-element.48, pred[]{:T(512)S(6)} %eq.75), kind=kLoop, calls=%fused_computation | loop fusion | flops 4718592 | bytes 12582913 | tf_op jit(solution)/shard_map/jit(_where)/select_n | solution.py:445
  389.3 2.6 collective-permute-done.39
  393.5 4.8 %collective-permute-done.46 = bf16[384,768]{1,0:T(8,128)(2,1)S(1)} collective-permute-done((bf16[384,768]{1,0:T(8,128)(2,1)S(1)}, bf16[384,768]{1,0:T(8,128)(2,1)S(1)}, u32[]{:S(2)}, u32[]{:S(2)}) %collective-permute-start.46) | collective-permute-done | bytes 589856 | tf_op jit(solution)/shard_map/ppermute | solution.py:441
  (187 shorter events, 57.8 us)
Async XLA Ops:
  0.6 91.5 %copy-start = (bf16[2048,768]{1,0:T(8,128)(2,1)S(1)}, bf16[2048,768]{1,0:T(8,128)(2,1)}, u32[]{:S(2)}) copy-start(bf16[2048,768]{1,0:T(8,128)(2,1)} %param.11) | copy-start | bytes 9437188
  12.2 6.9 %copy-start.5 = (bf16[768,768]{1,0:T(8,128)(2,1)S(1)}, bf16[768,768]{1,0:T(8,128)(2,1)}, u32[]{:S(2)}) copy-start(bf16[768,768]{1,0:T(8,128)(2,1)} %back_a_ref.1) | copy-start | bytes 3538948
  12.2 21.5 %copy-start.18 = (bf16[32,3]{0,1:T(4,128)(2,1)S(1)}, bf16[32,3]{0,1:T(4,128)(2,1)}, u32[]{:S(2)}) copy-start(bf16[32,3]{0,1:T(4,128)(2,1)} %param.18) | copy-start | bytes 580
  14.2 17.4 %collective-permute-start.1 = (bf16[384,768]{1,0:T(8,128)(2,1)}, bf16[384,768]{1,0:T(8,128)(2,1)}, u32[]{:S(2)}, u32[]{:S(2)}) collective-permute-start(bf16[384,768]{1,0:T(8,128)(2,1)} %constant_dynamic-slice_fusion.17), channel_id=1, source_target_pairs={{0,16},{8,24},{16,0},{24,8},{1,17},{9,25},{17,1},{25,9},{2,18},{10... | collective-permute-start | bytes 1769480 | tf_op jit(solution)/shard_map/ppermute | solution.py:441
  19.1 37.9 %collective-permute-start.6 = (bf16[384,768]{1,0:T(8,128)(2,1)}, bf16[384,768]{1,0:T(8,128)(2,1)}, u32[]{:S(2)}, u32[]{:S(2)}) collective-permute-start(bf16[384,768]{1,0:T(8,128)(2,1)} %constant_dynamic-slice_fusion.13), channel_id=1, source_target_pairs={{0,16},{8,24},{16,0},{24,8},{1,17},{9,25},{17,1},{25,9},{2,18},{10... | collective-permute-start | bytes 1769480 | tf_op jit(solution)/shard_map/ppermute | solution.py:441
  20.0 39.9 %collective-permute-start.9 = (bf16[384,768]{1,0:T(8,128)(2,1)}, bf16[384,768]{1,0:T(8,128)(2,1)}, u32[]{:S(2)}, u32[]{:S(2)}) collective-permute-start(bf16[384,768]{1,0:T(8,128)(2,1)} %constant_dynamic-slice_fusion.12), channel_id=1, source_target_pairs={{0,16},{8,24},{16,0},{24,8},{1,17},{9,25},{17,1},{25,9},{2,18},{10... | collective-permute-start | bytes 1769480 | tf_op jit(solution)/shard_map/ppermute | solution.py:441
  22.0 66.1 %collective-permute-start = (bf16[768,768]{1,0:T(8,128)(2,1)}, bf16[768,768]{1,0:T(8,128)(2,1)}, u32[]{:S(2)}, u32[]{:S(2)}) collective-permute-start(bf16[768,768]{1,0:T(8,128)(2,1)} %pad_maximum_fusion.2), channel_id=1, source_target_pairs={{0,8},{8,0},{16,24},{24,16},{1,9},{9,1},{17,25},{25,17},{2,10},{10... | collective-permute-start | bytes 3538952 | tf_op jit(solution)/shard_map/ppermute | solution.py:441
  22.0 133.9 %collective-permute-start.4 = (bf16[768,768]{1,0:T(8,128)(2,1)}, bf16[768,768]{1,0:T(8,128)(2,1)}, u32[]{:S(2)}, u32[]{:S(2)}) collective-permute-start(bf16[768,768]{1,0:T(8,128)(2,1)} %in_a_ref.1), channel_id=1, source_target_pairs={{0,8},{8,0},{16,24},{24,16},{1,9},{9,1},{17,25},{25,17},{2,10},{10... | collective-permute-start | bytes 3538952 | tf_op jit(solution)/shard_map/ppermute | solution.py:441
  31.7 29.3 %collective-permute-start.2 = (bf16[384,768]{1,0:T(8,128)(2,1)}, bf16[384,768]{1,0:T(8,128)(2,1)S(1)}, u32[]{:S(2)}, u32[]{:S(2)}) collective-permute-start(bf16[384,768]{1,0:T(8,128)(2,1)} %collective-permute-done.1), channel_id=1, source_target_pairs={{0,1},{1,0},{2,3},{3,2},{4,5},{5,4},{6,7},{7,6},{8,9},{9,8},{10,11... | collective-permute-start | bytes 1769480 | tf_op jit(solution)/shard_map/ppermute | solution.py:441
  57.0 16.4 %collective-permute-start.7 = (bf16[384,768]{1,0:T(8,128)(2,1)}, bf16[384,768]{1,0:T(8,128)(2,1)S(1)}, u32[]{:S(2)}, u32[]{:S(2)}) collective-permute-start(bf16[384,768]{1,0:T(8,128)(2,1)} %collective-permute-done.6), channel_id=1, source_target_pairs={{0,1},{1,0},{2,3},{3,2},{4,5},{5,4},{6,7},{7,6},{8,9},{9,8},{10,11... | collective-permute-start | bytes 1769480 | tf_op jit(solution)/shard_map/ppermute | solution.py:441
  59.9 25.6 %collective-permute-start.10 = (bf16[384,768]{1,0:T(8,128)(2,1)}, bf16[384,768]{1,0:T(8,128)(2,1)S(1)}, u32[]{:S(2)}, u32[]{:S(2)}) collective-permute-start(bf16[384,768]{1,0:T(8,128)(2,1)} %collective-permute-done.9), channel_id=1, source_target_pairs={{0,1},{1,0},{2,3},{3,2},{4,5},{5,4},{6,7},{7,6},{8,9},{9,8},{10,11... | collective-permute-start | bytes 1769480 | tf_op jit(solution)/shard_map/ppermute | solution.py:441
  60.9 15.1 %copy-start.9 = (bf16[384,768]{1,0:T(8,128)(2,1)}, bf16[384,768]{1,0:T(8,128)(2,1)S(1)}, u32[]{:S(2)}) copy-start(bf16[384,768]{1,0:T(8,128)(2,1)S(1)} %collective-permute-done.2) | copy-start | bytes 1769476
  60.9 95.0 %collective-permute-start.5 = (bf16[768,768]{1,0:T(8,128)(2,1)}, bf16[768,768]{1,0:T(8,128)(2,1)}, u32[]{:S(2)}, u32[]{:S(2)}) collective-permute-start(bf16[768,768]{1,0:T(8,128)(2,1)} %back_a_ref.1), channel_id=1, source_target_pairs={{0,8},{8,0},{16,24},{24,16},{1,9},{9,1},{17,25},{25,17},{2,10},{10... | collective-permute-start | bytes 3538952 | tf_op jit(solution)/shard_map/ppermute | solution.py:441
  73.3 56.1 %collective-permute-start.3 = (bf16[768,768]{1,0:T(8,128)(2,1)}, bf16[768,768]{1,0:T(8,128)(2,1)}, u32[]{:S(2)}, u32[]{:S(2)}) collective-permute-start(bf16[768,768]{1,0:T(8,128)(2,1)} %maximum_select_fusion.3), channel_id=1, source_target_pairs={{0,8},{8,0},{16,24},{24,16},{1,9},{9,1},{17,25},{25,17},{2,10},{10... | collective-permute-start | bytes 3538952 | tf_op jit(solution)/shard_map/ppermute | solution.py:441
  76.0 13.1 %copy-start.16 = (bf16[768]{0:T(1024)(128)(2,1)S(1)}, bf16[768]{0:T(1024)(128)(2,1)}, u32[]{:S(2)}) copy-start(bf16[768]{0:T(1024)(128)(2,1)} %param.12) | copy-start | bytes 4612
  76.0 15.0 %copy-start.17 = (bf16[768]{0:T(1024)(128)(2,1)S(1)}, bf16[768]{0:T(1024)(128)(2,1)}, u32[]{:S(2)}) copy-start(bf16[768]{0:T(1024)(128)(2,1)} %param.15) | copy-start | bytes 4612
  76.0 15.5 %copy-start.19 = (s32[4]{0:T(128)S(1)}, s32[4]{0:T(128)}, u32[]{:S(2)}) copy-start(s32[4]{0:T(128)} %param.19) | copy-start | bytes 52
  85.4 98.2 %collective-permute-start.8 = (bf16[768,768]{1,0:T(8,128)(2,1)}, bf16[768,768]{1,0:T(8,128)(2,1)}, u32[]{:S(2)}, u32[]{:S(2)}) collective-permute-start(bf16[768,768]{1,0:T(8,128)(2,1)} %maximum_select_fusion.4.in_a_ref), channel_id=1, source_target_pairs={{0,8},{8,0},{16,24},{24,16},{1,9},{9,1},{17,25},{25,17},{2,10},{10... | collective-permute-start | bytes 3538952 | tf_op jit(solution)/shard_map/ppermute | solution.py:441
  88.1 95.5 %collective-permute-start.11 = (bf16[768,768]{1,0:T(8,128)(2,1)}, bf16[768,768]{1,0:T(8,128)(2,1)}, u32[]{:S(2)}, u32[]{:S(2)}) collective-permute-start(bf16[768,768]{1,0:T(8,128)(2,1)} %maximum_select_fusion.5.back_a_ref), channel_id=1, source_target_pairs={{0,8},{8,0},{16,24},{24,16},{1,9},{9,1},{17,25},{25,17},{2,10},{10... | collective-permute-start | bytes 3538952 | tf_op jit(solution)/shard_map/ppermute | solution.py:441
  99.0 4.6 %copy-start.4 = (bf16[1,768,192]{1,2,0:T(8,128)(2,1)S(1)}, bf16[1,768,192]{1,2,0:T(8,128)(2,1)}, u32[]{:S(2)}) copy-start(bf16[1,768,192]{1,2,0:T(8,128)(2,1)} %get-tuple-element.59) | copy-start | bytes 884740
  113.4 14.4 %copy-start.10 = (bf16[384,768]{1,0:T(8,128)(2,1)S(1)}, bf16[384,768]{1,0:T(8,128)(2,1)}, u32[]{:S(2)}) copy-start(bf16[384,768]{1,0:T(8,128)(2,1)} %copy-done.9) | copy-start | bytes 1769476
  113.4 14.7 %copy-start.11 = (bf16[384,768]{0,1:T(8,128)(2,1)S(1)}, bf16[384,768]{0,1:T(8,128)(2,1)}, u32[]{:S(2)}) copy-start(bf16[384,768]{0,1:T(8,128)(2,1)} %copy.75) | copy-start | bytes 1769476
  210.7 105.9 %collective-permute-start.12 = (bf16[1024,768]{1,0:T(8,128)(2,1)}, bf16[1024,768]{1,0:T(8,128)(2,1)}, u32[]{:S(2)}, u32[]{:S(2)}) collective-permute-start(bf16[1024,768]{1,0:T(8,128)(2,1)} %get-tuple-element.38), channel_id=1, source_target_pairs={{0,8},{8,0},{16,24},{24,16},{1,9},{9,1},{17,25},{25,17},{2,10},{10... | collective-permute-start | bytes 4718600 | tf_op jit(solution)/shard_map/ppermute | solution.py:441
  223.8 36.5 %collective-permute-start.15 = (f32[3,32]{1,0:T(4,128)S(1)}, f32[3,32]{1,0:T(4,128)S(1)}, u32[]{:S(2)}, u32[]{:S(2)}) collective-permute-start(f32[3,32]{1,0:T(4,128)S(1)} %slice.78), channel_id=1, source_target_pairs={{0,8},{8,0},{16,24},{24,16},{1,9},{9,1},{17,25},{25,17},{2,10},{10... | collective-permute-start | bytes 1160 | tf_op jit(solution)/shard_map/ppermute | solution.py:441
  242.1 12.3 %copy-start.15 = (f32[1,768]{1,0:T(1,128)S(1)}, f32[1,768]{1,0:T(1,128)}, u32[]{:S(2)}) copy-start(f32[1,768]{1,0:T(1,128)} %get-tuple-element.50) | copy-start | bytes 9220
  242.1 12.3 %copy-start.2 = (bf16[768,1152]{1,0:T(8,128)(2,1)S(1)}, bf16[768,1152]{1,0:T(8,128)(2,1)}, u32[]{:S(2)}) copy-start(bf16[768,1152]{1,0:T(8,128)(2,1)} %grad_qkv.1) | copy-start | bytes 5308420
  254.4 8.9 %collective-permute-start.14 = (f32[1,1536]{1,0:T(1,128)S(1)}, f32[1,1536]{1,0:T(1,128)S(1)}, u32[]{:S(2)}, u32[]{:S(2)}) collective-permute-start(f32[1,1536]{1,0:T(1,128)S(1)} %constant_dynamic-update-slice_fusion), channel_id=1, source_target_pairs={{0,8},{8,0},{16,24},{24,16},{1,9},{9,1},{17,25},{25,17},{2,10},{10... | collective-permute-start | bytes 18440 | tf_op jit(solution)/shard_map/ppermute | solution.py:441
  258.7 1.7 collective-permute-start.26
  260.2 27.0 %collective-permute-start.19 = (bf16[768,576]{0,1:T(8,128)(2,1)}, bf16[768,576]{0,1:T(8,128)(2,1)}, u32[]{:S(2)}, u32[]{:S(2)}) collective-permute-start(bf16[768,576]{0,1:T(8,128)(2,1)} %bitcast.26), channel_id=1, source_target_pairs={{0,8},{8,0},{16,24},{24,16},{1,9},{9,1},{17,25},{25,17},{2,10},{10... | collective-permute-start | bytes 2654216 | tf_op jit(solution)/shard_map/ppermute | solution.py:441
  261.5 18.8 %copy-start.6 = (bf16[2,768,768]{2,1,0:T(8,128)(2,1)S(1)}, bf16[2,768,768]{2,1,0:T(8,128)(2,1)}, u32[]{:S(2)}) copy-start(bf16[2,768,768]{2,1,0:T(8,128)(2,1)} %get-tuple-element.54) | copy-start | bytes 7077892
  261.5 6.3 %collective-permute-start.27 = (bf16[96,768]{1,0:T(8,128)(2,1)S(1)}, bf16[96,768]{1,0:T(8,128)(2,1)S(1)}, u32[]{:S(2)}, u32[]{:S(2)}) collective-permute-start(bf16[96,768]{1,0:T(8,128)(2,1)S(1)} %constant_dynamic-slice_fusion.8), channel_id=1, source_target_pairs={{0,1},{1,0},{2,3},{3,2},{4,5},{5,4},{6,7},{7,6},{8,9},{9,8},{10,11... | collective-permute-start | bytes 442376 | tf_op jit(solution)/shard_map/ppermute | solution.py:441
  263.4 6.4 %collective-permute-start.16 = (f32[1632]{0:T(1024)S(1)}, f32[1632]{0:T(1024)S(1)}, u32[]{:S(2)}, u32[]{:S(2)}) collective-permute-start(f32[1632]{0:T(1024)S(1)} %pad_maximum_fusion.5), channel_id=1, source_target_pairs={{0,1},{1,0},{2,3},{3,2},{4,5},{5,4},{6,7},{7,6},{8,9},{9,8},{10,11... | collective-permute-start | bytes 19592 | tf_op jit(solution)/shard_map/ppermute | solution.py:441
  267.9 4.5 %collective-permute-start.28 = (bf16[48,768]{1,0:T(8,128)(2,1)S(1)}, bf16[48,768]{1,0:T(8,128)(2,1)S(1)}, u32[]{:S(2)}, u32[]{:S(2)}) collective-permute-start(bf16[48,768]{1,0:T(8,128)(2,1)S(1)} %constant_dynamic-slice_fusion.7), channel_id=1, source_target_pairs={{0,2},{1,3},{2,0},{3,1},{4,6},{5,7},{6,4},{7,5},{8,10},{9,11},{10,... | collective-permute-start | bytes 221192 | tf_op jit(solution)/shard_map/ppermute | solution.py:441
  269.8 7.0 %collective-permute-start.17 = (f32[1632]{0:T(1024)S(1)}, f32[1632]{0:T(1024)S(1)}, u32[]{:S(2)}, u32[]{:S(2)}) collective-permute-start(f32[1632]{0:T(1024)S(1)} %fusion.9), channel_id=1, source_target_pairs={{0,2},{1,3},{2,0},{3,1},{4,6},{5,7},{6,4},{7,5},{8,10},{9,11},{10,... | collective-permute-start | bytes 19592 | tf_op jit(solution)/shard_map/ppermute | solution.py:441
  272.5 4.9 %collective-permute-start.29 = (bf16[24,768]{1,0:T(8,128)(2,1)S(1)}, bf16[24,768]{1,0:T(8,128)(2,1)S(1)}, u32[]{:S(2)}, u32[]{:S(2)}) collective-permute-start(bf16[24,768]{1,0:T(8,128)(2,1)S(1)} %constant_dynamic-slice_fusion.6), channel_id=1, source_target_pairs={{0,4},{1,5},{2,6},{3,7},{4,0},{5,1},{6,2},{7,3},{8,12},{9,13},{10,... | collective-permute-start | bytes 110600 | tf_op jit(solution)/shard_map/ppermute | solution.py:441
  276.7 19.3 %collective-permute-start.33 = (bf16[768,768]{1,0:T(8,128)(2,1)S(1)}, bf16[768,768]{1,0:T(8,128)(2,1)}, u32[]{:S(2)}, u32[]{:S(2)}) collective-permute-start(bf16[768,768]{1,0:T(8,128)(2,1)S(1)} %slice_bitcast_fusion.1), channel_id=1, source_target_pairs={{0,8},{8,0},{16,24},{24,16},{1,9},{9,1},{17,25},{25,17},{2,10},{10... | collective-permute-start | bytes 3538952 | tf_op jit(solution)/shard_map/ppermute | solution.py:441
  276.8 4.6 %collective-permute-start.18 = (f32[1632]{0:T(1024)S(1)}, f32[1632]{0:T(1024)S(1)}, u32[]{:S(2)}, u32[]{:S(2)}) collective-permute-start(f32[1632]{0:T(1024)S(1)} %add.203), channel_id=1, source_target_pairs={{0,4},{1,5},{2,6},{3,7},{4,0},{5,1},{6,2},{7,3},{8,12},{9,13},{10,... | collective-permute-start | bytes 19592 | tf_op jit(solution)/shard_map/ppermute | solution.py:441
  277.4 5.3 %collective-permute-start.30 = (bf16[24,768]{1,0:T(8,128)(2,1)S(1)}, bf16[24,768]{1,0:T(8,128)(2,1)S(1)}, u32[]{:S(2)}, u32[]{:S(2)}) collective-permute-start(bf16[24,768]{1,0:T(8,128)(2,1)S(1)} %add_convert_fusion.12), channel_id=1, source_target_pairs={{0,4},{1,5},{2,6},{3,7},{4,0},{5,1},{6,2},{7,3},{8,12},{9,13},{10,... | collective-permute-start | bytes 110600 | tf_op jit(solution)/shard_map/ppermute | solution.py:441
  281.4 100.8 %collective-permute-start.13 = (f32[1024,768]{1,0:T(8,128)}, f32[1024,768]{1,0:T(8,128)}, u32[]{:S(2)}, u32[]{:S(2)}) collective-permute-start(f32[1024,768]{1,0:T(8,128)} %get-tuple-element.48), channel_id=1, source_target_pairs={{0,8},{8,0},{16,24},{24,16},{1,9},{9,1},{17,25},{25,17},{2,10},{10... | collective-permute-start | bytes 9437192 | tf_op jit(solution)/shard_map/ppermute | solution.py:441
  282.7 4.4 %collective-permute-start.31 = (bf16[48,768]{1,0:T(8,128)(2,1)S(1)}, bf16[48,768]{1,0:T(8,128)(2,1)S(1)}, u32[]{:S(2)}, u32[]{:S(2)}) collective-permute-start(bf16[48,768]{1,0:T(8,128)(2,1)S(1)} %maximum_select_fusion.19), channel_id=1, source_target_pairs={{0,2},{1,3},{2,0},{3,1},{4,6},{5,7},{6,4},{7,5},{8,10},{9,11},{10,... | collective-permute-start | bytes 221192 | tf_op jit(solution)/shard_map/ppermute | solution.py:441
  287.2 21.1 %collective-permute-start.40 = (bf16[768,768]{1,0:T(8,128)(2,1)}, bf16[768,768]{1,0:T(8,128)(2,1)S(1)}, u32[]{:S(2)}, u32[]{:S(2)}) collective-permute-start(bf16[768,768]{1,0:T(8,128)(2,1)} %slice_bitcast_fusion), channel_id=1, source_target_pairs={{0,8},{8,0},{16,24},{24,16},{1,9},{9,1},{17,25},{25,17},{2,10},{10... | collective-permute-start | bytes 3538952 | tf_op jit(solution)/shard_map/ppermute | solution.py:441
  287.2 6.3 %collective-permute-start.32 = (bf16[96,768]{1,0:T(8,128)(2,1)S(1)}, bf16[96,768]{1,0:T(8,128)(2,1)S(1)}, u32[]{:S(2)}, u32[]{:S(2)}) collective-permute-start(bf16[96,768]{1,0:T(8,128)(2,1)S(1)} %maximum_select_fusion.18), channel_id=1, source_target_pairs={{0,1},{1,0},{2,3},{3,2},{4,5},{5,4},{6,7},{7,6},{8,9},{9,8},{10,11... | collective-permute-start | bytes 442376 | tf_op jit(solution)/shard_map/ppermute | solution.py:441
  288.8 7.1 %copy-start.8 = (bf16[2,768,768]{2,1,0:T(8,128)(2,1)S(1)}, bf16[2,768,768]{2,1,0:T(8,128)(2,1)}, u32[]{:S(2)}) copy-start(bf16[2,768,768]{2,1,0:T(8,128)(2,1)} %get-tuple-element.53) | copy-start | bytes 7077892
  293.5 13.1 %collective-permute-start.20 = (bf16[384,576]{0,1:T(8,128)(2,1)S(1)}, bf16[384,576]{0,1:T(8,128)(2,1)S(1)}, u32[]{:S(2)}, u32[]{:S(2)}) collective-permute-start(bf16[384,576]{0,1:T(8,128)(2,1)S(1)} %constant_dynamic-slice_fusion.11), channel_id=1, source_target_pairs={{0,1},{1,0},{2,3},{3,2},{4,5},{5,4},{6,7},{7,6},{8,9},{9,8},{10,11... | collective-permute-start | bytes 1327112 | tf_op jit(solution)/shard_map/ppermute | solution.py:441
  297.5 10.8 %copy-start.7 = (bf16[2,768,768]{2,1,0:T(8,128)(2,1)S(1)}, bf16[2,768,768]{2,1,0:T(8,128)(2,1)}, u32[]{:S(2)}) copy-start(bf16[2,768,768]{2,1,0:T(8,128)(2,1)} %get-tuple-element.54) | copy-start | bytes 7077892
  297.6 26.6 %collective-permute-start.34 = (bf16[384,768]{1,0:T(8,128)(2,1)S(1)}, bf16[384,768]{1,0:T(8,128)(2,1)S(1)}, u32[]{:S(2)}, u32[]{:S(2)}) collective-permute-start(bf16[384,768]{1,0:T(8,128)(2,1)S(1)} %constant_dynamic-slice_fusion.5), channel_id=1, source_target_pairs={{0,1},{1,0},{2,3},{3,2},{4,5},{5,4},{6,7},{7,6},{8,9},{9,8},{10,11... | collective-permute-start | bytes 1769480 | tf_op jit(solution)/shard_map/ppermute | solution.py:441
  306.9 6.8 %collective-permute-start.21 = (bf16[192,576]{0,1:T(8,128)(2,1)S(1)}, bf16[192,576]{0,1:T(8,128)(2,1)S(1)}, u32[]{:S(2)}, u32[]{:S(2)}) collective-permute-start(bf16[192,576]{0,1:T(8,128)(2,1)S(1)} %constant_dynamic-slice_fusion.10), channel_id=1, source_target_pairs={{0,2},{1,3},{2,0},{3,1},{4,6},{5,7},{6,4},{7,5},{8,10},{9,11},{10,... | collective-permute-start | bytes 663560 | tf_op jit(solution)/shard_map/ppermute | solution.py:441
  308.6 8.0 %copy-start.12 = (bf16[1024,768]{1,0:T(8,128)(2,1)S(1)}, bf16[1024,768]{1,0:T(8,128)(2,1)}, u32[]{:S(2)}) copy-start(bf16[1024,768]{1,0:T(8,128)(2,1)} %get-tuple-element.38) | copy-start | bytes 4718596
  308.7 21.9 %collective-permute-start.41 = (bf16[384,768]{1,0:T(8,128)(2,1)S(1)}, bf16[384,768]{1,0:T(8,128)(2,1)S(1)}, u32[]{:S(2)}, u32[]{:S(2)}) collective-permute-start(bf16[384,768]{1,0:T(8,128)(2,1)S(1)} %constant_dynamic-slice_fusion.2), channel_id=1, source_target_pairs={{0,1},{1,0},{2,3},{3,2},{4,5},{5,4},{6,7},{7,6},{8,9},{9,8},{10,11... | collective-permute-start | bytes 1769480 | tf_op jit(solution)/shard_map/ppermute | solution.py:441
  314.0 10.0 %collective-permute-start.22 = (bf16[96,576]{0,1:T(8,128)(2,1)S(1)}, bf16[96,576]{0,1:T(8,128)(2,1)S(1)}, u32[]{:S(2)}, u32[]{:S(2)}) collective-permute-start(bf16[96,576]{0,1:T(8,128)(2,1)S(1)} %constant_dynamic-slice_fusion.9), channel_id=1, source_target_pairs={{0,4},{1,5},{2,6},{3,7},{4,0},{5,1},{6,2},{7,3},{8,12},{9,13},{10,... | collective-permute-start | bytes 331784 | tf_op jit(solution)/shard_map/ppermute | solution.py:441
  324.1 8.1 %collective-permute-start.23 = (bf16[96,576]{0,1:T(8,128)(2,1)S(1)}, bf16[96,576]{0,1:T(8,128)(2,1)S(1)}, u32[]{:S(2)}, u32[]{:S(2)}) collective-permute-start(bf16[96,576]{0,1:T(8,128)(2,1)S(1)} %add_convert_fusion.10), channel_id=1, source_target_pairs={{0,4},{1,5},{2,6},{3,7},{4,0},{5,1},{6,2},{7,3},{8,12},{9,13},{10,... | collective-permute-start | bytes 331784 | tf_op jit(solution)/shard_map/ppermute | solution.py:441
  324.4 13.0 %collective-permute-start.35 = (bf16[192,768]{1,0:T(8,128)(2,1)S(1)}, bf16[192,768]{1,0:T(8,128)(2,1)S(1)}, u32[]{:S(2)}, u32[]{:S(2)}) collective-permute-start(bf16[192,768]{1,0:T(8,128)(2,1)S(1)} %constant_dynamic-slice_fusion.4), channel_id=1, source_target_pairs={{0,2},{1,3},{2,0},{3,1},{4,6},{5,7},{6,4},{7,5},{8,10},{9,11},{10,... | collective-permute-start | bytes 884744 | tf_op jit(solution)/shard_map/ppermute | solution.py:441
  330.8 16.0 %collective-permute-start.42 = (bf16[192,768]{1,0:T(8,128)(2,1)S(1)}, bf16[192,768]{1,0:T(8,128)(2,1)S(1)}, u32[]{:S(2)}, u32[]{:S(2)}) collective-permute-start(bf16[192,768]{1,0:T(8,128)(2,1)S(1)} %constant_dynamic-slice_fusion.1), channel_id=1, source_target_pairs={{0,2},{1,3},{2,0},{3,1},{4,6},{5,7},{6,4},{7,5},{8,10},{9,11},{10,... | collective-permute-start | bytes 884744 | tf_op jit(solution)/shard_map/ppermute | solution.py:441
  332.5 29.3 %collective-permute-start.24 = (bf16[192,576]{0,1:T(8,128)(2,1)S(1)}, bf16[192,576]{0,1:T(8,128)(2,1)S(1)}, u32[]{:S(2)}, u32[]{:S(2)}) collective-permute-start(bf16[192,576]{0,1:T(8,128)(2,1)S(1)} %maximum_select_fusion.14), channel_id=1, source_target_pairs={{0,2},{1,3},{2,0},{3,1},{4,6},{5,7},{6,4},{7,5},{8,10},{9,11},{10,... | collective-permute-start | bytes 663560 | tf_op jit(solution)/shard_map/ppermute | solution.py:441
  337.5 14.1 %collective-permute-start.36 = (bf16[96,768]{1,0:T(8,128)(2,1)S(1)}, bf16[96,768]{1,0:T(8,128)(2,1)S(1)}, u32[]{:S(2)}, u32[]{:S(2)}) collective-permute-start(bf16[96,768]{1,0:T(8,128)(2,1)S(1)} %constant_dynamic-slice_fusion.3), channel_id=1, source_target_pairs={{0,4},{1,5},{2,6},{3,7},{4,0},{5,1},{6,2},{7,3},{8,12},{9,13},{10,... | collective-permute-start | bytes 442376 | tf_op jit(solution)/shard_map/ppermute | solution.py:441
  347.0 14.7 %collective-permute-start.43 = (bf16[96,768]{1,0:T(8,128)(2,1)S(1)}, bf16[96,768]{1,0:T(8,128)(2,1)S(1)}, u32[]{:S(2)}, u32[]{:S(2)}) collective-permute-start(bf16[96,768]{1,0:T(8,128)(2,1)S(1)} %constant_dynamic-slice_fusion), channel_id=1, source_target_pairs={{0,4},{1,5},{2,6},{3,7},{4,0},{5,1},{6,2},{7,3},{8,12},{9,13},{10,... | collective-permute-start | bytes 442376 | tf_op jit(solution)/shard_map/ppermute | solution.py:441
  351.6 13.2 %collective-permute-start.37 = (bf16[96,768]{1,0:T(8,128)(2,1)S(1)}, bf16[96,768]{1,0:T(8,128)(2,1)S(1)}, u32[]{:S(2)}, u32[]{:S(2)}) collective-permute-start(bf16[96,768]{1,0:T(8,128)(2,1)S(1)} %add_convert_fusion.8), channel_id=1, source_target_pairs={{0,4},{1,5},{2,6},{3,7},{4,0},{5,1},{6,2},{7,3},{8,12},{9,13},{10,... | collective-permute-start | bytes 442376 | tf_op jit(solution)/shard_map/ppermute | solution.py:441
  361.7 7.5 %collective-permute-start.44 = (bf16[96,768]{1,0:T(8,128)(2,1)S(1)}, bf16[96,768]{1,0:T(8,128)(2,1)S(1)}, u32[]{:S(2)}, u32[]{:S(2)}) collective-permute-start(bf16[96,768]{1,0:T(8,128)(2,1)S(1)} %add_convert_fusion.7), channel_id=1, source_target_pairs={{0,4},{1,5},{2,6},{3,7},{4,0},{5,1},{6,2},{7,3},{8,12},{9,13},{10,... | collective-permute-start | bytes 442376 | tf_op jit(solution)/shard_map/ppermute | solution.py:441
  362.2 18.6 %collective-permute-start.25 = (bf16[384,576]{0,1:T(8,128)(2,1)S(1)}, bf16[384,576]{0,1:T(8,128)(2,1)S(1)}, u32[]{:S(2)}, u32[]{:S(2)}) collective-permute-start(bf16[384,576]{0,1:T(8,128)(2,1)S(1)} %maximum_select_fusion.12), channel_id=1, source_target_pairs={{0,1},{1,0},{2,3},{3,2},{4,5},{5,4},{6,7},{7,6},{8,9},{9,8},{10,11... | collective-permute-start | bytes 1327112 | tf_op jit(solution)/shard_map/ppermute | solution.py:441
  364.9 10.5 %collective-permute-start.38 = (bf16[192,768]{1,0:T(8,128)(2,1)S(1)}, bf16[192,768]{1,0:T(8,128)(2,1)S(1)}, u32[]{:S(2)}, u32[]{:S(2)}) collective-permute-start(bf16[192,768]{1,0:T(8,128)(2,1)S(1)} %maximum_select_fusion.16), channel_id=1, source_target_pairs={{0,2},{1,3},{2,0},{3,1},{4,6},{5,7},{6,4},{7,5},{8,10},{9,11},{10,... | collective-permute-start | bytes 884744 | tf_op jit(solution)/shard_map/ppermute | solution.py:441
  369.3 9.8 %collective-permute-start.45 = (bf16[192,768]{1,0:T(8,128)(2,1)S(1)}, bf16[192,768]{1,0:T(8,128)(2,1)S(1)}, u32[]{:S(2)}, u32[]{:S(2)}) collective-permute-start(bf16[192,768]{1,0:T(8,128)(2,1)S(1)} %maximum_select_fusion.17), channel_id=1, source_target_pairs={{0,2},{1,3},{2,0},{3,1},{4,6},{5,7},{6,4},{7,5},{8,10},{9,11},{10,... | collective-permute-start | bytes 884744 | tf_op jit(solution)/shard_map/ppermute | solution.py:441
  375.6 16.3 %collective-permute-start.39 = (bf16[384,768]{1,0:T(8,128)(2,1)S(1)}, bf16[384,768]{1,0:T(8,128)(2,1)S(1)}, u32[]{:S(2)}, u32[]{:S(2)}) collective-permute-start(bf16[384,768]{1,0:T(8,128)(2,1)S(1)} %maximum_select_fusion.9), channel_id=1, source_target_pairs={{0,1},{1,0},{2,3},{3,2},{4,5},{5,4},{6,7},{7,6},{8,9},{9,8},{10,11... | collective-permute-start | bytes 1769480 | tf_op jit(solution)/shard_map/ppermute | solution.py:441
  379.2 19.1 %collective-permute-start.46 = (bf16[384,768]{1,0:T(8,128)(2,1)S(1)}, bf16[384,768]{1,0:T(8,128)(2,1)S(1)}, u32[]{:S(2)}, u32[]{:S(2)}) collective-permute-start(bf16[384,768]{1,0:T(8,128)(2,1)S(1)} %maximum_select_fusion.10), channel_id=1, source_target_pairs={{0,1},{1,0},{2,3},{3,2},{4,5},{5,4},{6,7},{7,6},{8,9},{9,8},{10,11... | collective-permute-start | bytes 1769480 | tf_op jit(solution)/shard_map/ppermute | solution.py:441
  391.9 8.1 %copy-start.1 = (bf16[2048,768]{1,0:T(8,128)(2,1)S(1)}, bf16[2048,768]{1,0:T(8,128)(2,1)}, u32[]{:S(2)}) copy-start(bf16[2048,768]{1,0:T(8,128)(2,1)} %param.11) | copy-start | bytes 9437188
  (3 other events, 10.6 us)

commit v2 on v0

v2 whole, which is shorter than its diff:
```python
import functools
import math

import jax
import jax.numpy as jnp
from jax import lax
from jax.experimental import pallas as pl
from jax.experimental.pallas import tpu as pltpu
from jax.sharding import PartitionSpec as P

HD = 64
PAIR = 2 * HD
EPS = 1e-06
MASKED = -1000000000.0
GELU_C = 0.7978845608028654
GELU_A = 0.044715
CHUNK = 256
VMEM_BYTES = 60 * 1024 * 1024

F32 = jnp.float32
BF16 = jnp.bfloat16


def dot_nn(a, b):
    return lax.dot_general(a, b, (((1,), (0,)), ((), ())), preferred_element_type=F32)


def dot_nt(a, b):
    return lax.dot_general(a, b, (((1,), (1,)), ((), ())), preferred_element_type=F32)


def dot_tn(a, b):
    return lax.dot_general(a, b, (((0,), (0,)), ((), ())), preferred_element_type=F32)


def whole(shape):
    return pl.BlockSpec(shape, lambda *_: (0,) * len(shape))


def shape_of(shape, dtype):
    return jax.ShapeDtypeStruct(shape, dtype)


def call(kernel, name, token, args, in_specs, outs, out_specs, grid=(1,), scratch=(), aliases=None):
    n_in, n_out = len(args), len(outs)

    def body(token_ref, *refs):
        del token_ref
        kernel(*refs[:n_in], *refs[n_in + 1 :])

    anywhere = pl.BlockSpec(memory_space=pl.ANY)
    res = pl.pallas_call(
        body,
        grid=grid,
        in_specs=[anywhere] + list(in_specs),
        out_specs=[anywhere] + list(out_specs),
        scratch_shapes=list(scratch),
        out_shape=[shape_of(token.shape, token.dtype)] + list(outs),
        input_output_aliases={0: 0, **(aliases or {})},
        compiler_params=pltpu.CompilerParams(vmem_limit_bytes=VMEM_BYTES),
        name=name,
    )(token, *args)
    return res[1:], res[0]


def rms_rows(v):
    return lax.rsqrt(jnp.mean(v * v, axis=-1, keepdims=True) + EPS)


def doc_rows(seq, width, docs, doc):
    return pl.BlockSpec((seq, width), lambda i: (lax.axis_index("core") * docs + doc, 0))


BIAS_ROWS = 16


def assemble(first_ref, second_ref, w_ref, width):
    cols = width // 4
    heads = cols // HD
    sources = [(first_ref, h) for h in range(heads)] + [(second_ref, h) for h in range(heads)]
    for p in range(heads):
        for part in range(3):
            for i in range(2):
                ref, head = sources[2 * p + i]
                src = part * cols + head * HD
                dst = (3 * p + part) * PAIR + i * HD
                w_ref[dst : dst + HD, :] = ref[src : src + HD, :]


def bias_along(first_ref, second_ref, left_ref, right_ref, u_ref, width):
    seq = left_ref.shape[0]
    left = left_ref[...].astype(F32).T[:1, :]
    right = right_ref[...].astype(F32).T[PAIR - 1 :, :]
    bucket = jnp.concatenate([left, pltpu.roll(right, 1, 1)], axis=1)
    index = lax.broadcasted_iota(jnp.int32, (PAIR, 2 * seq), 0).astype(F32)
    one_hot = (index == bucket).astype(BF16)
    heads = width // 4 // HD
    for at, ref in ((0, first_ref), (heads, second_ref)):
        u = dot_nn(ref[width:, :PAIR], one_hot)
        u_ref[at : at + heads, :] = u[:heads]


def attn_fwd_kernel(
    first, doc, docs, seq, len_ref, src_ref, gains_ref, *refs
):
    step = pl.program_id(0)
    if first:
        first_ref, second_ref, left_ref, right_ref, w_ref, u_ref, *refs = refs
    else:
        w_ref, u_ref, *refs = refs
    normed_ref, packed_ref, probs_ref, att_ref = refs

    @pl.when(step == 0)
    def _():
        if first:
            assemble(first_ref, second_ref, w_ref, src_ref.shape[1])
            bias_along(first_ref, second_ref, left_ref, right_ref, u_ref, src_ref.shape[1])
        for start in range(0, src_ref.shape[0], CHUNK):
            at = slice(start, start + CHUNK)
            v = src_ref[at, :].astype(F32)
            normed_ref[at, :] = (v * rms_rows(v) * gains_ref[:1, :]).astype(BF16)

    at = pl.multiple_of(step * 3 * PAIR, 3 * PAIR)
    packed = dot_nt(normed_ref[...], w_ref[pl.ds(at, 3 * PAIR), :])
    lane = lax.broadcasted_iota(jnp.int32, (seq, PAIR), 1)
    scale = 1.0 / math.sqrt(HD)
    packed_ref[:, :PAIR] = (packed[:, :PAIR].astype(BF16).astype(F32) * scale).astype(BF16)
    packed_ref[:, PAIR:] = packed[:, PAIR:].astype(BF16)
    key_pos = lax.broadcasted_iota(jnp.int32, (seq, 1), 0)
    length = len_ref[lax.axis_index("core") * docs + doc]
    for head in range(2):
        row = jnp.broadcast_to(u_ref[pl.ds(2 * step + head, 1), :], (seq, 2 * seq))
        rel = pltpu.roll(row, 0, 1, stride=1, stride_axis=0)[:, :seq]
        mine = (lane >= HD) if head else (lane < HD)
        q = packed_ref[:, :PAIR]
        k = packed_ref[:, PAIR : 2 * PAIR]
        v = packed_ref[:, 2 * PAIR :]
        k = jnp.where(mine, k, jnp.zeros_like(k))
        scores = dot_nt(k, q) + rel
        scores = jnp.where(key_pos < length, scores, MASKED)
        top = jnp.max(scores, axis=0, keepdims=True)
        e = jnp.exp(scores - top)
        total = jnp.sum(e, axis=0, keepdims=True)
        p = (e * (1.0 / total)).astype(BF16)
        probs_ref[head] = p
        vt = v.T[head * HD : (head + 1) * HD, :]
        o = dot_nn(vt, p)
        att_ref[:, head * HD : (head + 1) * HD] = o.T.astype(BF16)


def attn_fwd(ids, lengths, inputs, gains, weights, buckets, doc, docs):
    seq = buckets.shape[0]
    width = inputs.shape[1]
    pairs = width // (4 * HD)
    first = doc == 0
    specs = [pl.BlockSpec(memory_space=pltpu.SMEM), doc_rows(seq, width, docs, doc), whole(gains.shape)]
    args = (lengths, inputs, gains) + tuple(weights)
    specs += [whole(w.shape) for w in weights]
    outs, out_specs = [], []
    if first:
        last = seq // PAIR - 1
        args += (buckets, buckets)
        specs += [
            pl.BlockSpec((seq, PAIR), lambda p: (0, 0)),
            pl.BlockSpec((seq, PAIR), lambda p: (0, last)),
        ]
        outs = [shape_of((pairs * 3 * PAIR, width), BF16), shape_of((2 * pairs, 2 * seq), F32)]
        out_specs = [whole(o.shape) for o in outs]
    outs += [
        shape_of((seq, width), BF16),
        shape_of((seq, pairs * 3 * PAIR), BF16),
        shape_of((2 * pairs, seq, seq), BF16),
        shape_of((seq, pairs * PAIR), BF16),
    ]
    out_specs += [
        whole((seq, width)),
        pl.BlockSpec((seq, 3 * PAIR), lambda p: (0, p)),
        pl.BlockSpec((2, seq, seq), lambda p: (p, 0, 0)),
        pl.BlockSpec((seq, PAIR), lambda p: (0, p)),
    ]
    return call(
        functools.partial(attn_fwd_kernel, first, doc, docs, seq),
        "attn_fwd",
        ids,
        args,
        specs,
        outs,
        out_specs,
        grid=(pairs,),
    )


def ffn_kernel(
    src_ref, att_own_ref, att_oth_ref, wo_a_ref, wo_b_ref, wo_x_ref, wo_xc_ref, gains_ref, cot_ref,
    in_a_ref, in_b_ref, back_a_ref, back_b_ref,
    middle_ref, normed_ref, gsend_ref, hsend_ref, hid_ref, gpre_ref, acc_ref, gacc_ref,
):
    rows, width = src_ref.shape
    cols = width // 4
    step = pl.program_id(0)

    @pl.when(step == 0)
    def _():
        swapped = lax.axis_index("x") != 0
        wo_own = jnp.concatenate([wo_a_ref[...], wo_b_ref[...]], axis=0)
        wo_oth = jnp.concatenate([wo_x_ref[...], wo_xc_ref[...]], axis=0)
        wo_0 = jnp.where(swapped, wo_oth, wo_own)
        wo_1 = jnp.where(swapped, wo_own, wo_oth)
        for start in range(0, rows, CHUNK):
            at = slice(start, start + CHUNK)
            own, oth = att_own_ref[at, :], att_oth_ref[at, :]
            terms = dot_nn(jnp.where(swapped, oth, own), wo_0) + dot_nn(jnp.where(swapped, own, oth), wo_1)
            m = src_ref[at, :].astype(F32) + terms
            middle_ref[at, :] = m
            normed_ref[at, :] = (m * rms_rows(m) * gains_ref[1:, :]).astype(BF16)

    w_in = jnp.where(step == 0, in_a_ref[...], in_b_ref[...])
    w_back = jnp.where(step == 0, back_a_ref[...], back_b_ref[...])
    for start in range(0, rows, CHUNK):
        at = slice(start, start + CHUNK)
        pre = dot_nn(normed_ref[at, :], w_in)
        ghid = dot_nt(cot_ref[at, :], w_back)
        sq = pre * pre
        t = jnp.tanh(GELU_C * (pre + GELU_A * sq * pre))
        half_t = 0.5 * (1.0 + t)
        hidden = (pre * half_t).astype(BF16)
        slope = half_t + 0.5 * pre * (1.0 - t * t) * (GELU_C * (1.0 + 3.0 * GELU_A * sq))
        gpre = (ghid * slope).astype(BF16)
        out = dot_nn(hidden, w_back)
        gnorm = dot_nt(gpre, w_in)
        hid_ref[at, :] = hidden
        gpre_ref[at, :] = gpre

        @pl.when(step == 0)
        def _():
            acc_ref[at, :] = out
            gacc_ref[at, :] = gnorm

        @pl.when(step != 0)
        def _():
            hsend_ref[at, :] = (acc_ref[at, :] + out).astype(BF16)
            gsend_ref[at, :] = (gacc_ref[at, :] + gnorm).astype(BF16)


def ffn(ids, inputs, att_own, att_oth, wos, gains, cotangent, w_ins, w_backs, doc, docs):
    seq = att_own.shape[0]
    width = inputs.shape[1]
    units = w_ins[0].shape[1]
    mine = doc_rows(seq, width, docs, doc)
    outs = [
        shape_of((seq, width), F32),
        shape_of((seq, width), BF16),
        shape_of((seq, width), BF16),
        shape_of((seq, width), BF16),
        shape_of((seq, 2 * units), BF16),
        shape_of((seq, 2 * units), BF16),
    ]
    return call(
        ffn_kernel,
        "ffn",
        ids,
        (inputs, att_own, att_oth) + wos + (gains, cotangent) + w_ins + w_backs,
        [mine, whole(att_own.shape), whole(att_oth.shape)]
        + [whole(w.shape) for w in wos]
        + [whole(gains.shape), mine]
        + [whole(w.shape) for w in w_ins + w_backs],
        outs,
        [whole(o.shape) for o in outs[:4]] + [pl.BlockSpec((seq, units), lambda i: (0, i))] * 2,
        grid=(2,),
        scratch=[pltpu.VMEM((seq, width), F32), pltpu.VMEM((seq, width), F32)],
    )


def grad_back_kernel(docs, *refs):
    hid_refs, cot_ref, out_refs = refs[:docs], refs[docs], refs[docs + 1 :]
    hid = jnp.concatenate([r[...] for r in hid_refs], axis=0)
    units = out_refs[0].shape[0]
    for i in range(2):
        out_refs[i][...] = dot_tn(hid[:, i * units : (i + 1) * units], cot_ref[...]).astype(BF16)


def grad_back(ids, hids, cotangent, docs):
    seq, both = hids[0].shape
    width = cotangent.shape[1]
    outs = [shape_of((both // 2, width), BF16)] * 2
    return call(
        functools.partial(grad_back_kernel, docs),
        "grad_back",
        ids,
        tuple(hids) + (cotangent,),
        [whole(h.shape) for h in hids] + [pl.BlockSpec((docs * seq, width), lambda i: (lax.axis_index("core"), 0))],
        outs,
        [whole(o.shape) for o in outs],
    )


def grad_in_kernel(docs, *refs):
    normed_refs, gpre_refs, out_refs = refs[:docs], refs[docs : 2 * docs], refs[2 * docs :]
    normed = jnp.concatenate([r[...] for r in normed_refs], axis=0)
    gpre = jnp.concatenate([r[...] for r in gpre_refs], axis=0)
    units = out_refs[0].shape[1]
    for i in range(2):
        out_refs[i][...] = dot_tn(normed, gpre[:, i * units : (i + 1) * units]).astype(BF16)


def grad_in(ids, normeds, gpres, docs):
    width = normeds[0].shape[1]
    units = gpres[0].shape[1] // 2
    outs = [shape_of((width, units), BF16)] * 2
    args = tuple(normeds) + tuple(gpres)
    return call(
        functools.partial(grad_in_kernel, docs),
        "grad_in",
        ids,
        args,
        [whole(a.shape) for a in args],
        outs,
        [whole(o.shape) for o in outs],
    )


def fold_diagonals(g, seq):
    g = jnp.concatenate([g, jnp.zeros_like(g)], axis=1)
    n = seq
    while n > 8:
        n //= 2
        g = g[:n] + pltpu.roll(g[n:], 2 * seq - n, 1)
    while n > 1:
        n //= 2
        g = g[:n] + jnp.concatenate([g[n:, n:], g[n:, :n]], axis=1)
    return g


def attn_bwd_kernel(
    seq, middle_ref, gown_ref, goth_ref, gains_ref, cot_ref, wo_a_ref, wo_b_ref, w_ref, packed_ref, probs_ref,
    gmid_ref, low_ref, ggain_ref, gp_ref, nsend_ref, diag_ref, dout_ref, acc_ref,
):
    step = pl.program_id(0)
    pairs = pl.num_programs(0)

    @pl.when(step == 0)
    def _():
        wo_own = jnp.concatenate([wo_a_ref[...], wo_b_ref[...]], axis=0)
        ggain = jnp.zeros(ggain_ref.shape, F32)
        for start in range(0, seq, CHUNK):
            at = slice(start, start + CHUNK)
            m = middle_ref[at, :]
            gnorm = gown_ref[at, :].astype(F32) + goth_ref[at, :].astype(F32)
            r = rms_rows(m)
            ggain = ggain + jnp.sum(gnorm * m * r, axis=0, keepdims=True)
            back = gains_ref[1:, :] * gnorm
            inner = jnp.mean(back * m, axis=-1, keepdims=True)
            gm = cot_ref[at, :].astype(F32) + r * back - m * (r * r * r * inner)
            gmid_ref[at, :] = gm
            low = gm.astype(BF16)
            low_ref[at, :] = low
            dout = dot_nt(low, wo_own).astype(BF16)
            for p in range(dout_ref.shape[0]):
                dout_ref[p, at, :] = dout[:, p * PAIR : (p + 1) * PAIR]
        ggain_ref[...] = ggain

    lane = lax.broadcasted_iota(jnp.int32, (seq, PAIR), 1)
    scale = 1.0 / math.sqrt(HD)
    q = packed_ref[:, :PAIR]
    k = packed_ref[:, PAIR : 2 * PAIR]
    v = packed_ref[:, 2 * PAIR :]
    do = dout_ref[step]
    kt = k.T
    dqs, dks, dvs = [], [], []
    for head in range(2):
        mine = (lane >= HD) if head else (lane < HD)
        vm = jnp.where(mine, v, jnp.zeros_like(v))
        dp = dot_nt(vm, do)
        p_low = probs_ref[head]
        p = p_low.astype(F32)
        mean = jnp.sum(dp * p, axis=0, keepdims=True)
        ds = (p * (dp - mean)).astype(BF16)
        diag_ref[0, head : head + 1, :] = fold_diagonals(ds.astype(F32), seq)
        dvs.append(dot_nn(p_low, do))
        dks.append(dot_nn(ds, q))
        dqs.append(dot_nn(kt[head * HD : (head + 1) * HD, :], ds))
    dq = jnp.concatenate(dqs, axis=0).T * scale
    first = lane < HD
    gp_ref[:, :PAIR] = dq.astype(BF16)
    gp_ref[:, PAIR : 2 * PAIR] = jnp.where(first, dks[0], dks[1]).astype(BF16)
    gp_ref[:, 2 * PAIR :] = jnp.where(first, dvs[0], dvs[1]).astype(BF16)
    terms = dot_nn(gp_ref[...], w_ref[...])

    @pl.when(step == 0)
    def _():
        acc_ref[...] = terms

    @pl.when(step != 0)
    def _():
        acc_ref[...] += terms

    @pl.when(step == pairs - 1)
    def _():
        nsend_ref[...] = acc_ref[...].astype(BF16)


def attn_bwd(ids, middle, gown, goth, gains, cotangent, wo_a, wo_b, w_own, packed, probs, doc, docs):
    seq, width = middle.shape
    pairs = packed.shape[1] // (3 * PAIR)
    mine = doc_rows(seq, width, docs, doc)
    outs = [
        shape_of((seq, width), F32),
        shape_of((seq, width), BF16),
        shape_of((1, width), F32),
        shape_of(packed.shape, BF16),
        shape_of((seq, width), BF16),
        shape_of((pairs, 2, 2 * seq), F32),
    ]
    return call(
        functools.partial(attn_bwd_kernel, seq),
        "attn_bwd",
        ids,
        (middle, gown, goth, gains, cotangent, wo_a, wo_b, w_own, packed, probs),
        [whole(middle.shape), whole(gown.shape), whole(goth.shape), whole(gains.shape), mine]
        + [whole(wo_a.shape), whole(wo_b.shape)]
        + [
            pl.BlockSpec((3 * PAIR, width), lambda p: (p, 0)),
            pl.BlockSpec((seq, 3 * PAIR), lambda p: (0, p)),
            pl.BlockSpec((2, seq, seq), lambda p: (p, 0, 0)),
        ],
        outs,
        [
            whole((seq, width)),
            whole((seq, width)),
            whole((1, width)),
            pl.BlockSpec((seq, 3 * PAIR), lambda p: (0, p)),
            whole((seq, width)),
            pl.BlockSpec((1, 2, 2 * seq), lambda p: (p, 0, 0)),
        ],
        grid=(pairs,),
        scratch=[pltpu.VMEM((pairs, seq, PAIR), BF16), pltpu.VMEM((seq, width), F32)],
    )


def grad_attn_kernel(docs, pairs, *refs):
    groups = [refs[i * docs : (i + 1) * docs] for i in range(4)]
    (out_ref,) = refs[4 * docs :]
    normed, gp, low, att = (jnp.concatenate([r[...] for r in g], axis=0) for g in groups)
    step = pl.program_id(0)
    width = out_ref.shape[0] // 2
    cols = width // 4
    heads = cols // HD
    core = lax.axis_index("core")
    grads = dot_tn(gp, normed).astype(BF16)
    outer = dot_tn(att, low).astype(BF16)
    for p in range(pairs):

        @pl.when(step == p)
        def _(p=p):
            for i in range(2):
                head = 2 * p + i
                base = (core if head < heads else 1 - core) * width + (head % heads) * HD
                for part in range(3):
                    piece = grads[part * PAIR + i * HD : part * PAIR + (i + 1) * HD, :]
                    out_ref[pl.ds(pl.multiple_of(base + part * cols, HD), HD), :] = piece
                piece = outer[i * HD : (i + 1) * HD, :]
                out_ref[pl.ds(pl.multiple_of(base + 3 * cols, HD), HD), :] = piece


def grad_attn(ids, normeds, gps, lows, atts, docs):
    seq, width = normeds[0].shape
    pairs = atts[0].shape[1] // PAIR
    outs = [shape_of((2 * width, width), BF16)]
    return call(
        functools.partial(grad_attn_kernel, docs, pairs),
        "grad_attn",
        ids,
        tuple(normeds) + tuple(gps) + tuple(lows) + tuple(atts),
        [whole((seq, width))] * docs
        + [pl.BlockSpec((seq, 3 * PAIR), lambda p: (0, p))] * docs
        + [whole((seq, width))] * docs
        + [pl.BlockSpec((seq, PAIR), lambda p: (0, p))] * docs,
        outs,
        [whole((2 * width, width))],
        grid=(pairs,),
    )


def grad_input_kernel(docs, src_ref, gains_ref, *refs):
    gmid_refs, own_refs, oth_refs = (refs[i * docs : (i + 1) * docs] for i in range(3))
    full_ref, send_ref, ggain_ref = refs[3 * docs :]
    seq = gmid_refs[0].shape[0]
    ggain = jnp.zeros(ggain_ref.shape, F32)
    for doc in range(docs):
        for start in range(0, seq, CHUNK):
            here = slice(start, start + CHUNK)
            at = slice(doc * seq + start, doc * seq + start + CHUNK)
            gnorm = own_refs[doc][here, :].astype(F32) + oth_refs[doc][here, :].astype(F32)
            v = src_ref[at, :].astype(F32)
            r = rms_rows(v)
            ggain = ggain + jnp.sum(gnorm * v * r, axis=0, keepdims=True)
            back = gains_ref[:1, :] * gnorm
            inner = jnp.mean(back * v, axis=-1, keepdims=True)
            out = gmid_refs[doc][here, :] + r * back - v * (r * r * r * inner)
            full_ref[at, :] = out
            send_ref[at, :] = out
    ggain_ref[...] = ggain


def grad_input(ids, inputs, gains, gmids, owns, oths, docs):
    seq, width = gmids[0].shape
    rows = docs * seq
    mine = pl.BlockSpec((rows, width), lambda i: (lax.axis_index("core"), 0))
    return call(
        functools.partial(grad_input_kernel, docs),
        "grad_input",
        ids,
        (inputs, gains) + tuple(gmids) + tuple(owns) + tuple(oths),
        [mine, whole(gains.shape)] + [whole((seq, width))] * (3 * docs),
        [shape_of((2 * rows, width), F32), shape_of((rows, width), F32), shape_of((1, width), F32)],
        [mine, whole((rows, width)), whole((1, width))],
    )


def mix_kernel(docs, *refs):
    middle_refs, own_refs, oth_refs = (refs[i * docs : (i + 1) * docs] for i in range(3))
    full_ref, send_ref = refs[3 * docs :]
    seq = middle_refs[0].shape[0]
    for doc in range(docs):
        at = slice(doc * seq, (doc + 1) * seq)
        terms = own_refs[doc][...].astype(F32) + oth_refs[doc][...].astype(F32)
        out = (middle_refs[doc][...] + terms).astype(BF16)
        full_ref[at, :] = out
        send_ref[at, :] = out


def mix(ids, middles, owns, oths, docs):
    seq, width = middles[0].shape
    rows = docs * seq
    return call(
        functools.partial(mix_kernel, docs),
        "mix",
        ids,
        tuple(middles) + tuple(owns) + tuple(oths),
        [whole((seq, width))] * (3 * docs),
        [shape_of((2 * rows, width), BF16), shape_of((rows, width), BF16)],
        [pl.BlockSpec((rows, width), lambda i: (lax.axis_index("core"), 0)), whole((rows, width))],
    )


def place_kernel(full_ref, got_ref, out_ref):
    out_ref[...] = got_ref[...]


def place(ids, full, got):
    rows, width = got.shape
    steps = 4
    part = rows // steps
    return call(
        place_kernel,
        "place",
        ids,
        (full, got),
        [pl.BlockSpec(memory_space=pl.ANY), pl.BlockSpec((part, width), lambda i: (i, 0))],
        [shape_of(full.shape, full.dtype)],
        [pl.BlockSpec((part, width), lambda i: ((1 - lax.axis_index("core")) * steps + i, 0))],
        grid=(steps,),
        aliases={1: 1},
    )


def gate(ids, *arrays):
    anywhere = [pl.BlockSpec(memory_space=pl.ANY)] * len(arrays)
    shapes = [shape_of(v.shape, v.dtype) for v in arrays]
    aliases = {i + 1: i + 1 for i in range(len(arrays))}
    return call(lambda *refs: None, "gate", ids, arrays, anywhere, shapes, anywhere, aliases=aliases)


def need(ids, *arrays):
    anywhere = pl.BlockSpec(memory_space=pl.ANY)
    return call(lambda *refs: None, "need", ids, arrays, [anywhere] * len(arrays), [], [])[1]


def sum_core_kernel(a_ref, b_ref, c_ref, d_ref, ab_ref, cd_ref):
    ab_ref[...] = (a_ref[...].astype(F32) + b_ref[...].astype(F32)).astype(BF16)
    cd_ref[...] = (c_ref[...].astype(F32) + d_ref[...].astype(F32)).astype(BF16)


def sum_core(ids, a, b, c, d):
    steps = 4
    specs = [pl.BlockSpec((v.shape[0] // steps, v.shape[1]), lambda i: (i, 0)) for v in (a, b, c, d)]
    return call(
        sum_core_kernel,
        "sum_core",
        ids,
        (a, b, c, d),
        specs,
        [shape_of(a.shape, BF16), shape_of(c.shape, BF16)],
        [specs[0], specs[2]],
        grid=(steps,),
    )


def widen_kernel(*refs):
    half = len(refs) // 2
    for src, dst in zip(refs[:half], refs[half:]):
        dst[...] = src[...].astype(F32)


def widen(ids, *arrays):
    steps = 4
    specs = [pl.BlockSpec((v.shape[0] // steps, v.shape[1]), lambda i: (i, 0)) for v in arrays]
    return call(
        widen_kernel, "widen", ids, arrays, specs, [shape_of(v.shape, F32) for v in arrays], specs, grid=(steps,)
    )


def sum_kernel(got_ref, out_ref):
    rows = out_ref.shape[0]
    parts = got_ref.shape[0] // rows
    total = got_ref[:rows, :].astype(F32)
    for i in range(1, parts):
        total = total + got_ref[i * rows : (i + 1) * rows, :].astype(F32)
    out_ref[...] = total.astype(BF16)


def sum_parts(token, got, dp):
    width = got.shape[1]
    rows = got.shape[0] // (2 * dp)
    if rows % 16:
        total = jnp.sum(got.reshape(2 * dp, rows, width).astype(F32), axis=0).astype(BF16)
        return [jnp.tile(total, (dp, 1))], token
    return call(
        sum_kernel,
        "sum_parts",
        token,
        (got,),
        [whole(got.shape)],
        [shape_of((dp * rows, width), BF16)],
        [pl.BlockSpec((rows, width), lambda i: (i, 0))],
        grid=(dp,),
    )


def region(always, fn, ids):
    outs = jax.eval_shape(fn, ids)
    return lax.cond(always, fn, lambda _: jax.tree.map(lambda o: jnp.zeros(o.shape, o.dtype), outs), ids)


def per_device(dp, inputs, gain_attn, w_qkv, w_out, gain_ffn, w_in, w_back, bias_table, lengths, buckets, cotangent):
    width = inputs.shape[1]
    seq = buckets.shape[0]
    docs = lengths.shape[0] // 2
    table_rows, heads = bias_table.shape
    gains = jnp.stack([gain_attn, gain_ffn]).astype(F32)
    ids = jnp.zeros((8, 128), F32)

    def from_core(v):
        return lax.ppermute(v, "core", [(0, 1), (1, 0)])

    def from_x(v):
        return lax.ppermute(v, "x", [(0, 1), (1, 0)])

    def scatter(v):
        return lax.all_to_all(v, ("core", "dp"), 0, 0, tiled=True)

    def spread(v):
        return lax.all_to_all(v, "dp", 0, 0, tiled=True)

    bias = jnp.pad(bias_table.T, ((0, BIAS_ROWS - heads), (0, width - table_rows)))
    attn_w = jnp.concatenate([w_qkv.transpose(0, 2, 1).reshape(-1, width), bias], axis=0)
    attn_w = jnp.concatenate([attn_w[: 3 * width // 4], w_out, attn_w[3 * width // 4 :]], axis=0)
    attn_c = from_core(attn_w)
    wo_x = from_x(w_out)
    wo_c = from_core(w_out)
    in_c = from_core(w_in)
    back_c = from_core(w_back)

    every = range(docs)
    normed, packed, probs, att, att_x = [], [], [], [], []
    for doc in every:
        if doc == 0:
            (w_own, u, n, a, b, c), ids = attn_fwd(
                ids, lengths, inputs, gains, (attn_w, attn_c), buckets, doc, docs
            )
            (wo_x,), ids = gate(ids, wo_x)
            wo_xc = from_core(wo_x)
        else:
            (n, a, b, c), ids = attn_fwd(ids, lengths, inputs, gains, (w_own, u), buckets, doc, docs)
        normed.append(n)
        packed.append(a)
        probs.append(b)
        att.append(c)
        att_x.append(from_x(c))

    middle, normed2, gown, hown, hid, gpre, goth, hoth = [], [], [], [], [], [], [], []
    for doc in every:
        res, ids = ffn(
            ids, inputs, att[doc], att_x[doc], (w_out, wo_c, wo_x, wo_xc), gains, cotangent,
            (w_in, in_c), (w_back, back_c), doc, docs,
        )
        for group, r in zip((middle, normed2, gown, hown, hid, gpre), res):
            group.append(r)
        if doc + 1 < docs:
            ids = need(ids, att_x[doc + 1])
        (send,), ids = gate(ids, res[2])
        goth.append(from_x(send))
    always = lengths[0] > 0

    def ffn_grads(ids):
        (gback, gback_c), ids = grad_back(ids, hid, cotangent, docs)
        gback_c = from_core(gback_c)
        (gin, gin_c), ids = grad_in(ids, normed2, gpre, docs)
        (gback, gin), ids = sum_core(ids, gback, gback_c, gin, from_core(gin_c))
        return ids, gback, gin

    ids, gback, gin = region(always, ffn_grads, ids)
    ids = need(ids, *goth)
    (gback, gin), ids = gate(ids, gback, gin)
    gback, gin = lax.psum((gback, gin), "dp")

    def back_of(doc, ids):
        res, ids = attn_bwd(
            ids, middle[doc], gown[doc], goth[doc], gains, cotangent, w_out, wo_c, w_own, packed[doc], probs[doc],
            doc, docs,
        )
        return ids, res

    def attention_back(ids):
        ids, first = back_of(0, ids)
        noth = [from_x(first[4])]

        def others(ids):
            results = [first]
            for doc in range(1, docs):
                ids, res = back_of(doc, ids)
                results.append(res)
            gp, low = [r[3] for r in results], [r[1] for r in results]
            (gattn,), ids = grad_attn(ids, normed, gp, low, att, docs)
            return ids, results[1:], gattn

        ids, results, gattn = region(always, others, ids)
        gmid, low, ggain_two, gp, nown, diag = zip(first, *results)
        ids = need(ids, noth[0])
        for doc in range(1, docs):
            (send,), ids = gate(ids, nown[doc])
            noth.append(from_x(send))
        (gattn,), ids = gate(ids, gattn)
        gattn = scatter(gattn)
        hoth = []
        for doc in every:
            (send,), ids = gate(ids, hown[doc])
            hoth.append(from_x(send))
        (gsrc, gsrc_send, ggain_one), ids = grad_input(ids, inputs, gains, gmid, nown, noth, docs)
        gsrc_got = from_core(gsrc_send)

        diag_bucket = jnp.concatenate([buckets[:, 0], buckets[:1, -1], buckets[:-1, -1]])
        one_hot = (diag_bucket[:, None] == jnp.arange(table_rows)[None, :]).astype(F32)
        diag = sum(diag).reshape(2 * heads, 2 * seq)
        table = lax.dot_general(
            diag, one_hot, (((1,), (0,)), ((), ())), precision=lax.Precision.HIGHEST, preferred_element_type=F32
        )
        ggain_two = sum(ggain_two)
        small = jnp.concatenate([ggain_one.reshape(-1), ggain_two.reshape(-1), table[:heads].reshape(-1)])
        small_send = jnp.concatenate([ggain_one.reshape(-1), ggain_two.reshape(-1), table[heads:].reshape(-1)])
        small = small + from_core(small_send)
        for s in range(dp.bit_length() - 1):
            small = small + lax.ppermute(small, "dp", [(i, i ^ (1 << s)) for i in range(dp)])
        grad_gain_attn, grad_gain_ffn = small[:width], small[width : 2 * width]
        grad_table = small[2 * width :].reshape(heads, table_rows).T
        (gattn,), ids = sum_parts(ids, gattn, dp)
        gattn = spread(gattn)
        (gsrc,), ids = place(ids, gsrc, gsrc_got)
        (mixed, mixed_send), ids = mix(ids, middle, hown, hoth, docs)
        ids = need(ids, grad_gain_attn, grad_gain_ffn, grad_table)
        (mixed,), ids = place(ids, mixed, from_core(mixed_send))
        part = 3 * width // 4
        gattn = gattn.astype(F32)
        grad_w_qkv = gattn[:part].reshape(3, width // 4, width).transpose(0, 2, 1)
        grad_w_out = gattn[part:]
        return ids, mixed, gsrc, grad_gain_attn, grad_w_qkv, grad_w_out, grad_gain_ffn, grad_table

    ids, mixed, gsrc, grad_gain_attn, grad_w_qkv, grad_w_out, grad_gain_ffn, grad_table = region(
        always, attention_back, ids
    )
    (grad_w_back, grad_w_in), ids = widen(ids, gback, gin)
    return (
        mixed,
        gsrc,
        grad_gain_attn,
        grad_w_qkv,
        grad_w_out,
        grad_gain_ffn,
        grad_w_in,
        grad_w_back,
        grad_table,
    )


def solution(mesh):
    dp = mesh.shape["dp"]
    devices = mesh.devices.reshape(mesh.shape["tensor"] // 2, 2, dp)
    mesh = jax.sharding.Mesh(devices, ("x", "core", "dp"))
    return jax.shard_map(
        functools.partial(per_device, dp),
        mesh=mesh,
        in_specs=(
            P("dp", None),
            P(),
            P(None, None, ("x", "core")),
            P(("x", "core"), None),
            P(),
            P(None, ("x", "core")),
            P(("x", "core"), None),
            P(None, ("x", "core")),
            P("dp"),
            P(),
            P("dp", None),
        ),
        out_specs=(
            P("dp", None),
            P("dp", None),
            P(),
            P(None, None, ("x", "core")),
            P(("x", "core"), None),
            P(),
            P(None, ("x", "core")),
            P(("x", "core"), None),
            P(None, ("x", "core")),
        ),
        check_vma=False,
    )
```

time: 852 us -> 274 us (0.32)
  waiting for transfers between devices: 560 us -> 75 us
  Pallas kernels: 0 us -> 125 us
  matrix products: 118 us -> 0.37 us
  local copies, waits for them, and re-layouts: 68.5 us -> 17 us
  other arithmetic: 43.9 us -> 2.18 us
  blocking collectives: 39.1 us -> 0 us
  starting transfers between devices: 0.57 us -> 39.6 us
    psum x4 -> x1, waiting for transfers between devices: 560 us -> 0.01 us  [per_device(): gback, gin = lax.psum((gback, gin), 'dp')]
    pallas_call x0 -> x28, Pallas kernels: none -> 125 us  [call(): pl.pallas_call(body, grid=grid, in_specs=[anywhere] + list(in_specs), out...]
    dot_general x40 -> x1, matrix products: 115 us -> 0.37 us  [attention_back(): lax.dot_general(diag, one_hot, (((1,), (0,)), ((), ())), precision=lax.Pr...]
    all_to_all x0 -> x2, waiting for transfers between devices: none -> 43.9 us  [the longest x1 43.9 us: scatter(): return lax.all_to_all(v, ('core', 'dp'), 0, 0, tiled=True)]
    psum x1 -> x0, blocking collectives: 39.1 us -> none  [per_device(): lax.psum((grad_gain_attn, grad_w_qkv, grad_w_out, grad_gain_ffn, grad_w_i...]
    unnamed x171 -> x22, local copies, waits for them, and re-layouts: 37.2 us -> 5.93 us
    ppermute x0 -> x22, waiting for transfers between devices: none -> 31.1 us  [the longest x9 16.5 us: from_x(): return lax.ppermute(v, 'x', [(0, 1), (1, 0)])]
    ppermute x0 -> x22, starting transfers between devices: none -> 21.4 us  [the longest x9 12.2 us: from_x(): return lax.ppermute(v, 'x', [(0, 1), (1, 0)])]
  transfers between devices with their start and end apart: 4 -> 25, of which waited for: 4 -> 10; matrix products, arithmetic and copies ran while one was open for 12% -> 5% of each run, Pallas kernels for 0% -> 44%
where the time goes in v2:
time: 274 us; the launch traced here: 273 us
  Pallas kernels  125 us (46%)
  waiting for transfers between devices  75 us (27%)
  starting transfers between devices  39.6 us (14%)
  local copies, waits for them, and re-layouts  17 us (6%)
  between operations  14.2 us (5%)
    pallas_call x28, Pallas kernels, call(): pl.pallas_call(body, grid=grid, in_specs=[anywhere] + list(in_specs), out...  125 us
    all_to_all x1, waiting for transfers between devices, scatter(): return lax.all_to_all(v, ('core', 'dp'), 0, 0, tiled=True)  43.9 us
    ppermute x9, waiting for transfers between devices, from_x(): return lax.ppermute(v, 'x', [(0, 1), (1, 0)])  16.5 us
    ppermute x9, starting transfers between devices, from_x(): return lax.ppermute(v, 'x', [(0, 1), (1, 0)])  12.2 us
    all_to_all x1, starting transfers between devices, spread(): return lax.all_to_all(v, 'dp', 0, 0, tiled=True)  12.1 us
    ppermute x3, waiting for transfers between devices, attention_back(): lax.ppermute(small, 'dp', [(i, i ^ 1 << s) for i in range(dp)])  7.65 us
    cond x30, local copies, waits for them, and re-layouts  7.57 us
    ppermute x10, waiting for transfers between devices, from_core(): return lax.ppermute(v, 'core', [(0, 1), (1, 0)])  6.9 us
  transfers between devices with their start and end apart: 25, of which 10 were waited for; matrix products, arithmetic and copies ran while one was open for 5% of the time, Pallas kernels for 44%

profile of v2, /device:TPU:0, one launch (start us, length us, event | category | flops | bytes accessed | tf_op | source)
XLA Modules:
  0.0 273.2 jit_solution(5275707822207302770)
XLA Ops:
  7.3 1.4 fusion.3.refs_3_
  8.7 0.5 collective-permute-start.12
  9.3 0.4 collective-permute-start.18
  9.7 2.6 collective-permute-start.13
  12.3 0.2 collective-permute-start.15
  12.5 0.1 collective-permute-done.12.refs_4_
  12.6 1.0 copy-done.8
  13.7 10.2 %attn_fwd.2 = (f32[8,128]{1,0:T(8,128)S(1)}, bf16[1152,768]{1,0:T(8,128)(2,1)}, f32[6,1024]{1,0:T(8,128)}, bf16[512,768]{1,0:T(8,128)(2,1)}, bf16[512,1152]{1,0:...) custom-call(f32[8,128]{1,0:T(8,128)S(1)} %broadcast_31_token_ref.2.token_re, ...), custom_call_target="tpu_custom_call", output_to_operand_aliasing={{0}: (0, {})} | custom-call | tf_op jit(solution)/shard_map/attn_fwd/pallas_call | solution.py:52
  23.8 2.8 %collective-permute-start.14 = (bf16[512,384]{1,0:T(8,128)(2,1)}, bf16[512,384]{1,0:T(8,128)(2,1)}, u32[]{:S(2)}, u32[]{:S(2)}) collective-permute-start(bf16[512,384]{1,0:T(8,128)(2,1)} %get-tuple-element.261.refs_1_), channel_id=1, source_target_pairs={{0,16},{16,0},{1,17},{17,1},{2,18},{18,2},{3,19},{19,3},{4,20},{20... | collective-permute-start | bytes 1179656 | tf_op jit(solution)/shard_map/ppermute | solution.py:657
  26.7 9.2 %attn_fwd.3 = (f32[8,128]{1,0:T(8,128)S(1)}, bf16[512,768]{1,0:T(8,128)(2,1)}, bf16[512,1152]{1,0:T(8,128)(2,1)}, bf16[6,512,512]{2,1,0:T(8,128)(2,1)}, bf16[512,384]{1,0:T(8,128)(2,1)}) custom-call(f32[8,128]{1,0:T(8,128)S(1)} %get-tuple-element.257.token_ref, s32[4]{0:T(128)} %refs_0_.5, ...), custom_call_target="tpu_custom_call", output_to_operand_aliasing={{0}: (0, {})} | custom-call | tf_op jit(solution)/shard_map/attn_fwd/pallas_call | solution.py:52
  36.0 1.8 collective-permute-done.16.refs_6_
  37.8 0.7 copy-done.9
  38.5 13.0 %ffn.2 = (f32[8,128]{1,0:T(8,128)S(1)}, f32[512,768]{1,0:T(8,128)}, bf16[512,768]{1,0:T(8,128)(2,1)}, bf16[512,768]{1,0:T(8,128)(2,1)}, bf16[512,768]{1,0:T(8,12...) custom-call(f32[8,128]{1,0:T(8,128)S(1)} %get-tuple-element.260.token_ref, ...), custom_call_target="tpu_custom_call", output_to_operand_aliasing={{0}: (0, {})} | custom-call | tf_op jit(solution)/shard_map/ffn/pallas_call | solution.py:52
  51.5 2.1 copy.108.refs_0_
  53.5 1.9 collective-permute-start.20
  55.5 13.1 %ffn.3 = (f32[8,128]{1,0:T(8,128)S(1)}, f32[512,768]{1,0:T(8,128)}, bf16[512,768]{1,0:T(8,128)(2,1)}, bf16[512,768]{1,0:T(8,128)(2,1)}, bf16[512,768]{1,0:T(8,12...) custom-call(f32[8,128]{1,0:T(8,128)S(1)} %get-tuple-element.266.token_ref, ...), custom_call_target="tpu_custom_call", output_to_operand_aliasing={{0}: (0, {})} | custom-call | tf_op jit(solution)/shard_map/ffn/pallas_call | solution.py:52
  68.6 2.1 copy.111.refs_0_
  70.8 22.1 %conditional.3 = ((f32[8,128]{1,0:T(8,128)S(1)}, bf16[768,768]{1,0:T(8,128)(2,1)}, bf16[768,768]{1,0:T(8,128)(2,1)})) conditional(s32[]{:T(128)} %convert_element_type.17, () %tuple.32, (f32[8,128]{1,0:T(8,128)S(1)}, bf16[512,1536]{1,0:T(8,128)(2,1)}, bf16[512,1536]{1,0:T(8,128)(2,1)}, bf16[2048,768]{1,0:T(8,128)(2,1)}, bf16[512,768]{1,0:T(8,128)(2,1)}, ...), branch_computations={%region_0.1_spmd, %region_1.2_spmd} | conditional | bytes 18874512 | solution.py:642
  70.8 6.0 %grad_back.1 = (f32[8,128]{1,0:T(8,128)S(1)}, bf16[768,768]{1,0:T(8,128)(2,1)}, bf16[768,768]{1,0:T(8,128)(2,1)}) custom-call(f32[8,128]{1,0:T(8,128)S(1)} %get-tuple-element.100.token_ref, bf16[512,1536]{1,0:T(8,128)(2,1)} %get-tuple-element.101.refs_0_, bf16[512,1536]{1,0:T(8,128)(2,1)} %get-tuple-element.102.refs_1_, ...), custom_call_target="tpu_custom_call", output_to_operand_aliasing={{0}: (0, {})} | custom-call | tf_op jit(solution)/shard_map/cond/branch_1_fun/grad_back/pallas_call | solution.py:52
  76.8 6.0 %grad_in.1 = (f32[8,128]{1,0:T(8,128)S(1)}, bf16[768,768]{1,0:T(8,128)(2,1)}, bf16[768,768]{1,0:T(8,128)(2,1)}) custom-call(f32[8,128]{1,0:T(8,128)S(1)} %get-tuple-element.104.token_ref, bf16[512,768]{1,0:T(8,128)(2,1)} %get-tuple-element.105.refs_0_, bf16[512,768]{1,0:T(8,128)(2,1)} %get-tuple-element.106.refs_1_, ...), custom_call_target="tpu_custom_call", output_to_operand_aliasing={{0}: (0, {})} | custom-call | tf_op jit(solution)/shard_map/cond/branch_1_fun/grad_in/pallas_call | solution.py:52
  82.9 0.5 collective-permute-start
  83.4 2.5 collective-permute-done.1.refs_3_
  85.9 1.7 collective-permute-done.refs_1_
  87.6 1.0 copy-done.11
  88.6 4.3 %sum_core.1 = (f32[8,128]{1,0:T(8,128)S(1)}, bf16[768,768]{1,0:T(8,128)(2,1)}, bf16[768,768]{1,0:T(8,128)(2,1)}) custom-call(f32[8,128]{1,0:T(8,128)S(1)} %get-tuple-element.109.token_ref, bf16[768,768]{1,0:T(8,128)(2,1)} %get-tuple-element.110.refs_0_, bf16[768,768]{1,0:T(8,128)(2,1)} %copy-done.11, ...), custom_call_target="tpu_custom_call", output_to_operand_aliasing={{0}: (0, {})} | custom-call | tf_op jit(solution)/shard_map/cond/branch_1_fun/sum_core/pallas_call | solution.py:52
  93.0 169.1 %conditional.4 = (f32[8,128]{1,0:T(8,128)S(1)}, bf16[2048,768]{1,0:T(8,128)(2,1)}, f32[2048,768]{1,0:T(8,128)}, f32[768]{0:T(1024)}, f32[3,768,192]{1,2,0:T(8,12...) conditional(s32[]{:T(128)} %convert_element_type.17, () %tuple.31, (pred[]{:T(512)}, ...), branch_computations={%region_2.3_spmd, %region_3.6_spmd} | conditional | flops 2414081 | bytes 72538616 | solution.py:642
  93.0 13.0 %attn_bwd.3 = (f32[8,128]{1,0:T(8,128)S(1)}, f32[512,768]{1,0:T(8,128)}, bf16[512,768]{1,0:T(8,128)(2,1)}, f32[1,768]{1,0:T(1,128)}, bf16[512,1152]{1,0:T(8,128)...) custom-call(f32[8,128]{1,0:T(8,128)S(1)} %get-tuple-element.141.token_ref, ...), custom_call_target="tpu_custom_call", output_to_operand_aliasing={{0}: (0, {})} | custom-call | tf_op jit(solution)/shard_map/cond/branch_1_fun/attn_bwd/pallas_call | solution.py:52
  106.0 2.0 collective-permute-start.2
  108.1 19.9 %conditional = (f32[8,128]{1,0:T(8,128)S(1)}, f32[512,768]{1,0:T(8,128)}, f32[1,768]{1,0:T(1,128)S(1)}, bf16[512,768]{1,0:T(8,128)(2,1)}, f32[3,2,1024]{2,1,0:T(2,128)S(1)}, /*index=5*/bf16[1536,768]{1,0:T(8,128)(2,1)}) conditional(s32[]{:T(128)} %convert_element_type.3, () %tuple.22, (f32[8,128]{1,0:T(8,128)S(1)}, f32[512,768]{1,0:T(8,128)}, ...), branch_computations={%region_4.4_spmd, %region_5.5_spmd} | conditional | bytes 4750404 | solution.py:642
  108.1 13.0 %attn_bwd.2 = (f32[8,128]{1,0:T(8,128)S(1)}, f32[512,768]{1,0:T(8,128)}, bf16[512,768]{1,0:T(8,128)(2,1)}, f32[1,768]{1,0:T(1,128)S(1)}, bf16[512,1152]{1,0:T(8,...) custom-call(f32[8,128]{1,0:T(8,128)S(1)} %get-tuple-element.114.token_ref, ...), custom_call_target="tpu_custom_call", output_to_operand_aliasing={{0}: (0, {})} | custom-call | tf_op jit(solution)/shard_map/cond/branch_1_fun/cond/branch_1_fun/attn_bwd/pallas_call | solution.py:52
  121.1 6.9 %grad_attn.1 = (f32[8,128]{1,0:T(8,128)S(1)}, bf16[1536,768]{1,0:T(8,128)(2,1)}) custom-call(f32[8,128]{1,0:T(8,128)S(1)} %get-tuple-element.125.token_ref, bf16[512,768]{1,0:T(8,128)(2,1)} %get-tuple-element.126.refs_0_, bf16[512,768]{1,0:T(8,128)(2,1)} %get-tuple-element.127.refs_1_, ...), custom_call_target="tpu_custom_call", output_to_operand_aliasing={{0}: (0, {})} | custom-call | tf_op jit(solution)/shard_map/cond/branch_1_fun/cond/branch_1_fun/grad_attn/pallas_call | solution.py:52
  128.0 2.1 copy.86.refs_0_
  130.1 6.0 %all-to-all-start = ((bf16[16,96,768]{2,1,0:T(8,128)(2,1)}), bf16[16,96,768]{2,1,0:T(8,128)(2,1)}, u32[]{:S(2)}, u32[]{:S(2)}) async-start(bf16[16,96,768]{2,1,0:T(8,128)(2,1)} %bitcast), calls=%async_computation | async-start | bytes 4718592 | tf_op jit(solution)/shard_map/cond/branch_1_fun/all_to_all | solution.py:660
  136.1 0.7 collective-permute-start.3
  136.8 2.1 copy.92.refs_0_
  138.8 0.9 copy.90.refs_0_
  139.7 16.5 %collective-permute-done.3.refs_7_ = bf16[512,768]{1,0:T(8,128)(2,1)} collective-permute-done((bf16[512,768]{1,0:T(8,128)(2,1)}, bf16[512,768]{1,0:T(8,128)(2,1)}, u32[]{:S(2)}, u32[]{:S(2)}) %collective-permute-start.3) | collective-permute-done | bytes 786464 | tf_op jit(solution)/shard_map/cond/branch_1_fun/ppermute | solution.py:657
  156.3 7.2 %grad_input.1 = (f32[8,128]{1,0:T(8,128)S(1)}, f32[2048,768]{1,0:T(8,128)}, f32[1024,768]{1,0:T(8,128)}, f32[1,768]{1,0:T(1,128)}) custom-call(f32[8,128]{1,0:T(8,128)S(1)} %get-tuple-element.173.token_ref, bf16[2048,768]{1,0:T(8,128)(2,1)S(1)} %get-tuple-element.174.refs_0_, ...), custom_call_target="tpu_custom_call", output_to_operand_aliasing={{0}: (0, {})} | custom-call | tf_op jit(solution)/shard_map/cond/branch_1_fun/grad_input/pallas_call | solution.py:52
  163.4 0.6 collective-permute-start.6
  164.0 1.4 collective-permute-start.5
  165.4 43.9 %all-to-all-done = bf16[16,96,768]{2,1,0:T(8,128)(2,1)} async-done(((bf16[16,96,768]{2,1,0:T(8,128)(2,1)}), bf16[16,96,768]{2,1,0:T(8,128)(2,1)}, u32[]{:S(2)}, u32[]{:S(2)}) %all-to-all-start) | async-done | bytes 2359328 | tf_op jit(solution)/shard_map/cond/branch_1_fun/all_to_all | solution.py:660
  209.3 5.8 %sum_parts.1 = (f32[8,128]{1,0:T(8,128)S(1)}, bf16[768,768]{1,0:T(8,128)(2,1)}) custom-call(f32[8,128]{1,0:T(8,128)S(1)} %get-tuple-element.178.token_ref, bf16[1536,768]{1,0:T(8,128)(2,1)} %bitcast.1.refs_0_), custom_call_target="tpu_custom_call", output_to_operand_aliasing={{0}: (0, {})} | custom-call | tf_op jit(solution)/shard_map/cond/branch_1_fun/sum_parts/pallas_call | solution.py:52
  215.2 12.1 %all-to-all-start.1 = ((bf16[8,96,768]{2,1,0:T(8,128)(2,1)}), bf16[8,96,768]{2,1,0:T(8,128)(2,1)S(1)}, u32[]{:S(2)}, u32[]{:S(2)}) async-start(bf16[8,96,768]{2,1,0:T(8,128)(2,1)} %bitcast.18), calls=%async_computation.1 | async-start | bytes 2359296 | tf_op jit(solution)/shard_map/cond/branch_1_fun/all_to_all | solution.py:663
  227.3 4.3 %place.2 = (f32[8,128]{1,0:T(8,128)S(1)}, f32[2048,768]{1,0:T(8,128)}) custom-call(f32[8,128]{1,0:T(8,128)S(1)} %get-tuple-element.180.token_ref, f32[2048,768]{1,0:T(8,128)} %get-tuple-element.181.refs_0_, f32[1024,768]{1,0:T(8,128)} %collective-permute-done.4.refs_1_), custom_call_target="tpu_custom_call", output_to_operand_aliasing={{0}: (0, {}), {1}: (1, {})} | custom-call | tf_op jit(solution)/shard_map/cond/branch_1_fun/place/pallas_call | solution.py:52
  231.6 0.9 copy-done.12
  232.5 4.8 %mix.1 = (f32[8,128]{1,0:T(8,128)S(1)}, bf16[2048,768]{1,0:T(8,128)(2,1)}, bf16[1024,768]{1,0:T(8,128)(2,1)}) custom-call(f32[8,128]{1,0:T(8,128)S(1)} %get-tuple-element.183.token_ref, f32[512,768]{1,0:T(8,128)} %get-tuple-element.142.refs_0_, f32[512,768]{1,0:T(8,128)} %get-tuple-element.153.refs_1_, ...), custom_call_target="tpu_custom_call", output_to_operand_aliasing={{0}: (0, {})} | custom-call | tf_op jit(solution)/shard_map/cond/branch_1_fun/mix/pallas_call | solution.py:52
  237.4 0.3 copy.62
  237.7 0.5 slice.49
  238.3 0.7 pad_add_fusion
  239.0 0.4 fusion
  239.6 0.6 collective-permute-start.7
  240.2 0.7 collective-permute-done.7
  240.9 2.0 collective-permute-start.8
  243.0 1.7 collective-permute-done.8
  244.7 2.2 collective-permute-start.9
  246.9 1.6 collective-permute-done.9
  248.5 2.7 collective-permute-start.10
  251.2 4.3 %collective-permute-done.10 = f32[1632]{0:T(1024)S(1)} collective-permute-done((f32[1632]{0:T(1024)S(1)}, f32[1632]{0:T(1024)S(1)}, u32[]{:S(2)}, u32[]{:S(2)}) %collective-permute-start.10) | collective-permute-done | bytes 6560 | tf_op jit(solution)/shard_map/cond/branch_1_fun/ppermute | solution.py:763
  255.6 0.1 copy.61
  255.8 0.5 copy-done.13
  256.3 3.6 %place.3 = (f32[8,128]{1,0:T(8,128)S(1)}, bf16[2048,768]{1,0:T(8,128)(2,1)}) custom-call(f32[8,128]{1,0:T(8,128)S(1)} %need.5.token_ref, bf16[2048,768]{1,0:T(8,128)(2,1)} %get-tuple-element.193.refs_0_, bf16[1024,768]{1,0:T(8,128)(2,1)} %collective-permute-done.11.refs_1_), custom_call_target="tpu_custom_call", output_to_operand_aliasing={{0}: (0, {}), {1}: (1, {})} | custom-call | tf_op jit(solution)/shard_map/cond/branch_1_fun/place/pallas_call | solution.py:52
  259.9 0.9 slice.55
  260.7 1.4 slice.54
  262.1 4.3 %widen.1 = (f32[8,128]{1,0:T(8,128)S(1)}, f32[768,768]{1,0:T(8,128)}, f32[768,768]{1,0:T(8,128)}) custom-call(f32[8,128]{1,0:T(8,128)S(1)} %get-tuple-element.298.token_ref, bf16[768,768]{1,0:T(8,128)(2,1)} %get-tuple-element.348.refs_0_, bf16[768,768]{1,0:T(8,128)(2,1)} %get-tuple-element.349.refs_1_), custom_call_target="tpu_custom_call", output_to_operand_aliasing={{0}: (0, {})} | custom-call | tf_op jit(solution)/shard_map/widen/pallas_call | solution.py:52
  (99 shorter events, 1.0 us)
Async XLA Ops:
  7.2 2.5 copy-start.2
  7.2 5.2 %copy-start.20 = (bf16[768]{0:T(1024)(128)(2,1)S(1)}, bf16[768]{0:T(1024)(128)(2,1)}, u32[]{:S(2)}) copy-start(bf16[768]{0:T(1024)(128)(2,1)} %param.18) | copy-start | bytes 4612
  7.2 5.2 %copy-start.21 = (bf16[768]{0:T(1024)(128)(2,1)S(1)}, bf16[768]{0:T(1024)(128)(2,1)}, u32[]{:S(2)}) copy-start(bf16[768]{0:T(1024)(128)(2,1)} %param.21) | copy-start | bytes 4612
  7.2 254.9 %all-reduce.4.cloned.1.call-start = ((), (), s32[]{:S(2)}) async-start(), calls=%async_computation.2 | async-start | bytes 4718592 | tf_op jit(solution)/shard_map/psum | solution.py:715
  8.7 4.0 %copy-start.3 = (bf16[784,768]{1,0:T(8,128)(2,1)}, bf16[784,768]{1,0:T(8,128)(2,1)S(1)}, u32[]{:S(2)}) copy-start(bf16[784,768]{1,0:T(8,128)(2,1)S(1)} %fusion.3.refs_3_) | copy-start | bytes 3612676
  8.7 4.0 %collective-permute-start.12 = (bf16[784,768]{1,0:T(8,128)(2,1)S(1)}, bf16[784,768]{1,0:T(8,128)(2,1)S(1)}, u32[]{:S(2)}, u32[]{:S(2)}) collective-permute-start(bf16[784,768]{1,0:T(8,128)(2,1)S(1)} %fusion.3.refs_3_), channel_id=1, source_target_pairs={{0,8},{8,0},{1,9},{9,1},{2,10},{10,2},{3,11},{11,3},{4,12},{12,4},... | collective-permute-start | bytes 3612680 | tf_op jit(solution)/shard_map/ppermute | solution.py:654
  9.2 26.8 %collective-permute-start.17 = (bf16[768,768]{1,0:T(8,128)(2,1)}, bf16[768,768]{1,0:T(8,128)(2,1)}, u32[]{:S(2)}, u32[]{:S(2)}) collective-permute-start(bf16[768,768]{1,0:T(8,128)(2,1)} %refs_9_.3), channel_id=1, source_target_pairs={{0,8},{8,0},{1,9},{9,1},{2,10},{10,2},{3,11},{11,3},{4,12},{12,4},... | collective-permute-start | bytes 3538952 | tf_op jit(solution)/shard_map/ppermute | solution.py:654
  9.3 26.7 %collective-permute-start.18 = (bf16[768,768]{1,0:T(8,128)(2,1)}, bf16[768,768]{1,0:T(8,128)(2,1)}, u32[]{:S(2)}, u32[]{:S(2)}) collective-permute-start(bf16[768,768]{1,0:T(8,128)(2,1)} %refs_11_.3), channel_id=1, source_target_pairs={{0,8},{8,0},{1,9},{9,1},{2,10},{10,2},{3,11},{11,3},{4,12},{12,4},... | collective-permute-start | bytes 3538952 | tf_op jit(solution)/shard_map/ppermute | solution.py:654
  9.7 17.0 %collective-permute-start.13 = (bf16[192,768]{1,0:T(8,128)(2,1)S(1)}, bf16[192,768]{1,0:T(8,128)(2,1)}, u32[]{:S(2)}, u32[]{:S(2)}) collective-permute-start(bf16[192,768]{1,0:T(8,128)(2,1)S(1)} %copy-done.2), channel_id=1, source_target_pairs={{0,16},{16,0},{1,17},{17,1},{2,18},{18,2},{3,19},{19,3},{4,20},{20... | collective-permute-start | bytes 884744 | tf_op jit(solution)/shard_map/ppermute | solution.py:657
  12.3 23.7 %collective-permute-start.15 = (bf16[192,768]{1,0:T(8,128)(2,1)S(1)}, bf16[192,768]{1,0:T(8,128)(2,1)S(1)}, u32[]{:S(2)}, u32[]{:S(2)}) collective-permute-start(bf16[192,768]{1,0:T(8,128)(2,1)S(1)} %copy-done.2), channel_id=1, source_target_pairs={{0,8},{8,0},{1,9},{9,1},{2,10},{10,2},{3,11},{11,3},{4,12},{12,4},... | collective-permute-start | bytes 884744 | tf_op jit(solution)/shard_map/ppermute | solution.py:654
  12.6 1.0 copy-start.8
  13.7 13.0 %copy-start = (bf16[2048,768]{1,0:T(8,128)(2,1)S(1)}, bf16[2048,768]{1,0:T(8,128)(2,1)}, u32[]{:S(2)}) copy-start(bf16[2048,768]{1,0:T(8,128)(2,1)} %refs_0_.7) | copy-start | bytes 9437188
  23.8 14.0 %collective-permute-start.14 = (bf16[512,384]{1,0:T(8,128)(2,1)}, bf16[512,384]{1,0:T(8,128)(2,1)}, u32[]{:S(2)}, u32[]{:S(2)}) collective-permute-start(bf16[512,384]{1,0:T(8,128)(2,1)} %get-tuple-element.261.refs_1_), channel_id=1, source_target_pairs={{0,16},{16,0},{1,17},{17,1},{2,18},{18,2},{3,19},{19,3},{4,20},{20... | collective-permute-start | bytes 1179656 | tf_op jit(solution)/shard_map/ppermute | solution.py:657
  35.9 17.6 %collective-permute-start.19 = (bf16[512,384]{1,0:T(8,128)(2,1)}, bf16[512,384]{1,0:T(8,128)(2,1)}, u32[]{:S(2)}, u32[]{:S(2)}) collective-permute-start(bf16[512,384]{1,0:T(8,128)(2,1)} %get-tuple-element.264.refs_1_), channel_id=1, source_target_pairs={{0,16},{16,0},{1,17},{17,1},{2,18},{18,2},{3,19},{19,3},{4,20},{20... | collective-permute-start | bytes 1179656 | tf_op jit(solution)/shard_map/ppermute | solution.py:657
  35.9 19.5 %copy-start.4 = (bf16[192,768]{1,0:T(8,128)(2,1)}, bf16[192,768]{1,0:T(8,128)(2,1)S(1)}, u32[]{:S(2)}) copy-start(bf16[192,768]{1,0:T(8,128)(2,1)S(1)} %collective-permute-done.15.refs_4_) | copy-start | bytes 884740
  35.9 1.8 collective-permute-start.16
  37.8 0.7 copy-start.9
  53.5 39.4 %collective-permute-start.20 = (bf16[512,768]{1,0:T(8,128)(2,1)}, bf16[512,768]{1,0:T(8,128)(2,1)}, u32[]{:S(2)}, u32[]{:S(2)}) collective-permute-start(bf16[512,768]{1,0:T(8,128)(2,1)} %get-tuple-element.277), channel_id=1, source_target_pairs={{0,16},{16,0},{1,17},{17,1},{2,18},{18,2},{3,19},{19,3},{4,20},{20... | collective-permute-start | bytes 2359304 | tf_op jit(solution)/shard_map/ppermute | solution.py:657
  68.6 2.2 copy-start.22
  70.7 22.3 %collective-permute-start.21 = (bf16[512,768]{1,0:T(8,128)(2,1)}, bf16[512,768]{1,0:T(8,128)(2,1)}, u32[]{:S(2)}, u32[]{:S(2)}) collective-permute-start(bf16[512,768]{1,0:T(8,128)(2,1)} %get-tuple-element.278), channel_id=1, source_target_pairs={{0,16},{16,0},{1,17},{17,1},{2,18},{18,2},{3,19},{19,3},{4,20},{20... | collective-permute-start | bytes 2359304 | tf_op jit(solution)/shard_map/ppermute | solution.py:657
  82.9 3.1 %collective-permute-start.1 = (bf16[768,768]{1,0:T(8,128)(2,1)}, bf16[768,768]{1,0:T(8,128)(2,1)S(1)}, u32[]{:S(2)}, u32[]{:S(2)}) collective-permute-start(bf16[768,768]{1,0:T(8,128)(2,1)} %get-tuple-element.113), channel_id=1, source_target_pairs={{0,8},{8,0},{1,9},{9,1},{2,10},{10,2},{3,11},{11,3},{4,12},{12,4},... | collective-permute-start | bytes 3538952 | tf_op jit(solution)/shard_map/cond/branch_1_fun/ppermute | solution.py:654
  82.9 4.7 %collective-permute-start = (bf16[768,768]{1,0:T(8,128)(2,1)}, bf16[768,768]{1,0:T(8,128)(2,1)S(1)}, u32[]{:S(2)}, u32[]{:S(2)}) collective-permute-start(bf16[768,768]{1,0:T(8,128)(2,1)} %get-tuple-element.111), channel_id=1, source_target_pairs={{0,8},{8,0},{1,9},{9,1},{2,10},{10,2},{3,11},{11,3},{4,12},{12,4},... | collective-permute-start | bytes 3538952 | tf_op jit(solution)/shard_map/cond/branch_1_fun/ppermute | solution.py:654
  85.9 1.7 copy-start.10
  87.6 1.0 copy-start.11
  106.0 24.0 %collective-permute-start.2 = (bf16[512,768]{1,0:T(8,128)(2,1)}, bf16[512,768]{1,0:T(8,128)(2,1)}, u32[]{:S(2)}, u32[]{:S(2)}) collective-permute-start(bf16[512,768]{1,0:T(8,128)(2,1)} %get-tuple-element.165.refs_4_), channel_id=1, source_target_pairs={{0,16},{16,0},{1,17},{17,1},{2,18},{18,2},{3,19},{19,3},{4,20},{20... | collective-permute-start | bytes 2359304 | tf_op jit(solution)/shard_map/cond/branch_1_fun/ppermute | solution.py:657
  108.1 13.0 %copy-start.7 = (bf16[512,384]{1,0:T(8,128)(2,1)S(1)}, bf16[512,384]{1,0:T(8,128)(2,1)}, u32[]{:S(2)}) copy-start(bf16[512,384]{1,0:T(8,128)(2,1)} %get-tuple-element.132.refs_6_) | copy-start | bytes 1179652 | tf_op jit(solution)/shard_map/cond/branch_1_fun/cond
  130.1 79.3 %all-to-all-start = ((bf16[16,96,768]{2,1,0:T(8,128)(2,1)}), bf16[16,96,768]{2,1,0:T(8,128)(2,1)}, u32[]{:S(2)}, u32[]{:S(2)}) async-start(bf16[16,96,768]{2,1,0:T(8,128)(2,1)} %bitcast), calls=%async_computation | async-start | bytes 4718592 | tf_op jit(solution)/shard_map/cond/branch_1_fun/all_to_all | solution.py:660
  136.1 2.8 %copy-start.5 = (bf16[512,768]{1,0:T(8,128)(2,1)S(1)}, bf16[512,768]{1,0:T(8,128)(2,1)}, u32[]{:S(2)}) copy-start(bf16[512,768]{1,0:T(8,128)(2,1)} %get-tuple-element.170.refs_2_) | copy-start | bytes 2359300 | tf_op jit(solution)/shard_map/cond
  136.1 20.2 %collective-permute-start.3 = (bf16[512,768]{1,0:T(8,128)(2,1)}, bf16[512,768]{1,0:T(8,128)(2,1)}, u32[]{:S(2)}, u32[]{:S(2)}) collective-permute-start(bf16[512,768]{1,0:T(8,128)(2,1)} %get-tuple-element.177), channel_id=1, source_target_pairs={{0,16},{16,0},{1,17},{17,1},{2,18},{18,2},{3,19},{19,3},{4,20},{20... | collective-permute-start | bytes 2359304 | tf_op jit(solution)/shard_map/cond/branch_1_fun/ppermute | solution.py:657
  163.4 63.9 %collective-permute-start.4 = (f32[1024,768]{1,0:T(8,128)}, f32[1024,768]{1,0:T(8,128)}, u32[]{:S(2)}, u32[]{:S(2)}) collective-permute-start(f32[1024,768]{1,0:T(8,128)} %get-tuple-element.182), channel_id=1, source_target_pairs={{0,8},{8,0},{1,9},{9,1},{2,10},{10,2},{3,11},{11,3},{4,12},{12,4},... | collective-permute-start | bytes 9437192 | tf_op jit(solution)/shard_map/cond/branch_1_fun/ppermute | solution.py:654
  163.4 68.2 %collective-permute-start.6 = (bf16[512,768]{1,0:T(8,128)(2,1)}, bf16[512,768]{1,0:T(8,128)(2,1)S(1)}, u32[]{:S(2)}, u32[]{:S(2)}) collective-permute-start(bf16[512,768]{1,0:T(8,128)(2,1)} %get-tuple-element.185), channel_id=1, source_target_pairs={{0,16},{16,0},{1,17},{17,1},{2,18},{18,2},{3,19},{19,3},{4,20},{20... | collective-permute-start | bytes 2359304 | tf_op jit(solution)/shard_map/cond/branch_1_fun/ppermute | solution.py:657
  164.0 67.6 %collective-permute-start.5 = (bf16[512,768]{1,0:T(8,128)(2,1)}, bf16[512,768]{1,0:T(8,128)(2,1)}, u32[]{:S(2)}, u32[]{:S(2)}) collective-permute-start(bf16[512,768]{1,0:T(8,128)(2,1)} %get-tuple-element.184), channel_id=1, source_target_pairs={{0,16},{16,0},{1,17},{17,1},{2,18},{18,2},{3,19},{19,3},{4,20},{20... | collective-permute-start | bytes 2359304 | tf_op jit(solution)/shard_map/cond/branch_1_fun/ppermute | solution.py:657
  215.2 44.7 %all-to-all-start.1 = ((bf16[8,96,768]{2,1,0:T(8,128)(2,1)}), bf16[8,96,768]{2,1,0:T(8,128)(2,1)S(1)}, u32[]{:S(2)}, u32[]{:S(2)}) async-start(bf16[8,96,768]{2,1,0:T(8,128)(2,1)} %bitcast.18), calls=%async_computation.1 | async-start | bytes 2359296 | tf_op jit(solution)/shard_map/cond/branch_1_fun/all_to_all | solution.py:663
  227.3 5.2 %copy-start.6 = (bf16[512,768]{1,0:T(8,128)(2,1)S(1)}, bf16[512,768]{1,0:T(8,128)(2,1)}, u32[]{:S(2)}) copy-start(bf16[512,768]{1,0:T(8,128)(2,1)} %get-tuple-element.170.refs_2_) | copy-start | bytes 2359300 | tf_op jit(solution)/shard_map/cond
  231.6 0.9 copy-start.12
  232.5 4.9 %copy-start.1 = (s32[512,512]{1,0:T(8,128)S(1)}, s32[512,512]{1,0:T(8,128)}, u32[]{:S(2)}) copy-start(s32[512,512]{1,0:T(8,128)} %get-tuple-element.337) | copy-start | bytes 3145732 | tf_op jit(solution)/shard_map/cond
  237.3 1.0 copy-start.14
  237.3 2.2 copy-start.17
  237.3 2.2 copy-start.18
  237.3 19.0 %collective-permute-start.11 = (bf16[1024,768]{1,0:T(8,128)(2,1)}, bf16[1024,768]{1,0:T(8,128)(2,1)}, u32[]{:S(2)}, u32[]{:S(2)}) collective-permute-start(bf16[1024,768]{1,0:T(8,128)(2,1)} %get-tuple-element.194), channel_id=1, source_target_pairs={{0,8},{8,0},{1,9},{9,1},{2,10},{10,2},{3,11},{11,3},{4,12},{12,4},... | collective-permute-start | bytes 4718600 | tf_op jit(solution)/shard_map/cond/branch_1_fun/ppermute | solution.py:654
  239.6 1.4 collective-permute-start.7
  240.9 3.7 %collective-permute-start.8 = (f32[1632]{0:T(1024)S(1)}, f32[1632]{0:T(1024)S(1)}, u32[]{:S(2)}, u32[]{:S(2)}) collective-permute-start(f32[1632]{0:T(1024)S(1)} %maximum_add_fusion), channel_id=1, source_target_pairs={{0,1},{1,0},{2,3},{3,2},{4,5},{5,4},{6,7},{7,6},{8,9},{9,8},{10,11... | collective-permute-start | bytes 19592 | tf_op jit(solution)/shard_map/cond/branch_1_fun/ppermute | solution.py:763
  244.7 3.8 %collective-permute-start.9 = (f32[1632]{0:T(1024)S(1)}, f32[1632]{0:T(1024)S(1)}, u32[]{:S(2)}, u32[]{:S(2)}) collective-permute-start(f32[1632]{0:T(1024)S(1)} %add.19), channel_id=1, source_target_pairs={{0,2},{1,3},{2,0},{3,1},{4,6},{5,7},{6,4},{7,5},{8,10},{9,11},{10,... | collective-permute-start | bytes 19592 | tf_op jit(solution)/shard_map/cond/branch_1_fun/ppermute | solution.py:763
  248.5 7.0 %collective-permute-start.10 = (f32[1632]{0:T(1024)S(1)}, f32[1632]{0:T(1024)S(1)}, u32[]{:S(2)}, u32[]{:S(2)}) collective-permute-start(f32[1632]{0:T(1024)S(1)} %add.20), channel_id=1, source_target_pairs={{0,4},{1,5},{2,6},{3,7},{4,0},{5,1},{6,2},{7,3},{8,12},{9,13},{10,... | collective-permute-start | bytes 19592 | tf_op jit(solution)/shard_map/cond/branch_1_fun/ppermute | solution.py:763
  255.7 0.6 copy-start.13
  255.7 4.1 %copy-start.15 = (f32[768]{0:T(1024)}, f32[768]{0:T(1024)S(1)}, u32[]{:S(2)}) copy-start(f32[768]{0:T(1024)S(1)} %get-tuple-element.386.refs_1_) | copy-start | bytes 9220 | tf_op jit(solution)/shard_map/cond
  255.7 4.1 %copy-start.16 = (f32[768]{0:T(1024)}, f32[768]{0:T(1024)S(1)}, u32[]{:S(2)}) copy-start(f32[768]{0:T(1024)S(1)} %get-tuple-element.383.refs_0_) | copy-start | bytes 9220 | tf_op jit(solution)/shard_map/cond
  262.1 4.3 %copy-start.19 = (f32[32,3]{0,1:T(4,128)}, f32[32,3]{0,1:T(4,128)S(1)}, u32[]{:S(2)}) copy-start(f32[32,3]{0,1:T(4,128)S(1)} %get-tuple-element.347) | copy-start | bytes 1156
Sparse Core Ops, SparseCore 0:
  93.1 134.0 all-reduce.3

commit v3 on v2

--- a/solution.py
+++ b/solution.py
@@ -15,7 +15,7 @@
 GELU_C = 0.7978845608028654
 GELU_A = 0.044715
 CHUNK = 256
-VMEM_BYTES = 60 * 1024 * 1024
+VMEM_BYTES = 18 * 1024 * 1024
 
 F32 = jnp.float32
 BF16 = jnp.bfloat16
@@ -190,14 +190,23 @@
     )
 
 
-def ffn_kernel(
-    src_ref, att_own_ref, att_oth_ref, wo_a_ref, wo_b_ref, wo_x_ref, wo_xc_ref, gains_ref, cot_ref,
-    in_a_ref, in_b_ref, back_a_ref, back_b_ref,
-    middle_ref, normed_ref, gsend_ref, hsend_ref, hid_ref, gpre_ref, acc_ref, gacc_ref,
-):
-    rows, width = src_ref.shape
-    cols = width // 4
+TILE = 256
+
+
+def ffn_kernel(first, *refs):
+    (
+        src_ref, att_own_ref, att_oth_ref, wo_a_ref, wo_b_ref, wo_x_ref, wo_xc_ref, gains_ref, cot_ref,
+        in_a_ref, in_b_ref, back_a_ref, back_b_ref, *refs,
+    ) = refs
+    if not first:
+        gback_a_in, gback_b_in, gin_a_in, gin_b_in, *refs = refs
+    (
+        middle_ref, gsend_ref, hsend_ref, gback_a_ref, gback_b_ref, gin_a_ref, gin_b_ref,
+        normed_ref, normed_t_ref, acc_ref, gacc_ref,
+    ) = refs
+    rows = src_ref.shape[0]
     step = pl.program_id(0)
+    half = pl.num_programs(0) // 2
 
     @pl.when(step == 0)
     def _():
@@ -212,110 +221,106 @@
             terms = dot_nn(jnp.where(swapped, oth, own), wo_0) + dot_nn(jnp.where(swapped, own, oth), wo_1)
             m = src_ref[at, :].astype(F32) + terms
             middle_ref[at, :] = m
-            normed_ref[at, :] = (m * rms_rows(m) * gains_ref[1:, :]).astype(BF16)
-
-    w_in = jnp.where(step == 0, in_a_ref[...], in_b_ref[...])
-    w_back = jnp.where(step == 0, back_a_ref[...], back_b_ref[...])
-    for start in range(0, rows, CHUNK):
-        at = slice(start, start + CHUNK)
+            normed = (m * rms_rows(m) * gains_ref[1:, :]).astype(BF16)
+            normed_ref[at, :] = normed
+            normed_t_ref[:, at] = normed.T
+        acc_ref[...] = jnp.zeros(acc_ref.shape, F32)
+        gacc_ref[...] = jnp.zeros(gacc_ref.shape, F32)
+
+    mine = step < half
+    w_in = jnp.where(mine, in_a_ref[...], in_b_ref[...])
+    w_back = jnp.where(mine, back_a_ref[...], back_b_ref[...])
+    hiddens, gpres = [], []
+    for start in range(0, rows, 2 * CHUNK):
+        at = slice(start, start + 2 * CHUNK)
         pre = dot_nn(normed_ref[at, :], w_in)
         ghid = dot_nt(cot_ref[at, :], w_back)
         sq = pre * pre
-        t = jnp.tanh(GELU_C * (pre + GELU_A * sq * pre))
-        half_t = 0.5 * (1.0 + t)
-        hidden = (pre * half_t).astype(BF16)
-        slope = half_t + 0.5 * pre * (1.0 - t * t) * (GELU_C * (1.0 + 3.0 * GELU_A * sq))
+        t = jnp.tanh(pre * (GELU_C + (GELU_C * GELU_A) * sq))
+        half_t = 0.5 + 0.5 * t
+        act = pre * half_t
+        hidden = act.astype(BF16)
+        slope = half_t + (act * (1.0 - t)) * (GELU_C + (3.0 * GELU_C * GELU_A) * sq)
         gpre = (ghid * slope).astype(BF16)
-        out = dot_nn(hidden, w_back)
-        gnorm = dot_nt(gpre, w_in)
-        hid_ref[at, :] = hidden
-        gpre_ref[at, :] = gpre
-
-        @pl.when(step == 0)
-        def _():
-            acc_ref[at, :] = out
-            gacc_ref[at, :] = gnorm
-
-        @pl.when(step != 0)
-        def _():
-            hsend_ref[at, :] = (acc_ref[at, :] + out).astype(BF16)
-            gsend_ref[at, :] = (gacc_ref[at, :] + gnorm).astype(BF16)
-
-
-def ffn(ids, inputs, att_own, att_oth, wos, gains, cotangent, w_ins, w_backs, doc, docs):
+        acc_ref[at, :] += dot_nn(hidden, w_back)
+        gacc_ref[at, :] += dot_nt(gpre, w_in)
+        hiddens.append(hidden)
+        gpres.append(gpre)
+    gback = dot_tn(jnp.concatenate(hiddens, axis=0), cot_ref[...])
+    gin = dot_nn(normed_t_ref[...], jnp.concatenate(gpres, axis=0))
+
+    @pl.when(mine)
+    def _():
+        if first:
+            gback_a_ref[...] = gback.astype(BF16)
+            gin_a_ref[...] = gin.astype(BF16)
+        else:
+            gback_a_ref[...] = (gback + gback_a_in[...].astype(F32)).astype(BF16)
+            gin_a_ref[...] = (gin + gin_a_in[...].astype(F32)).astype(BF16)
+
+    @pl.when(jnp.logical_not(mine))
+    def _():
+        if first:
+            gback_b_ref[...] = gback.astype(BF16)
+            gin_b_ref[...] = gin.astype(BF16)
+        else:
+            gback_b_ref[...] = (gback + gback_b_in[...].astype(F32)).astype(BF16)
+            gin_b_ref[...] = (gin + gin_b_in[...].astype(F32)).astype(BF16)
+
+    @pl.when(step == 2 * half - 1)
+    def _():
+        hsend_ref[...] = acc_ref[...].astype(BF16)
+        gsend_ref[...] = gacc_ref[...].astype(BF16)
+
+
+def ffn(ids, inputs, att_own, att_oth, wos, gains, cotangent, w_ins, w_backs, grads, doc, docs):
     seq = att_own.shape[0]
     width = inputs.shape[1]
     units = w_ins[0].shape[1]
+    tiles = units // TILE
     mine = doc_rows(seq, width, docs, doc)
+
+    def first_half(i):
+        return jnp.minimum(i, tiles - 1)
+
+    def second_half(i):
+        return jnp.maximum(i - tiles, 0)
+
+    def back_spec(of):
+        return pl.BlockSpec((TILE, width), lambda i: (of(i), 0))
+
+    def in_spec(of):
+        return pl.BlockSpec((width, TILE), lambda i: (0, of(i)))
+
+    grad_specs = [back_spec(first_half), back_spec(second_half), in_spec(first_half), in_spec(second_half)]
     outs = [
         shape_of((seq, width), F32),
         shape_of((seq, width), BF16),
         shape_of((seq, width), BF16),
-        shape_of((seq, width), BF16),
-        shape_of((seq, 2 * units), BF16),
-        shape_of((seq, 2 * units), BF16),
+        shape_of((units, width), BF16),
+        shape_of((units, width), BF16),
+        shape_of((width, units), BF16),
+        shape_of((width, units), BF16),
     ]
     return call(
-        ffn_kernel,
+        functools.partial(ffn_kernel, grads is None),
         "ffn",
         ids,
-        (inputs, att_own, att_oth) + wos + (gains, cotangent) + w_ins + w_backs,
+        (inputs, att_own, att_oth) + wos + (gains, cotangent) + w_ins + w_backs + tuple(grads or ()),
         [mine, whole(att_own.shape), whole(att_oth.shape)]
         + [whole(w.shape) for w in wos]
         + [whole(gains.shape), mine]
-        + [whole(w.shape) for w in w_ins + w_backs],
+        + [in_spec(first_half), in_spec(second_half), back_spec(first_half), back_spec(second_half)]
+        + (grad_specs if grads else []),
         outs,
-        [whole(o.shape) for o in outs[:4]] + [pl.BlockSpec((seq, units), lambda i: (0, i))] * 2,
-        grid=(2,),
-        scratch=[pltpu.VMEM((seq, width), F32), pltpu.VMEM((seq, width), F32)],
-    )
-
-
-def grad_back_kernel(docs, *refs):
-    hid_refs, cot_ref, out_refs = refs[:docs], refs[docs], refs[docs + 1 :]
-    hid = jnp.concatenate([r[...] for r in hid_refs], axis=0)
-    units = out_refs[0].shape[0]
-    for i in range(2):
-        out_refs[i][...] = dot_tn(hid[:, i * units : (i + 1) * units], cot_ref[...]).astype(BF16)
-
-
-def grad_back(ids, hids, cotangent, docs):
-    seq, both = hids[0].shape
-    width = cotangent.shape[1]
-    outs = [shape_of((both // 2, width), BF16)] * 2
-    return call(
-        functools.partial(grad_back_kernel, docs),
-        "grad_back",
-        ids,
-        tuple(hids) + (cotangent,),
-        [whole(h.shape) for h in hids] + [pl.BlockSpec((docs * seq, width), lambda i: (lax.axis_index("core"), 0))],
-        outs,
-        [whole(o.shape) for o in outs],
-    )
-
-
-def grad_in_kernel(docs, *refs):
-    normed_refs, gpre_refs, out_refs = refs[:docs], refs[docs : 2 * docs], refs[2 * docs :]
-    normed = jnp.concatenate([r[...] for r in normed_refs], axis=0)
-    gpre = jnp.concatenate([r[...] for r in gpre_refs], axis=0)
-    units = out_refs[0].shape[1]
-    for i in range(2):
-        out_refs[i][...] = dot_tn(normed, gpre[:, i * units : (i + 1) * units]).astype(BF16)
-
-
-def grad_in(ids, normeds, gpres, docs):
-    width = normeds[0].shape[1]
-    units = gpres[0].shape[1] // 2
-    outs = [shape_of((width, units), BF16)] * 2
-    args = tuple(normeds) + tuple(gpres)
-    return call(
-        functools.partial(grad_in_kernel, docs),
-        "grad_in",
-        ids,
-        args,
-        [whole(a.shape) for a in args],
-        outs,
-        [whole(o.shape) for o in outs],
+        [whole(o.shape) for o in outs[:3]] + grad_specs,
+        grid=(2 * tiles,),
+        scratch=[
+            pltpu.VMEM((seq, width), BF16),
+            pltpu.VMEM((width, seq), BF16),
+            pltpu.VMEM((seq, width), F32),
+            pltpu.VMEM((seq, width), F32),
+        ],
     )
 
 
@@ -602,6 +607,26 @@
         dst[...] = src[...].astype(F32)
 
 
+def widen_attn(ids, total):
+    steps = 4
+    width = total.shape[1]
+    part = total.shape[0] // (4 * steps)
+    specs = [
+        pl.BlockSpec((3 * part, width), lambda i: (i, 0)),
+        pl.BlockSpec((part, width), lambda i: (3 * steps + i, 0)),
+    ]
+    return call(
+        widen_kernel,
+        "widen_attn",
+        ids,
+        (total, total),
+        specs,
+        [shape_of((12 * part, width), F32), shape_of((4 * part, width), F32)],
+        [pl.BlockSpec((n * part, width), lambda i: (i, 0)) for n in (3, 1)],
+        grid=(steps,),
+    )
+
+
 def widen(ids, *arrays):
     steps = 4
     specs = [pl.BlockSpec((v.shape[0] // steps, v.shape[1]), lambda i: (i, 0)) for v in arrays]
@@ -688,30 +713,27 @@
         att.append(c)
         att_x.append(from_x(c))
 
-    middle, normed2, gown, hown, hid, gpre, goth, hoth = [], [], [], [], [], [], [], []
+    middle, gown, hown, goth, grads = [], [], [], [], None
     for doc in every:
-        res, ids = ffn(
+        (m, g, h, *grads), ids = ffn(
             ids, inputs, att[doc], att_x[doc], (w_out, wo_c, wo_x, wo_xc), gains, cotangent,
-            (w_in, in_c), (w_back, back_c), doc, docs,
+            (w_in, in_c), (w_back, back_c), grads, doc, docs,
         )
-        for group, r in zip((middle, normed2, gown, hown, hid, gpre), res):
-            group.append(r)
+        middle.append(m)
+        hown.append(h)
         if doc + 1 < docs:
             ids = need(ids, att_x[doc + 1])
-        (send,), ids = gate(ids, res[2])
-        goth.append(from_x(send))
+        (g,), ids = gate(ids, g)
+        gown.append(g)
+        goth.append(from_x(g))
     always = lengths[0] > 0
 
     def ffn_grads(ids):
-        (gback, gback_c), ids = grad_back(ids, hid, cotangent, docs)
-        gback_c = from_core(gback_c)
-        (gin, gin_c), ids = grad_in(ids, normed2, gpre, docs)
-        (gback, gin), ids = sum_core(ids, gback, gback_c, gin, from_core(gin_c))
-        return ids, gback, gin
-
-    ids, gback, gin = region(always, ffn_grads, ids)
-    ids = need(ids, *goth)
-    (gback, gin), ids = gate(ids, gback, gin)
+        gback, gback_c, gin, gin_c = grads
+        return sum_core(ids, gback, from_core(gback_c), gin, from_core(gin_c))[::-1]
+
+    ids = need(ids, goth[0])
+    ids, (gback, gin) = region(always, ffn_grads, ids)
     gback, gin = lax.psum((gback, gin), "dp")
 
     def back_of(doc, ids):
@@ -721,9 +743,12 @@
         )
         return ids, res
 
+    ids, first = back_of(0, ids)
+    ids = need(ids, *goth[1:])
+
     def attention_back(ids):
-        ids, first = back_of(0, ids)
-        noth = [from_x(first[4])]
+        (nown_0,), ids = gate(ids, first[4])
+        noth = [from_x(nown_0)]
 
         def others(ids):
             results = [first]
@@ -737,48 +762,48 @@
         ids, results, gattn = region(always, others, ids)
         gmid, low, ggain_two, gp, nown, diag = zip(first, *results)
         ids = need(ids, noth[0])
+        nown = [nown_0] + list(nown[1:])
         for doc in range(1, docs):
-            (send,), ids = gate(ids, nown[doc])
-            noth.append(from_x(send))
+            (nown[doc],), ids = gate(ids, nown[doc])
+            noth.append(from_x(nown[doc]))
         (gattn,), ids = gate(ids, gattn)
         gattn = scatter(gattn)
-        hoth = []
+        hsent, hoth = [], []
         for doc in every:
             (send,), ids = gate(ids, hown[doc])
+            hsent.append(send)
             hoth.append(from_x(send))
         (gsrc, gsrc_send, ggain_one), ids = grad_input(ids, inputs, gains, gmid, nown, noth, docs)
         gsrc_got = from_core(gsrc_send)
 
-        diag_bucket = jnp.concatenate([buckets[:, 0], buckets[:1, -1], buckets[:-1, -1]])
-        one_hot = (diag_bucket[:, None] == jnp.arange(table_rows)[None, :]).astype(F32)
-        diag = sum(diag).reshape(2 * heads, 2 * seq)
-        table = lax.dot_general(
-            diag, one_hot, (((1,), (0,)), ((), ())), precision=lax.Precision.HIGHEST, preferred_element_type=F32
-        )
-        ggain_two = sum(ggain_two)
-        small = jnp.concatenate([ggain_one.reshape(-1), ggain_two.reshape(-1), table[:heads].reshape(-1)])
-        small_send = jnp.concatenate([ggain_one.reshape(-1), ggain_two.reshape(-1), table[heads:].reshape(-1)])
-        small = small + from_core(small_send)
-        for s in range(dp.bit_length() - 1):
-            small = small + lax.ppermute(small, "dp", [(i, i ^ (1 << s)) for i in range(dp)])
-        grad_gain_attn, grad_gain_ffn = small[:width], small[width : 2 * width]
-        grad_table = small[2 * width :].reshape(heads, table_rows).T
+        (gsrc,), ids = place(ids, gsrc, gsrc_got)
+        ids = need(ids, *hoth)
         (gattn,), ids = sum_parts(ids, gattn, dp)
-        gattn = spread(gattn)
-        (gsrc,), ids = place(ids, gsrc, gsrc_got)
-        (mixed, mixed_send), ids = mix(ids, middle, hown, hoth, docs)
-        ids = need(ids, grad_gain_attn, grad_gain_ffn, grad_table)
-        (mixed,), ids = place(ids, mixed, from_core(mixed_send))
-        part = 3 * width // 4
-        gattn = gattn.astype(F32)
-        grad_w_qkv = gattn[:part].reshape(3, width // 4, width).transpose(0, 2, 1)
-        grad_w_out = gattn[part:]
-        return ids, mixed, gsrc, grad_gain_attn, grad_w_qkv, grad_w_out, grad_gain_ffn, grad_table
-
-    ids, mixed, gsrc, grad_gain_attn, grad_w_qkv, grad_w_out, grad_gain_ffn, grad_table = region(
-        always, attention_back, ids
-    )
+        return ids, gattn, gsrc, ggain_one, ggain_two, diag, hsent, hoth
+
+    ids, gattn, gsrc, ggain_one, ggain_two, diag, hsent, hoth = region(always, attention_back, ids)
+    gattn = spread(gattn)
+    diag_bucket = jnp.concatenate([buckets[:, 0], buckets[:1, -1], buckets[:-1, -1]])
+    one_hot = (diag_bucket[:, None] == jnp.arange(table_rows)[None, :]).astype(F32)
+    diag = sum(diag).reshape(2 * heads, 2 * seq)
+    table = lax.dot_general(
+        diag, one_hot, (((1,), (0,)), ((), ())), precision=lax.Precision.HIGHEST, preferred_element_type=F32
+    )
+    ggain_two = sum(ggain_two)
+    small = jnp.concatenate([ggain_one.reshape(-1), ggain_two.reshape(-1), table[:heads].reshape(-1)])
+    small_send = jnp.concatenate([ggain_one.reshape(-1), ggain_two.reshape(-1), table[heads:].reshape(-1)])
+    small = small + from_core(small_send)
+    for s in range(dp.bit_length() - 1):
+        small = small + lax.ppermute(small, "dp", [(i, i ^ (1 << s)) for i in range(dp)])
+    grad_gain_attn, grad_gain_ffn = small[:width], small[width : 2 * width]
+    grad_table = small[2 * width :].reshape(heads, table_rows).T
+    (mixed, mixed_send), ids = mix(ids, middle, hsent, hoth, docs)
+    ids = need(ids, grad_gain_attn, grad_gain_ffn, grad_table)
+    mixed_got = from_core(mixed_send)
     (grad_w_back, grad_w_in), ids = widen(ids, gback, gin)
+    (mixed,), ids = place(ids, mixed, mixed_got)
+    (grad_w_qkv, grad_w_out), ids = widen_attn(ids, gattn)
+    grad_w_qkv = grad_w_qkv.reshape(3, width // 4, width).transpose(0, 2, 1)
     return (
         mixed,
         gsrc,

time: 274 us -> 260 us (0.949)
  Pallas kernels: 125 us -> 107 us
    all_to_all x1, waiting for transfers between devices: 43.9 us -> 6.68 us  [scatter(): return lax.all_to_all(v, ('core', 'dp'), 0, 0, tiled=True)]
    ppermute x9, waiting for transfers between devices: 16.5 us -> 52.9 us  [from_x(): return lax.ppermute(v, 'x', [(0, 1), (1, 0)])]
    pallas_call x28 -> x29, Pallas kernels: 125 us -> 107 us  [call(): pl.pallas_call(body, grid=grid, in_specs=[anywhere] + list(in_specs), out...]
    ppermute x3, waiting for transfers between devices: 7.65 us -> 11.6 us  [per_device(): lax.ppermute(small, 'dp', [(i, i ^ 1 << s) for i in range(dp)])]
    unnamed x22 -> x47, local copies, waits for them, and re-layouts: 5.93 us -> 7.83 us
    cond x30 -> x28, local copies, waits for them, and re-layouts: 7.57 us -> 6.53 us
  transfers between devices with their start and end apart: 25 -> 25, of which waited for: 10 -> 13; matrix products, arithmetic and copies ran while one was open for 5% -> 3% of each run, Pallas kernels for 44% -> 41%
where the time goes in v3:
time: 260 us; the launch traced here: 259 us
  Pallas kernels  107 us (41%)
  waiting for transfers between devices  77.7 us (30%)
  starting transfers between devices  41 us (16%)
  local copies, waits for them, and re-layouts  15.7 us (6%)
  between operations  14.4 us (6%)
    pallas_call x29, Pallas kernels, call(): pl.pallas_call(body, grid=grid, in_specs=[anywhere] + list(in_specs), out...  107 us
    ppermute x9, waiting for transfers between devices, from_x(): return lax.ppermute(v, 'x', [(0, 1), (1, 0)])  52.9 us
    all_to_all x1, starting transfers between devices, spread(): return lax.all_to_all(v, 'dp', 0, 0, tiled=True)  13.5 us
    ppermute x3, waiting for transfers between devices, per_device(): lax.ppermute(small, 'dp', [(i, i ^ 1 << s) for i in range(dp)])  11.6 us
    ppermute x9, starting transfers between devices, from_x(): return lax.ppermute(v, 'x', [(0, 1), (1, 0)])  11.2 us
    ppermute x3, starting transfers between devices, per_device(): lax.ppermute(small, 'dp', [(i, i ^ 1 << s) for i in range(dp)])  8.01 us
    unnamed x47, local copies, waits for them, and re-layouts  7.83 us
    all_to_all x1, waiting for transfers between devices, scatter(): return lax.all_to_all(v, ('core', 'dp'), 0, 0, tiled=True)  6.68 us
  transfers between devices with their start and end apart: 25, of which 13 were waited for; matrix products, arithmetic and copies ran while one was open for 3% of the time, Pallas kernels for 41%

profile of v3, /device:TPU:0, one launch (start us, length us, event | category | flops | bytes accessed | tf_op | source)
XLA Modules:
  0.0 258.9 jit_solution(17862317107481635217)
XLA Ops:
  7.3 1.5 fusion.1.refs_3_
  8.8 0.5 collective-permute-start.7
  9.4 0.4 collective-permute-start.13
  9.8 2.6 collective-permute-start.8
  12.6 9.3 %attn_fwd.2 = (f32[8,128]{1,0:T(8,128)S(1)}, bf16[1152,768]{1,0:T(8,128)(2,1)}, f32[6,1024]{1,0:T(8,128)S(1)}, bf16[512,768]{1,0:T(8,128)(2,1)}, bf16[512,1152]{...) custom-call(f32[8,128]{1,0:T(8,128)S(1)} %broadcast_29_token_ref.2.t, ...), custom_call_target="tpu_custom_call", output_to_operand_aliasing={{0}: (0, {})} | custom-call | tf_op jit(solution)/shard_map/attn_fwd/pallas_call | solution.py:52
  22.0 2.1 collective-permute-start.9
  24.1 9.5 %attn_fwd.3 = (f32[8,128]{1,0:T(8,128)S(1)}, bf16[512,768]{1,0:T(8,128)(2,1)}, bf16[512,1152]{1,0:T(8,128)(2,1)}, bf16[6,512,512]{2,1,0:T(8,128)(2,1)}, bf16[512,384]{1,0:T(8,128)(2,1)S(1)}) custom-call(f32[8,128]{1,0:T(8,128)S(1)} %get-tuple-element.251.token_ref, s32[4]{0:T(128)S(1)} %copy-done.16, ...), custom_call_target="tpu_custom_call", output_to_operand_aliasing={{0}: (0, {})} | custom-call | tf_op jit(solution)/shard_map/attn_fwd/pallas_call | solution.py:52
  33.6 1.6 collective-permute-start.14
  35.2 1.6 collective-permute-done.11.refs_6_
  36.8 13.4 %ffn.2 = (f32[8,128]{1,0:T(8,128)S(1)}, f32[512,768]{1,0:T(8,128)S(1)}, bf16[512,768]{1,0:T(8,128)(2,1)}, bf16[512,768]{1,0:T(8,128)(2,1)}, bf16[768,768]{1,0:T(...) custom-call(f32[8,128]{1,0:T(8,128)S(1)} %get-tuple-element.254.toke, ...), custom_call_target="tpu_custom_call", output_to_operand_aliasing={{0}: (0, {})} | custom-call | tf_op jit(solution)/shard_map/ffn/pallas_call | solution.py:52
  50.2 0.6 collective-permute-start.15
  50.8 15.0 %ffn.3 = (f32[8,128]{1,0:T(8,128)S(1)}, f32[512,768]{1,0:T(8,128)}, bf16[512,768]{1,0:T(8,128)(2,1)}, bf16[512,768]{1,0:T(8,128)(2,1)}, bf16[768,768]{1,0:T(8,12...) custom-call(f32[8,128]{1,0:T(8,128)S(1)} %get-tuple-element.260.toke, ...), custom_call_target="tpu_custom_call", output_to_operand_aliasing={{0}: (0, {})} | custom-call | tf_op jit(solution)/shard_map/ffn/pallas_call | solution.py:52
  65.8 1.5 collective-permute-start.16
  67.3 3.6 %collective-permute-done.15.refs_0_.refs_2_ = bf16[512,768]{1,0:T(8,128)(2,1)S(1)} collective-permute-done((bf16[512,768]{1,0:T(8,128)(2,1)}, bf16[512,768]{1,0:T(8,128)(2,1)S(1)}, u32[]{:S(2)}, u32[]{:S(2)}) %collective-permute-start.15) | collective-permute-done | bytes 786464 | tf_op jit(solution)/shard_map/ppermute | solution.py:682
  70.9 8.7 %conditional.3 = ((f32[8,128]{1,0:T(8,128)S(1)}, bf16[768,768]{1,0:T(8,128)(2,1)}, bf16[768,768]{1,0:T(8,128)(2,1)})) conditional(s32[]{:T(128)} %convert_element_type.13, () %tuple.34, (bf16[768,768]{1,0:T(8,128)(2,1)}, bf16[768,768]{1,0:T(8,128)(2,1)}, f32[8,128]{1,0:T(8,128)S(1)}, bf16[768,768]{1,0:T(8,128)(2,1)}, bf16[768,768]{1,0:T(8,128)(2,1)}) %tuple.35), branch_computations={%region_0.1_spmd, %region_1.2_spmd} | conditional | bytes 9437272 | solution.py:667
  70.9 0.5 collective-permute-start.1
  71.4 2.5 collective-permute-done.refs_1_
  74.0 1.7 collective-permute-done.1.refs_3_
  75.7 3.9 %sum_core.1 = (f32[8,128]{1,0:T(8,128)S(1)}, bf16[768,768]{1,0:T(8,128)(2,1)}, bf16[768,768]{1,0:T(8,128)(2,1)}) custom-call(f32[8,128]{1,0:T(8,128)S(1)} %get-tuple-element.95.token_ref, bf16[768,768]{1,0:T(8,128)(2,1)} %get-tuple-element.96.refs_0_, bf16[768,768]{1,0:T(8,128)(2,1)S(1)} %collective-permute-done.refs_1_, ...), custom_call_target="tpu_custom_call", output_to_operand_aliasing={{0}: (0, {})} | custom-call | tf_op jit(solution)/shard_map/cond/branch_1_fun/sum_core/pallas_call | solution.py:52
  79.6 1.9 copy-done.9
  81.5 1.3 copy-done.11
  82.8 11.8 %attn_bwd.3 = (f32[8,128]{1,0:T(8,128)S(1)}, f32[512,768]{1,0:T(8,128)}, bf16[512,768]{1,0:T(8,128)(2,1)}, f32[1,768]{1,0:T(1,128)S(1)}, bf16[512,1152]{1,0:T(8,...) custom-call(f32[8,128]{1,0:T(8,128)S(1)} %get-tuple-element.273.token_ref, ...), custom_call_target="tpu_custom_call", output_to_operand_aliasing={{0}: (0, {})} | custom-call | tf_op jit(solution)/shard_map/attn_bwd/pallas_call | solution.py:52
  94.6 103.4 %conditional.4 = (f32[8,128]{1,0:T(8,128)S(1)}, bf16[768,768]{1,0:T(8,128)(2,1)}, f32[2048,768]{1,0:T(8,128)}, f32[1,768]{1,0:T(1,128)S(1)}, f32[1,768]{1,0:T(1,...) conditional(s32[]{:T(128)} %convert_element_type.13, () %tuple.33, ...), branch_computations={%region_2.3_spmd, %region_3.6_spmd} | conditional | flops 1 | bytes 74828672 | solution.py:667
  94.6 0.4 collective-permute-start.2
  95.0 16.5 %conditional = (f32[8,128]{1,0:T(8,128)S(1)}, f32[512,768]{1,0:T(8,128)}, f32[1,768]{1,0:T(1,128)}, bf16[512,768]{1,0:T(8,128)(2,1)S(1)}, f32[3,2,1024]{2,1,0:T(2,128)}, /*index=5*/bf16[1536,768]{1,0:T(8,128)(2,1)S(1)}) conditional(s32[]{:T(128)} %convert_element_type.1, () %tuple.24, (f32[8,128]{1,0:T(8,128)S(1)}, f32[512,768]{1,0:T(8,128)}, ...), branch_computations={%region_4.4_spmd, %region_5.5_spmd} | conditional | bytes 17301720 | solution.py:667
  95.0 12.7 %attn_bwd.2 = (f32[8,128]{1,0:T(8,128)S(1)}, f32[512,768]{1,0:T(8,128)}, bf16[512,768]{1,0:T(8,128)(2,1)S(1)}, f32[1,768]{1,0:T(1,128)}, bf16[512,1152]{1,0:T(8,...) custom-call(f32[8,128]{1,0:T(8,128)S(1)} %get-tuple-element.100.token_ref, ...), custom_call_target="tpu_custom_call", output_to_operand_aliasing={{0}: (0, {})} | custom-call | tf_op jit(solution)/shard_map/cond/branch_1_fun/cond/branch_1_fun/attn_bwd/pallas_call | solution.py:52
  107.8 3.7 %grad_attn.1 = (f32[8,128]{1,0:T(8,128)S(1)}, bf16[1536,768]{1,0:T(8,128)(2,1)S(1)}) custom-call(f32[8,128]{1,0:T(8,128)S(1)} %get-tuple-element.111.token_ref, bf16[512,768]{1,0:T(8,128)(2,1)S(1)} %copy-done.29, bf16[512,768]{1,0:T(8,128)(2,1)S(1)} %copy-done.30, bf16[512,1152]{1,0:T(8,128)(2,1)S(1)} %copy-done.28, ...), custom_call_target="tpu_custom_call", output_to_operand_aliasing={{0}: (0, {})} | custom-call | tf_op jit(solution)/shard_map/cond/branch_1_fun/cond/branch_1_fun/grad_attn/pallas_call | solution.py:52
  111.5 3.0 %collective-permute-done.2.refs_0_.refs_6_ = bf16[512,768]{1,0:T(8,128)(2,1)S(1)} collective-permute-done((bf16[512,768]{1,0:T(8,128)(2,1)}, bf16[512,768]{1,0:T(8,128)(2,1)S(1)}, u32[]{:S(2)}, u32[]{:S(2)}) %collective-permute-start.2) | collective-permute-done | bytes 786464 | tf_op jit(solution)/shard_map/cond/branch_1_fun/ppermute | solution.py:682
  114.5 0.9 copy-done.6
  115.4 1.4 copy-done.19
  116.8 5.9 %all-to-all-start = ((bf16[16,96,768]{2,1,0:T(8,128)(2,1)}), bf16[16,96,768]{2,1,0:T(8,128)(2,1)S(1)}, u32[]{:S(2)}, u32[]{:S(2)}) async-start(bf16[16,96,768]{2,1,0:T(8,128)(2,1)} %bitcast.22), calls=%async_computation | async-start | bytes 4718592 | tf_op jit(solution)/shard_map/cond/branch_1_fun/all_to_all | solution.py:685
  122.7 0.5 collective-permute-start.3
  123.2 19.6 %collective-permute-done.3.refs_7_ = bf16[512,768]{1,0:T(8,128)(2,1)S(1)} collective-permute-done((bf16[512,768]{1,0:T(8,128)(2,1)}, bf16[512,768]{1,0:T(8,128)(2,1)S(1)}, u32[]{:S(2)}, u32[]{:S(2)}) %collective-permute-start.3) | collective-permute-done | bytes 786464 | tf_op jit(solution)/shard_map/cond/branch_1_fun/ppermute | solution.py:682
  142.8 7.1 %grad_input.1 = (f32[8,128]{1,0:T(8,128)S(1)}, f32[2048,768]{1,0:T(8,128)}, f32[1024,768]{1,0:T(8,128)}, f32[1,768]{1,0:T(1,128)S(1)}) custom-call(f32[8,128]{1,0:T(8,128)S(1)} %get-tuple-element.155.token_ref, bf16[2048,768]{1,0:T(8,128)(2,1)} %get-tuple-element.156.refs_0_, ...), custom_call_target="tpu_custom_call", output_to_operand_aliasing={{0}: (0, {})} | custom-call | tf_op jit(solution)/shard_map/cond/branch_1_fun/grad_input/pallas_call | solution.py:52
  150.0 0.4 collective-permute-start.6
  150.4 1.6 collective-permute-start.5
  152.0 2.1 copy.134
  154.2 2.1 copy.133
  156.2 4.2 %place.2 = (f32[8,128]{1,0:T(8,128)S(1)}, f32[2048,768]{1,0:T(8,128)}) custom-call(f32[8,128]{1,0:T(8,128)S(1)} %get-tuple-element.160.token_ref, f32[2048,768]{1,0:T(8,128)} %get-tuple-element.161.refs_0_, f32[1024,768]{1,0:T(8,128)} %collective-permute-done.4.refs_1_), custom_call_target="tpu_custom_call", output_to_operand_aliasing={{0}: (0, {}), {1}: (1, {})} | custom-call | tf_op jit(solution)/shard_map/cond/branch_1_fun/place/pallas_call | solution.py:52
  160.5 10.2 %collective-permute-done.6.refs_1_ = bf16[512,768]{1,0:T(8,128)(2,1)} collective-permute-done((bf16[512,768]{1,0:T(8,128)(2,1)}, bf16[512,768]{1,0:T(8,128)(2,1)}, u32[]{:S(2)}, u32[]{:S(2)}) %collective-permute-start.6) | collective-permute-done | bytes 786464 | tf_op jit(solution)/shard_map/cond/branch_1_fun/ppermute | solution.py:682
  170.6 16.5 %collective-permute-done.5.refs_0_ = bf16[512,768]{1,0:T(8,128)(2,1)} collective-permute-done((bf16[512,768]{1,0:T(8,128)(2,1)}, bf16[512,768]{1,0:T(8,128)(2,1)}, u32[]{:S(2)}, u32[]{:S(2)}) %collective-permute-start.5) | collective-permute-done | bytes 786464 | tf_op jit(solution)/shard_map/cond/branch_1_fun/ppermute | solution.py:682
  187.1 6.7 %all-to-all-done = bf16[16,96,768]{2,1,0:T(8,128)(2,1)S(1)} async-done(((bf16[16,96,768]{2,1,0:T(8,128)(2,1)}), bf16[16,96,768]{2,1,0:T(8,128)(2,1)S(1)}, u32[]{:S(2)}, u32[]{:S(2)}) %all-to-all-start) | async-done | bytes 2359328 | tf_op jit(solution)/shard_map/cond/branch_1_fun/all_to_all | solution.py:685
  193.8 4.2 %sum_parts.1 = (f32[8,128]{1,0:T(8,128)S(1)}, bf16[768,768]{1,0:T(8,128)(2,1)}) custom-call(f32[8,128]{1,0:T(8,128)S(1)} %need.7.token_ref, bf16[1536,768]{1,0:T(8,128)(2,1)S(1)} %bitcast.18), custom_call_target="tpu_custom_call", output_to_operand_aliasing={{0}: (0, {})} | custom-call | tf_op jit(solution)/shard_map/cond/branch_1_fun/sum_parts/pallas_call | solution.py:52
  198.0 13.5 %all-to-all-start.1 = ((bf16[8,96,768]{2,1,0:T(8,128)(2,1)}), bf16[8,96,768]{2,1,0:T(8,128)(2,1)S(1)}, u32[]{:S(2)}, u32[]{:S(2)}) async-start(bf16[8,96,768]{2,1,0:T(8,128)(2,1)} %bitcast.8), calls=%async_computation.1 | async-start | bytes 2359296 | tf_op jit(solution)/shard_map/all_to_all | solution.py:688
  211.5 1.4 copy-done.2
  212.9 4.4 %mix.1 = (f32[8,128]{1,0:T(8,128)S(1)}, bf16[2048,768]{1,0:T(8,128)(2,1)}, bf16[1024,768]{1,0:T(8,128)(2,1)}) custom-call(f32[8,128]{1,0:T(8,128)S(1)} %get-tuple-element.292.token_ref, f32[512,768]{1,0:T(8,128)S(1)} %copy-done.2, f32[512,768]{1,0:T(8,128)} %get-tuple-element.280.refs_1_, ...), custom_call_target="tpu_custom_call", output_to_operand_aliasing={{0}: (0, {})} | custom-call | tf_op jit(solution)/shard_map/mix/pallas_call | solution.py:52
  217.4 0.6 slice.39
  218.0 0.2 slice_reduce_fusion
  218.4 0.7 pad_add_fusion
  219.1 0.4 fusion.2
  219.6 0.6 collective-permute-start.17
  220.3 0.7 collective-permute-done.17
  221.1 2.0 collective-permute-start.18
  223.1 1.6 collective-permute-done.18
  224.7 2.0 collective-permute-start.19
  226.7 5.0 %collective-permute-done.19 = f32[1632]{0:T(1024)S(1)} collective-permute-done((f32[1632]{0:T(1024)S(1)}, f32[1632]{0:T(1024)S(1)}, u32[]{:S(2)}, u32[]{:S(2)}) %collective-permute-start.19) | collective-permute-done | bytes 6560 | tf_op jit(solution)/shard_map/ppermute | solution.py:797
  231.7 4.0 %collective-permute-start.20 = (f32[1632]{0:T(1024)S(1)}, f32[1632]{0:T(1024)S(1)}, u32[]{:S(2)}, u32[]{:S(2)}) collective-permute-start(f32[1632]{0:T(1024)S(1)} %add.28), channel_id=1, source_target_pairs={{0,4},{1,5},{2,6},{3,7},{4,0},{5,1},{6,2},{7,3},{8,12},{9,13},{10,... | collective-permute-start | bytes 19592 | tf_op jit(solution)/shard_map/ppermute | solution.py:797
  235.7 5.0 %collective-permute-done.20 = f32[1632]{0:T(1024)S(1)} collective-permute-done((f32[1632]{0:T(1024)S(1)}, f32[1632]{0:T(1024)S(1)}, u32[]{:S(2)}, u32[]{:S(2)}) %collective-permute-start.20) | collective-permute-done | bytes 6560 | tf_op jit(solution)/shard_map/ppermute | solution.py:797
  240.8 0.7 copy.62
  241.5 1.3 copy-done.12
  242.8 1.3 copy-done.13
  244.1 2.5 widen.1
  246.6 3.6 %place.3 = (f32[8,128]{1,0:T(8,128)S(1)}, bf16[2048,768]{1,0:T(8,128)(2,1)}) custom-call(f32[8,128]{1,0:T(8,128)S(1)} %get-tuple-element.305.token_ref, bf16[2048,768]{1,0:T(8,128)(2,1)} %get-tuple-element.306.refs_0_, bf16[1024,768]{1,0:T(8,128)(2,1)} %collective-permute-done.21.refs_1_), custom_call_target="tpu_custom_call", output_to_operand_aliasing={{0}: (0, {}), {1}: (1, {})} | custom-call | tf_op jit(solution)/shard_map/place/pallas_call | solution.py:52
  250.2 1.9 widen_attn.1
  (120 shorter events, 1.2 us)
Async XLA Ops:
  7.2 2.1 copy-start.3
  7.2 5.3 %copy-start.34 = (bf16[768]{0:T(1024)(128)(2,1)S(1)}, bf16[768]{0:T(1024)(128)(2,1)}, u32[]{:S(2)}) copy-start(bf16[768]{0:T(1024)(128)(2,1)} %param.21) | copy-start | bytes 4612
  7.2 5.3 %copy-start.35 = (bf16[768]{0:T(1024)(128)(2,1)S(1)}, bf16[768]{0:T(1024)(128)(2,1)}, u32[]{:S(2)}) copy-start(bf16[768]{0:T(1024)(128)(2,1)} %param.18) | copy-start | bytes 4612
  7.2 234.3 %all-reduce.4.cloned.1.call-start = ((), (), s32[]{:S(2)}) async-start(), calls=%async_computation.2 | async-start | bytes 4718592 | tf_op jit(solution)/shard_map/psum | solution.py:737
  7.3 5.3 %copy-start = (s32[512,512]{1,0:T(8,128)S(1)}, s32[512,512]{1,0:T(8,128)}, u32[]{:S(2)}) copy-start(s32[512,512]{1,0:T(8,128)} %refs_6_.1) | copy-start | bytes 3145732
  7.3 5.3 %copy-start.16 = (s32[4]{0:T(128)S(1)}, s32[4]{0:T(128)}, u32[]{:S(2)}) copy-start(s32[4]{0:T(128)} %refs_0_.5) | copy-start | bytes 52
  8.8 3.8 %collective-permute-start.7 = (bf16[784,768]{1,0:T(8,128)(2,1)S(1)}, bf16[784,768]{1,0:T(8,128)(2,1)S(1)}, u32[]{:S(2)}, u32[]{:S(2)}) collective-permute-start(bf16[784,768]{1,0:T(8,128)(2,1)S(1)} %fusion.1.refs_3_), channel_id=1, source_target_pairs={{0,8},{8,0},{1,9},{9,1},{2,10},{10,2},{3,11},{11,3},{4,12},{12,4},... | collective-permute-start | bytes 3612680 | tf_op jit(solution)/shard_map/ppermute | solution.py:679
  9.3 25.9 %collective-permute-start.12 = (bf16[768,768]{1,0:T(8,128)(2,1)S(1)}, bf16[768,768]{1,0:T(8,128)(2,1)S(1)}, u32[]{:S(2)}, u32[]{:S(2)}) collective-permute-start(bf16[768,768]{1,0:T(8,128)(2,1)S(1)} %copy-done.3), channel_id=1, source_target_pairs={{0,8},{8,0},{1,9},{9,1},{2,10},{10,2},{3,11},{11,3},{4,12},{12,4},... | collective-permute-start | bytes 3538952 | tf_op jit(solution)/shard_map/ppermute | solution.py:679
  9.4 25.9 %collective-permute-start.13 = (bf16[768,768]{1,0:T(8,128)(2,1)}, bf16[768,768]{1,0:T(8,128)(2,1)S(1)}, u32[]{:S(2)}, u32[]{:S(2)}) collective-permute-start(bf16[768,768]{1,0:T(8,128)(2,1)} %refs_11_.3), channel_id=1, source_target_pairs={{0,8},{8,0},{1,9},{9,1},{2,10},{10,2},{3,11},{11,3},{4,12},{12,4},... | collective-permute-start | bytes 3538952 | tf_op jit(solution)/shard_map/ppermute | solution.py:679
  9.8 14.3 %collective-permute-start.8 = (bf16[192,768]{1,0:T(8,128)(2,1)}, bf16[192,768]{1,0:T(8,128)(2,1)S(1)}, u32[]{:S(2)}, u32[]{:S(2)}) collective-permute-start(bf16[192,768]{1,0:T(8,128)(2,1)} %refs_5_.3), channel_id=1, source_target_pairs={{0,16},{16,0},{1,17},{17,1},{2,18},{18,2},{3,19},{19,3},{4,20},{20... | collective-permute-start | bytes 884744 | tf_op jit(solution)/shard_map/ppermute | solution.py:682
  12.4 22.8 %collective-permute-start.10 = (bf16[192,768]{1,0:T(8,128)(2,1)}, bf16[192,768]{1,0:T(8,128)(2,1)S(1)}, u32[]{:S(2)}, u32[]{:S(2)}) collective-permute-start(bf16[192,768]{1,0:T(8,128)(2,1)} %refs_5_.3), channel_id=1, source_target_pairs={{0,8},{8,0},{1,9},{9,1},{2,10},{10,2},{3,11},{11,3},{4,12},{12,4},... | collective-permute-start | bytes 884744 | tf_op jit(solution)/shard_map/ppermute | solution.py:679
  12.6 11.5 %copy-start.17 = (bf16[2048,768]{1,0:T(8,128)(2,1)S(1)}, bf16[2048,768]{1,0:T(8,128)(2,1)}, u32[]{:S(2)}) copy-start(bf16[2048,768]{1,0:T(8,128)(2,1)} %refs_0_.7) | copy-start | bytes 9437188
  12.6 24.2 %copy-start.18 = (bf16[2048,768]{1,0:T(8,128)(2,1)S(1)}, bf16[2048,768]{1,0:T(8,128)(2,1)}, u32[]{:S(2)}) copy-start(bf16[2048,768]{1,0:T(8,128)(2,1)} %refs_4_.1) | copy-start | bytes 9437188
  22.0 11.7 %copy-start.8 = (bf16[6,512,512]{2,1,0:T(8,128)(2,1)}, bf16[6,512,512]{2,1,0:T(8,128)(2,1)S(1)}, u32[]{:S(2)}) copy-start(bf16[6,512,512]{2,1,0:T(8,128)(2,1)S(1)} %get-tuple-element.276.refs_9_) | copy-start | bytes 9437188
  22.0 11.7 %copy-start.10 = (bf16[512,1152]{1,0:T(8,128)(2,1)}, bf16[512,1152]{1,0:T(8,128)(2,1)S(1)}, u32[]{:S(2)}) copy-start(bf16[512,1152]{1,0:T(8,128)(2,1)S(1)} %get-tuple-element.275.refs_8_) | copy-start | bytes 3538948
  22.0 14.9 %copy-start.24 = (bf16[512,384]{1,0:T(8,128)(2,1)}, bf16[512,384]{1,0:T(8,128)(2,1)S(1)}, u32[]{:S(2)}) copy-start(bf16[512,384]{1,0:T(8,128)(2,1)S(1)} %get-tuple-element.255.refs_1_) | copy-start | bytes 1179652
  22.0 14.8 %collective-permute-start.9 = (bf16[512,384]{1,0:T(8,128)(2,1)S(1)}, bf16[512,384]{1,0:T(8,128)(2,1)S(1)}, u32[]{:S(2)}, u32[]{:S(2)}) collective-permute-start(bf16[512,384]{1,0:T(8,128)(2,1)S(1)} %get-tuple-element.255.refs_1_), channel_id=1, source_target_pairs={{0,16},{16,0},{1,17},{17,1},{2,18},{18,2},{3,19},{19,3},{4,20},{20... | collective-permute-start | bytes 1179656 | tf_op jit(solution)/shard_map/ppermute | solution.py:682
  24.1 12.7 %copy-start.4 = (bf16[768,768]{1,0:T(8,128)(2,1)S(1)}, bf16[768,768]{1,0:T(8,128)(2,1)}, u32[]{:S(2)}) copy-start(bf16[768,768]{1,0:T(8,128)(2,1)} %refs_9_.3) | copy-start | bytes 3538948
  24.1 12.7 %copy-start.5 = (bf16[768,768]{1,0:T(8,128)(2,1)S(1)}, bf16[768,768]{1,0:T(8,128)(2,1)}, u32[]{:S(2)}) copy-start(bf16[768,768]{1,0:T(8,128)(2,1)} %refs_11_.3) | copy-start | bytes 3538948
  24.1 12.7 %copy-start.20 = (bf16[192,768]{1,0:T(8,128)(2,1)S(1)}, bf16[192,768]{1,0:T(8,128)(2,1)}, u32[]{:S(2)}) copy-start(bf16[192,768]{1,0:T(8,128)(2,1)} %refs_5_.3) | copy-start | bytes 884740
  33.6 17.2 %copy-start.26 = (bf16[512,384]{1,0:T(8,128)(2,1)}, bf16[512,384]{1,0:T(8,128)(2,1)S(1)}, u32[]{:S(2)}) copy-start(bf16[512,384]{1,0:T(8,128)(2,1)S(1)} %get-tuple-element.258.refs_1_) | copy-start | bytes 1179652
  33.6 16.6 %collective-permute-start.14 = (bf16[512,384]{1,0:T(8,128)(2,1)S(1)}, bf16[512,384]{1,0:T(8,128)(2,1)S(1)}, u32[]{:S(2)}, u32[]{:S(2)}) collective-permute-start(bf16[512,384]{1,0:T(8,128)(2,1)S(1)} %get-tuple-element.258.refs_1_), channel_id=1, source_target_pairs={{0,16},{16,0},{1,17},{17,1},{2,18},{18,2},{3,19},{19,3},{4,20},{20... | collective-permute-start | bytes 1179656 | tf_op jit(solution)/shard_map/ppermute | solution.py:682
  35.2 15.6 %copy-start.23 = (bf16[192,768]{1,0:T(8,128)(2,1)}, bf16[192,768]{1,0:T(8,128)(2,1)S(1)}, u32[]{:S(2)}) copy-start(bf16[192,768]{1,0:T(8,128)(2,1)S(1)} %collective-permute-done.10.refs_4_.refs_6_) | copy-start | bytes 884740
  35.2 1.6 collective-permute-start.11
  50.2 29.4 %copy-start.1 = (f32[512,768]{1,0:T(8,128)}, f32[512,768]{1,0:T(8,128)S(1)}, u32[]{:S(2)}) copy-start(f32[512,768]{1,0:T(8,128)S(1)} %get-tuple-element.274.refs_0_) | copy-start | bytes 4718596
  50.2 20.7 %collective-permute-start.15 = (bf16[512,768]{1,0:T(8,128)(2,1)}, bf16[512,768]{1,0:T(8,128)(2,1)S(1)}, u32[]{:S(2)}, u32[]{:S(2)}) collective-permute-start(bf16[512,768]{1,0:T(8,128)(2,1)} %get-tuple-element.270.refs_1_), channel_id=1, source_target_pairs={{0,16},{16,0},{1,17},{17,1},{2,18},{18,2},{3,19},{19,3},{4,20},{20... | collective-permute-start | bytes 2359304 | tf_op jit(solution)/shard_map/ppermute | solution.py:682
  65.8 28.8 %collective-permute-start.16 = (bf16[512,768]{1,0:T(8,128)(2,1)}, bf16[512,768]{1,0:T(8,128)(2,1)}, u32[]{:S(2)}, u32[]{:S(2)}) collective-permute-start(bf16[512,768]{1,0:T(8,128)(2,1)} %get-tuple-element.278), channel_id=1, source_target_pairs={{0,16},{16,0},{1,17},{17,1},{2,18},{18,2},{3,19},{19,3},{4,20},{20... | collective-permute-start | bytes 2359304 | tf_op jit(solution)/shard_map/ppermute | solution.py:682
  70.9 3.1 %collective-permute-start = (bf16[768,768]{1,0:T(8,128)(2,1)}, bf16[768,768]{1,0:T(8,128)(2,1)S(1)}, u32[]{:S(2)}, u32[]{:S(2)}) collective-permute-start(bf16[768,768]{1,0:T(8,128)(2,1)} %get-tuple-element.97), channel_id=1, source_target_pairs={{0,8},{8,0},{1,9},{9,1},{2,10},{10,2},{3,11},{11,3},{4,12},{12,4},... | collective-permute-start | bytes 3538952 | tf_op jit(solution)/shard_map/cond/branch_1_fun/ppermute | solution.py:679
  70.9 4.7 %collective-permute-start.1 = (bf16[768,768]{1,0:T(8,128)(2,1)}, bf16[768,768]{1,0:T(8,128)(2,1)S(1)}, u32[]{:S(2)}, u32[]{:S(2)}) collective-permute-start(bf16[768,768]{1,0:T(8,128)(2,1)} %get-tuple-element.99), channel_id=1, source_target_pairs={{0,8},{8,0},{1,9},{9,1},{2,10},{10,2},{3,11},{11,3},{4,12},{12,4},... | collective-permute-start | bytes 3538952 | tf_op jit(solution)/shard_map/cond/branch_1_fun/ppermute | solution.py:679
  79.6 1.9 copy-start.9
  81.5 1.3 copy-start.11
  94.6 19.9 %collective-permute-start.2 = (bf16[512,768]{1,0:T(8,128)(2,1)}, bf16[512,768]{1,0:T(8,128)(2,1)S(1)}, u32[]{:S(2)}, u32[]{:S(2)}) collective-permute-start(bf16[512,768]{1,0:T(8,128)(2,1)} %get-tuple-element.147.refs_4_), channel_id=1, source_target_pairs={{0,16},{16,0},{1,17},{17,1},{2,18},{18,2},{3,19},{19,3},{4,20},{20... | collective-permute-start | bytes 2359304 | tf_op jit(solution)/shard_map/cond/branch_1_fun/ppermute | solution.py:682
  95.0 12.8 %copy-start.25 = (bf16[512,384]{1,0:T(8,128)(2,1)S(1)}, bf16[512,384]{1,0:T(8,128)(2,1)}, u32[]{:S(2)}) copy-start(bf16[512,384]{1,0:T(8,128)(2,1)} %get-tuple-element.118.refs_6_) | copy-start | bytes 1179652 | tf_op jit(solution)/shard_map/cond/branch_1_fun/cond
  95.0 12.8 %copy-start.27 = (bf16[512,384]{1,0:T(8,128)(2,1)S(1)}, bf16[512,384]{1,0:T(8,128)(2,1)}, u32[]{:S(2)}) copy-start(bf16[512,384]{1,0:T(8,128)(2,1)} %get-tuple-element.119.refs_7_) | copy-start | bytes 1179652 | tf_op jit(solution)/shard_map/cond/branch_1_fun/cond
  95.0 12.8 %copy-start.28 = (bf16[512,1152]{1,0:T(8,128)(2,1)S(1)}, bf16[512,1152]{1,0:T(8,128)(2,1)}, u32[]{:S(2)}) copy-start(bf16[512,1152]{1,0:T(8,128)(2,1)} %get-tuple-element.114.refs_2_) | copy-start | bytes 3538948 | tf_op jit(solution)/shard_map/cond/branch_1_fun/cond
  95.0 12.8 %copy-start.29 = (bf16[512,768]{1,0:T(8,128)(2,1)S(1)}, bf16[512,768]{1,0:T(8,128)(2,1)}, u32[]{:S(2)}) copy-start(bf16[512,768]{1,0:T(8,128)(2,1)} %get-tuple-element.112.refs_0_) | copy-start | bytes 2359300 | tf_op jit(solution)/shard_map/cond/branch_1_fun/cond
  95.0 12.8 %copy-start.30 = (bf16[512,768]{1,0:T(8,128)(2,1)S(1)}, bf16[512,768]{1,0:T(8,128)(2,1)}, u32[]{:S(2)}) copy-start(bf16[512,768]{1,0:T(8,128)(2,1)} %get-tuple-element.113.refs_1_) | copy-start | bytes 2359300 | tf_op jit(solution)/shard_map/cond/branch_1_fun/cond
  95.0 12.8 %copy-start.31 = (bf16[512,768]{1,0:T(8,128)(2,1)S(1)}, bf16[512,768]{1,0:T(8,128)(2,1)}, u32[]{:S(2)}) copy-start(bf16[512,768]{1,0:T(8,128)(2,1)} %get-tuple-element.116.refs_4_) | copy-start | bytes 2359300 | tf_op jit(solution)/shard_map/cond/branch_1_fun/cond
  114.5 0.9 copy-start.6
  114.5 2.3 copy-start.21
  115.4 1.4 copy-start.19
  116.8 77.0 %all-to-all-start = ((bf16[16,96,768]{2,1,0:T(8,128)(2,1)}), bf16[16,96,768]{2,1,0:T(8,128)(2,1)S(1)}, u32[]{:S(2)}, u32[]{:S(2)}) async-start(bf16[16,96,768]{2,1,0:T(8,128)(2,1)} %bitcast.22), calls=%async_computation | async-start | bytes 4718592 | tf_op jit(solution)/shard_map/cond/branch_1_fun/all_to_all | solution.py:685
  122.7 20.2 %copy-start.7 = (bf16[512,768]{1,0:T(8,128)(2,1)S(1)}, bf16[512,768]{1,0:T(8,128)(2,1)}, u32[]{:S(2)}) copy-start(bf16[512,768]{1,0:T(8,128)(2,1)} %copy-done.6) | copy-start | bytes 2359300 | tf_op jit(solution)/shard_map/cond
  122.7 20.2 %copy-start.22 = (bf16[512,768]{1,0:T(8,128)(2,1)S(1)}, bf16[512,768]{1,0:T(8,128)(2,1)}, u32[]{:S(2)}) copy-start(bf16[512,768]{1,0:T(8,128)(2,1)} %copy-done.21) | copy-start | bytes 2359300 | tf_op jit(solution)/shard_map/cond
  122.7 20.2 %collective-permute-start.3 = (bf16[512,768]{1,0:T(8,128)(2,1)}, bf16[512,768]{1,0:T(8,128)(2,1)S(1)}, u32[]{:S(2)}, u32[]{:S(2)}) collective-permute-start(bf16[512,768]{1,0:T(8,128)(2,1)} %copy-done.21), channel_id=1, source_target_pairs={{0,16},{16,0},{1,17},{17,1},{2,18},{18,2},{3,19},{19,3},{4,20},{20... | collective-permute-start | bytes 2359304 | tf_op jit(solution)/shard_map/cond/branch_1_fun/ppermute | solution.py:682
  150.0 6.2 %collective-permute-start.4 = (f32[1024,768]{1,0:T(8,128)}, f32[1024,768]{1,0:T(8,128)}, u32[]{:S(2)}, u32[]{:S(2)}) collective-permute-start(f32[1024,768]{1,0:T(8,128)} %get-tuple-element.162), channel_id=1, source_target_pairs={{0,8},{8,0},{1,9},{9,1},{2,10},{10,2},{3,11},{11,3},{4,12},{12,4},... | collective-permute-start | bytes 9437192 | tf_op jit(solution)/shard_map/cond/branch_1_fun/ppermute | solution.py:679
  150.0 20.7 %collective-permute-start.6 = (bf16[512,768]{1,0:T(8,128)(2,1)}, bf16[512,768]{1,0:T(8,128)(2,1)}, u32[]{:S(2)}, u32[]{:S(2)}) collective-permute-start(bf16[512,768]{1,0:T(8,128)(2,1)} %get-tuple-element.378), channel_id=1, source_target_pairs={{0,16},{16,0},{1,17},{17,1},{2,18},{18,2},{3,19},{19,3},{4,20},{20... | collective-permute-start | bytes 2359304 | tf_op jit(solution)/shard_map/cond/branch_1_fun/ppermute | solution.py:682
  150.4 36.7 %collective-permute-start.5 = (bf16[512,768]{1,0:T(8,128)(2,1)}, bf16[512,768]{1,0:T(8,128)(2,1)}, u32[]{:S(2)}, u32[]{:S(2)}) collective-permute-start(bf16[512,768]{1,0:T(8,128)(2,1)} %get-tuple-element.377), channel_id=1, source_target_pairs={{0,16},{16,0},{1,17},{17,1},{2,18},{18,2},{3,19},{19,3},{4,20},{20... | collective-permute-start | bytes 2359304 | tf_op jit(solution)/shard_map/cond/branch_1_fun/ppermute | solution.py:682
  187.1 10.9 %copy-start.32 = (f32[3,2,1024]{2,1,0:T(2,128)S(1)}, f32[3,2,1024]{2,1,0:T(2,128)}, u32[]{:S(2)}) copy-start(f32[3,2,1024]{2,1,0:T(2,128)} %get-tuple-element.376) | copy-start | bytes 73732 | tf_op jit(solution)/shard_map/cond
  187.1 10.9 %copy-start.33 = (f32[1,768]{1,0:T(1,128)S(1)}, f32[1,768]{1,0:T(1,128)}, u32[]{:S(2)}) copy-start(f32[1,768]{1,0:T(1,128)} %get-tuple-element.374) | copy-start | bytes 9220 | tf_op jit(solution)/shard_map/cond
  198.0 52.2 %all-to-all-start.1 = ((bf16[8,96,768]{2,1,0:T(8,128)(2,1)}), bf16[8,96,768]{2,1,0:T(8,128)(2,1)S(1)}, u32[]{:S(2)}, u32[]{:S(2)}) async-start(bf16[8,96,768]{2,1,0:T(8,128)(2,1)} %bitcast.8), calls=%async_computation.1 | async-start | bytes 2359296 | tf_op jit(solution)/shard_map/all_to_all | solution.py:688
  211.5 1.4 copy-start.2
  217.4 29.2 %collective-permute-start.21 = (bf16[1024,768]{1,0:T(8,128)(2,1)}, bf16[1024,768]{1,0:T(8,128)(2,1)}, u32[]{:S(2)}, u32[]{:S(2)}) collective-permute-start(bf16[1024,768]{1,0:T(8,128)(2,1)} %get-tuple-element.307), channel_id=1, source_target_pairs={{0,8},{8,0},{1,9},{9,1},{2,10},{10,2},{3,11},{11,3},{4,12},{12,4},... | collective-permute-start | bytes 4718600 | tf_op jit(solution)/shard_map/ppermute | solution.py:679
  219.6 1.4 collective-permute-start.17
  221.1 3.7 %collective-permute-start.18 = (f32[1632]{0:T(1024)S(1)}, f32[1632]{0:T(1024)S(1)}, u32[]{:S(2)}, u32[]{:S(2)}) collective-permute-start(f32[1632]{0:T(1024)S(1)} %maximum_add_fusion), channel_id=1, source_target_pairs={{0,1},{1,0},{2,3},{3,2},{4,5},{5,4},{6,7},{7,6},{8,9},{9,8},{10,11... | collective-permute-start | bytes 19592 | tf_op jit(solution)/shard_map/ppermute | solution.py:797
  224.7 7.0 %collective-permute-start.19 = (f32[1632]{0:T(1024)S(1)}, f32[1632]{0:T(1024)S(1)}, u32[]{:S(2)}, u32[]{:S(2)}) collective-permute-start(f32[1632]{0:T(1024)S(1)} %add.27), channel_id=1, source_target_pairs={{0,2},{1,3},{2,0},{3,1},{4,6},{5,7},{6,4},{7,5},{8,10},{9,11},{10,... | collective-permute-start | bytes 19592 | tf_op jit(solution)/shard_map/ppermute | solution.py:797
  231.7 8.9 %collective-permute-start.20 = (f32[1632]{0:T(1024)S(1)}, f32[1632]{0:T(1024)S(1)}, u32[]{:S(2)}, u32[]{:S(2)}) collective-permute-start(f32[1632]{0:T(1024)S(1)} %add.28), channel_id=1, source_target_pairs={{0,4},{1,5},{2,6},{3,7},{4,0},{5,1},{6,2},{7,3},{8,12},{9,13},{10,... | collective-permute-start | bytes 19592 | tf_op jit(solution)/shard_map/ppermute | solution.py:797
  241.5 5.1 %copy-start.14 = (f32[768]{0:T(1024)}, f32[768]{0:T(1024)S(1)}, u32[]{:S(2)}) copy-start(f32[768]{0:T(1024)S(1)} %get-tuple-element.336.refs_1_) | copy-start | bytes 9220
  241.5 5.1 %copy-start.15 = (f32[768]{0:T(1024)}, f32[768]{0:T(1024)S(1)}, u32[]{:S(2)}) copy-start(f32[768]{0:T(1024)S(1)} %get-tuple-element.337.refs_0_) | copy-start | bytes 9220
  241.5 1.3 copy-start.12
  242.8 1.3 copy-start.13
Sparse Core Ops, SparseCore 0:
  79.7 133.9 all-reduce.3

commit v4 on v3

--- a/solution.py
+++ b/solution.py
@@ -41,7 +41,7 @@
     return jax.ShapeDtypeStruct(shape, dtype)
 
 
-def call(kernel, name, token, args, in_specs, outs, out_specs, grid=(1,), scratch=(), aliases=None):
+def call(kernel, name, token, args, in_specs, outs, out_specs, grid=(1,), scratch=(), aliases=None, vmem=VMEM_BYTES):
     n_in, n_out = len(args), len(outs)
 
     def body(token_ref, *refs):
@@ -57,7 +57,7 @@
         scratch_shapes=list(scratch),
         out_shape=[shape_of(token.shape, token.dtype)] + list(outs),
         input_output_aliases={0: 0, **(aliases or {})},
-        compiler_params=pltpu.CompilerParams(vmem_limit_bytes=VMEM_BYTES),
+        compiler_params=pltpu.CompilerParams(vmem_limit_bytes=vmem),
         name=name,
     )(token, *args)
     return res[1:], res[0]
@@ -315,6 +315,7 @@
         outs,
         [whole(o.shape) for o in outs[:3]] + grad_specs,
         grid=(2 * tiles,),
+        vmem=56 * 1024 * 1024,
         scratch=[
             pltpu.VMEM((seq, width), BF16),
             pltpu.VMEM((width, seq), BF16),
@@ -444,13 +445,11 @@
 
 def grad_attn_kernel(docs, pairs, *refs):
     groups = [refs[i * docs : (i + 1) * docs] for i in range(4)]
-    (out_ref,) = refs[4 * docs :]
+    mine_ref, other_ref = refs[4 * docs :]
     normed, gp, low, att = (jnp.concatenate([r[...] for r in g], axis=0) for g in groups)
     step = pl.program_id(0)
-    width = out_ref.shape[0] // 2
-    cols = width // 4
+    cols = mine_ref.shape[0] // 4
     heads = cols // HD
-    core = lax.axis_index("core")
     grads = dot_tn(gp, normed).astype(BF16)
     outer = dot_tn(att, low).astype(BF16)
     for p in range(pairs):
@@ -459,18 +458,18 @@
         def _(p=p):
             for i in range(2):
                 head = 2 * p + i
-                base = (core if head < heads else 1 - core) * width + (head % heads) * HD
+                ref = mine_ref if head < heads else other_ref
+                at = (head % heads) * HD
                 for part in range(3):
                     piece = grads[part * PAIR + i * HD : part * PAIR + (i + 1) * HD, :]
-                    out_ref[pl.ds(pl.multiple_of(base + part * cols, HD), HD), :] = piece
-                piece = outer[i * HD : (i + 1) * HD, :]
-                out_ref[pl.ds(pl.multiple_of(base + 3 * cols, HD), HD), :] = piece
+                    ref[part * cols + at : part * cols + at + HD, :] = piece
+                ref[3 * cols + at : 3 * cols + at + HD, :] = outer[i * HD : (i + 1) * HD, :]
 
 
 def grad_attn(ids, normeds, gps, lows, atts, docs):
     seq, width = normeds[0].shape
     pairs = atts[0].shape[1] // PAIR
-    outs = [shape_of((2 * width, width), BF16)]
+    outs = [shape_of((width, width), BF16)] * 2
     return call(
         functools.partial(grad_attn_kernel, docs, pairs),
         "grad_attn",
@@ -481,7 +480,7 @@
         + [whole((seq, width))] * docs
         + [pl.BlockSpec((seq, PAIR), lambda p: (0, p))] * docs,
         outs,
-        [whole((2 * width, width))],
+        [whole((width, width))] * 2,
         grid=(pairs,),
     )
 
@@ -581,24 +580,16 @@
     return call(lambda *refs: None, "need", ids, arrays, [anywhere] * len(arrays), [], [])[1]
 
 
-def sum_core_kernel(a_ref, b_ref, c_ref, d_ref, ab_ref, cd_ref):
-    ab_ref[...] = (a_ref[...].astype(F32) + b_ref[...].astype(F32)).astype(BF16)
-    cd_ref[...] = (c_ref[...].astype(F32) + d_ref[...].astype(F32)).astype(BF16)
-
-
-def sum_core(ids, a, b, c, d):
-    steps = 4
-    specs = [pl.BlockSpec((v.shape[0] // steps, v.shape[1]), lambda i: (i, 0)) for v in (a, b, c, d)]
-    return call(
-        sum_core_kernel,
-        "sum_core",
-        ids,
-        (a, b, c, d),
-        specs,
-        [shape_of(a.shape, BF16), shape_of(c.shape, BF16)],
-        [specs[0], specs[2]],
-        grid=(steps,),
-    )
+def sum_core_kernel(*refs):
+    for i, out_ref in enumerate(refs[2 * len(refs) // 3 :]):
+        out_ref[...] = (refs[2 * i][...].astype(F32) + refs[2 * i + 1][...].astype(F32)).astype(BF16)
+
+
+def sum_core(ids, *arrays):
+    steps = 2
+    specs = [pl.BlockSpec((v.shape[0] // steps, v.shape[1]), lambda i: (i, 0)) for v in arrays]
+    outs = [shape_of(v.shape, BF16) for v in arrays[::2]]
+    return call(sum_core_kernel, "sum_core", ids, arrays, specs, outs, specs[::2], grid=(steps,))
 
 
 def widen_kernel(*refs):
@@ -646,9 +637,9 @@
 
 def sum_parts(token, got, dp):
     width = got.shape[1]
-    rows = got.shape[0] // (2 * dp)
+    rows = got.shape[0] // dp
     if rows % 16:
-        total = jnp.sum(got.reshape(2 * dp, rows, width).astype(F32), axis=0).astype(BF16)
+        total = jnp.sum(got.reshape(dp, rows, width).astype(F32), axis=0).astype(BF16)
         return [jnp.tile(total, (dp, 1))], token
     return call(
         sum_kernel,
@@ -680,9 +671,6 @@
 
     def from_x(v):
         return lax.ppermute(v, "x", [(0, 1), (1, 0)])
-
-    def scatter(v):
-        return lax.all_to_all(v, ("core", "dp"), 0, 0, tiled=True)
 
     def spread(v):
         return lax.all_to_all(v, "dp", 0, 0, tiled=True)
@@ -756,51 +744,58 @@
                 ids, res = back_of(doc, ids)
                 results.append(res)
             gp, low = [r[3] for r in results], [r[1] for r in results]
-            (gattn,), ids = grad_attn(ids, normed, gp, low, att, docs)
-            return ids, results[1:], gattn
-
-        ids, results, gattn = region(always, others, ids)
+            (gattn, gattn_c), ids = grad_attn(ids, normed, gp, low, att, docs)
+            return ids, results[1:], gattn, gattn_c
+
+        ids, results, gattn, gattn_c = region(always, others, ids)
         gmid, low, ggain_two, gp, nown, diag = zip(first, *results)
         ids = need(ids, noth[0])
-        nown = [nown_0] + list(nown[1:])
-        for doc in range(1, docs):
-            (nown[doc],), ids = gate(ids, nown[doc])
-            noth.append(from_x(nown[doc]))
-        (gattn,), ids = gate(ids, gattn)
-        gattn = scatter(gattn)
-        hsent, hoth = [], []
-        for doc in every:
-            (send,), ids = gate(ids, hown[doc])
-            hsent.append(send)
-            hoth.append(from_x(send))
-        (gsrc, gsrc_send, ggain_one), ids = grad_input(ids, inputs, gains, gmid, nown, noth, docs)
-        gsrc_got = from_core(gsrc_send)
-
-        (gsrc,), ids = place(ids, gsrc, gsrc_got)
-        ids = need(ids, *hoth)
+        (gattn_c,), ids = gate(ids, gattn_c)
+        (gattn,), ids = sum_core(ids, gattn, from_core(gattn_c))
+        gattn = spread(gattn)
+
+        def rows_back(ids):
+            mine, got = [nown_0] + list(nown[1:]), list(noth)
+            for doc in range(1, docs):
+                (mine[doc],), ids = gate(ids, mine[doc])
+                got.append(from_x(mine[doc]))
+            sent, hoth = list(hown), []
+            for doc in range(docs // 2):
+                (sent[doc],), ids = gate(ids, sent[doc])
+                hoth.append(from_x(sent[doc]))
+            (gsrc, gsrc_send, ggain_one), ids = grad_input(ids, inputs, gains, gmid, mine, got, docs)
+            diag_bucket = jnp.concatenate([buckets[:, 0], buckets[:1, -1], buckets[:-1, -1]])
+            one_hot = (diag_bucket[:, None] == jnp.arange(table_rows)[None, :]).astype(F32)
+            diags = sum(diag).reshape(2 * heads, 2 * seq)
+            table = lax.dot_general(
+                diags, one_hot, (((1,), (0,)), ((), ())), precision=lax.Precision.HIGHEST, preferred_element_type=F32
+            )
+            ggain_ffn = sum(ggain_two)
+            small = jnp.concatenate([ggain_one.reshape(-1), ggain_ffn.reshape(-1), table[:heads].reshape(-1)])
+            small_send = jnp.concatenate([ggain_one.reshape(-1), ggain_ffn.reshape(-1), table[heads:].reshape(-1)])
+            small = small + from_core(small_send)
+            for s in range(dp.bit_length() - 1):
+                small = small + lax.ppermute(small, "dp", [(i, i ^ (1 << s)) for i in range(dp)])
+            grad_gain_attn, grad_gain_ffn = small[:width], small[width : 2 * width]
+            grad_table = small[2 * width :].reshape(heads, table_rows).T
+            ids = need(ids, grad_gain_attn, grad_gain_ffn, grad_table)
+            (gsrc,), ids = place(ids, gsrc, from_core(gsrc_send))
+            ids = need(ids, *hoth)
+            return ids, gsrc, (grad_gain_attn, grad_gain_ffn, grad_table), sent, hoth
+
+        ids, gsrc, smalls, hsent, hoth = region(always, rows_back, ids)
         (gattn,), ids = sum_parts(ids, gattn, dp)
-        return ids, gattn, gsrc, ggain_one, ggain_two, diag, hsent, hoth
-
-    ids, gattn, gsrc, ggain_one, ggain_two, diag, hsent, hoth = region(always, attention_back, ids)
+        return ids, gattn, gsrc, smalls, hsent, hoth
+
+    ids, gattn, gsrc, smalls, hsent, hoth = region(always, attention_back, ids)
+    grad_gain_attn, grad_gain_ffn, grad_table = smalls
+    for doc in range(docs // 2, docs):
+        (hsent[doc],), ids = gate(ids, hsent[doc])
+        hoth.append(from_x(hsent[doc]))
     gattn = spread(gattn)
-    diag_bucket = jnp.concatenate([buckets[:, 0], buckets[:1, -1], buckets[:-1, -1]])
-    one_hot = (diag_bucket[:, None] == jnp.arange(table_rows)[None, :]).astype(F32)
-    diag = sum(diag).reshape(2 * heads, 2 * seq)
-    table = lax.dot_general(
-        diag, one_hot, (((1,), (0,)), ((), ())), precision=lax.Precision.HIGHEST, preferred_element_type=F32
-    )
-    ggain_two = sum(ggain_two)
-    small = jnp.concatenate([ggain_one.reshape(-1), ggain_two.reshape(-1), table[:heads].reshape(-1)])
-    small_send = jnp.concatenate([ggain_one.reshape(-1), ggain_two.reshape(-1), table[heads:].reshape(-1)])
-    small = small + from_core(small_send)
-    for s in range(dp.bit_length() - 1):
-        small = small + lax.ppermute(small, "dp", [(i, i ^ (1 << s)) for i in range(dp)])
-    grad_gain_attn, grad_gain_ffn = small[:width], small[width : 2 * width]
-    grad_table = small[2 * width :].reshape(heads, table_rows).T
+    (grad_w_back, grad_w_in), ids = widen(ids, gback, gin)
     (mixed, mixed_send), ids = mix(ids, middle, hsent, hoth, docs)
-    ids = need(ids, grad_gain_attn, grad_gain_ffn, grad_table)
     mixed_got = from_core(mixed_send)
-    (grad_w_back, grad_w_in), ids = widen(ids, gback, gin)
     (mixed,), ids = place(ids, mixed, mixed_got)
     (grad_w_qkv, grad_w_out), ids = widen_attn(ids, gattn)
     grad_w_qkv = grad_w_qkv.reshape(3, width // 4, width).transpose(0, 2, 1)

time: 260 us -> 236 us (0.908)
  waiting for transfers between devices: 77.7 us -> 58 us
  starting transfers between devices: 41 us -> 33.6 us
  local copies, waits for them, and re-layouts: 15.7 us -> 19 us
    ppermute x9, waiting for transfers between devices: 52.9 us -> 22.3 us  [from_x(): return lax.ppermute(v, 'x', [(0, 1), (1, 0)])]
    all_to_all x1 -> x2, waiting for transfers between devices: 0.01 us -> 9.18 us  [spread(): return lax.all_to_all(v, 'dp', 0, 0, tiled=True)]
    psum x1, waiting for transfers between devices: 0.02 us -> 9.15 us  [per_device(): gback, gin = lax.psum((gback, gin), 'dp')]
    ppermute x3, waiting for transfers between devices: 11.6 us -> 3.99 us  [rows_back(): lax.ppermute(small, 'dp', [(i, i ^ 1 << s) for i in range(dp)])]
    ppermute x10 -> x11, waiting for transfers between devices: 6.55 us -> 13.3 us  [from_core(): return lax.ppermute(v, 'core', [(0, 1), (1, 0)])]
    all_to_all x1 -> x0, waiting for transfers between devices: 6.68 us -> none  [scatter(): return lax.all_to_all(v, ('core', 'dp'), 0, 0, tiled=True)]
    all_to_all x1 -> x0, starting transfers between devices: 5.85 us -> none  [scatter(): return lax.all_to_all(v, ('core', 'dp'), 0, 0, tiled=True)]
    slice x8, local copies, waits for them, and re-layouts: 1.17 us -> 4.01 us  [the longest x1 1.18 us: rows_back(): buckets[:1, -1]]
  transfers between devices with their start and end apart: 25 -> 26, of which waited for: 13 -> 15; matrix products, arithmetic and copies ran while one was open for 3% -> 5% of each run, Pallas kernels for 41% -> 44%
where the time goes in v4:
time: 236 us; the launch traced here: 235 us
  Pallas kernels  108 us (46%)
  waiting for transfers between devices  58 us (25%)
  starting transfers between devices  33.6 us (14%)
  local copies, waits for them, and re-layouts  19 us (8%)
  between operations  14.3 us (6%)
    pallas_call x30, Pallas kernels, call(): pl.pallas_call(body, grid=grid, in_specs=[anywhere] + list(in_specs), out...  108 us
    ppermute x9, waiting for transfers between devices, from_x(): return lax.ppermute(v, 'x', [(0, 1), (1, 0)])  22.3 us
    ppermute x9, starting transfers between devices, from_x(): return lax.ppermute(v, 'x', [(0, 1), (1, 0)])  13.9 us
    ppermute x11, waiting for transfers between devices, from_core(): return lax.ppermute(v, 'core', [(0, 1), (1, 0)])  13.3 us
    all_to_all x2, starting transfers between devices, spread(): return lax.all_to_all(v, 'dp', 0, 0, tiled=True)  11.6 us
    all_to_all x2, waiting for transfers between devices, spread(): return lax.all_to_all(v, 'dp', 0, 0, tiled=True)  9.18 us
    psum x1, waiting for transfers between devices, per_device(): gback, gin = lax.psum((gback, gin), 'dp')  9.15 us
    unnamed x48, local copies, waits for them, and re-layouts  6.84 us
  transfers between devices with their start and end apart: 26, of which 15 were waited for; matrix products, arithmetic and copies ran while one was open for 5% of the time, Pallas kernels for 44%

profile of v4, /device:TPU:0, one launch (start us, length us, event | category | flops | bytes accessed | tf_op | source)
XLA Modules:
  0.0 235.4 jit_solution(1359839428775869489)
XLA Ops:
  7.3 1.4 fusion.3.refs_3_
  8.7 0.5 collective-permute-start.11
  9.8 2.6 %collective-permute-start.12 = (bf16[192,768]{1,0:T(8,128)(2,1)S(1)}, bf16[192,768]{1,0:T(8,128)(2,1)S(1)}, u32[]{:S(2)}, u32[]{:S(2)}) collective-permute-start(bf16[192,768]{1,0:T(8,128)(2,1)S(1)} %copy-done.14), channel_id=1, source_target_pairs={{0,16},{16,0},{1,17},{17,1},{2,18},{18,2},{3,19},{19,3},{4,20},{20... | collective-permute-start | bytes 884744 | tf_op jit(solution)/shard_map/ppermute | solution.py:673
  12.7 9.0 %attn_fwd.2 = (f32[8,128]{1,0:T(8,128)S(1)}, bf16[1152,768]{1,0:T(8,128)(2,1)S(1)}, f32[6,1024]{1,0:T(8,128)S(1)}, bf16[512,768]{1,0:T(8,128)(2,1)}, bf16[512,11...) custom-call(f32[8,128]{1,0:T(8,128)S(1)} %broadcast_39_token_ref.2.t, ...), custom_call_target="tpu_custom_call", output_to_operand_aliasing={{0}: (0, {})} | custom-call | tf_op jit(solution)/shard_map/attn_fwd/pallas_call | solution.py:52
  21.7 2.9 %collective-permute-start.13 = (bf16[512,384]{1,0:T(8,128)(2,1)S(1)}, bf16[512,384]{1,0:T(8,128)(2,1)S(1)}, u32[]{:S(2)}, u32[]{:S(2)}) collective-permute-start(bf16[512,384]{1,0:T(8,128)(2,1)S(1)} %get-tuple-element.311.refs_1_), channel_id=1, source_target_pairs={{0,16},{16,0},{1,17},{17,1},{2,18},{18,2},{3,19},{19,3},{4,20},{20... | collective-permute-start | bytes 1179656 | tf_op jit(solution)/shard_map/ppermute | solution.py:673
  24.6 8.4 %attn_fwd.3 = (f32[8,128]{1,0:T(8,128)S(1)}, bf16[512,768]{1,0:T(8,128)(2,1)}, bf16[512,1152]{1,0:T(8,128)(2,1)}, bf16[6,512,512]{2,1,0:T(8,128)(2,1)}, bf16[512,384]{1,0:T(8,128)(2,1)S(1)}) custom-call(f32[8,128]{1,0:T(8,128)S(1)} %get-tuple-element.307.token_ref, s32[4]{0:T(128)S(1)} %copy-done.10, ...), custom_call_target="tpu_custom_call", output_to_operand_aliasing={{0}: (0, {})} | custom-call | tf_op jit(solution)/shard_map/attn_fwd/pallas_call | solution.py:52
  33.3 1.5 collective-permute-done.15.refs_6_
  34.8 0.7 copy-done.28
  35.6 16.3 %ffn.2 = (f32[8,128]{1,0:T(8,128)S(1)}, f32[512,768]{1,0:T(8,128)}, bf16[512,768]{1,0:T(8,128)(2,1)}, bf16[512,768]{1,0:T(8,128)(2,1)}, bf16[768,768]{1,0:T(8,12...) custom-call(f32[8,128]{1,0:T(8,128)S(1)} %get-tuple-element.310.toke, ...), custom_call_target="tpu_custom_call", output_to_operand_aliasing={{0}: (0, {})} | custom-call | tf_op jit(solution)/shard_map/ffn/pallas_call | solution.py:52
  52.0 2.0 collective-permute-start.19
  54.0 17.4 %ffn.3 = (f32[8,128]{1,0:T(8,128)S(1)}, f32[512,768]{1,0:T(8,128)}, bf16[512,768]{1,0:T(8,128)(2,1)S(1)}, bf16[512,768]{1,0:T(8,128)(2,1)}, bf16[768,768]{1,0:T(...) custom-call(f32[8,128]{1,0:T(8,128)S(1)} %get-tuple-element.316.toke, ...), custom_call_target="tpu_custom_call", output_to_operand_aliasing={{0}: (0, {})} | custom-call | tf_op jit(solution)/shard_map/ffn/pallas_call | solution.py:52
  71.4 0.6 collective-permute-done.19.refs_0_.refs_2_
  72.3 7.6 %conditional.4 = ((f32[8,128]{1,0:T(8,128)S(1)}, bf16[768,768]{1,0:T(8,128)(2,1)}, bf16[768,768]{1,0:T(8,128)(2,1)})) conditional(s32[]{:T(128)} %convert_element_type.14, () %tuple.40, (bf16[768,768]{1,0:T(8,128)(2,1)}, bf16[768,768]{1,0:T(8,128)(2,1)}, f32[8,128]{1,0:T(8,128)S(1)}, bf16[768,768]{1,0:T(8,128)(2,1)}, bf16[768,768]{1,0:T(8,128)(2,1)}) %tuple.41), branch_computations={%region_0.1_spmd, %region_1.2_spmd} | conditional | bytes 9437272 | solution.py:658
  72.3 0.5 collective-permute-start.1
  72.8 2.5 %collective-permute-done.refs_1_ = bf16[768,768]{1,0:T(8,128)(2,1)S(1)} collective-permute-done((bf16[768,768]{1,0:T(8,128)(2,1)}, bf16[768,768]{1,0:T(8,128)(2,1)S(1)}, u32[]{:S(2)}, u32[]{:S(2)}) %collective-permute-start) | collective-permute-done | bytes 1179680 | tf_op jit(solution)/shard_map/cond/branch_1_fun/ppermute | solution.py:670
  75.3 1.7 collective-permute-done.1.refs_3_
  77.0 2.8 %sum_core.2 = (f32[8,128]{1,0:T(8,128)S(1)}, bf16[768,768]{1,0:T(8,128)(2,1)}, bf16[768,768]{1,0:T(8,128)(2,1)}) custom-call(f32[8,128]{1,0:T(8,128)S(1)} %get-tuple-element.126.token_ref, bf16[768,768]{1,0:T(8,128)(2,1)} %get-tuple-element.127.refs_0_, bf16[768,768]{1,0:T(8,128)(2,1)S(1)} %collective-permute-done.refs_1_, ...), custom_call_target="tpu_custom_call", output_to_operand_aliasing={{0}: (0, {})} | custom-call | tf_op jit(solution)/shard_map/cond/branch_1_fun/sum_core/pallas_call | solution.py:52
  79.9 1.5 collective-permute-start.20
  81.4 1.9 copy-done.2
  83.3 1.3 copy-done.6
  84.6 11.7 %attn_bwd.3 = (f32[8,128]{1,0:T(8,128)S(1)}, f32[512,768]{1,0:T(8,128)}, bf16[512,768]{1,0:T(8,128)(2,1)}, f32[1,768]{1,0:T(1,128)}, bf16[512,1152]{1,0:T(8,128)...) custom-call(f32[8,128]{1,0:T(8,128)S(1)} %get-tuple-element.329.token_ref, ...), custom_call_target="tpu_custom_call", output_to_operand_aliasing={{0}: (0, {})} | custom-call | tf_op jit(solution)/shard_map/attn_bwd/pallas_call | solution.py:52
  96.3 3.5 %collective-permute-done.20.refs_0_ = bf16[512,768]{1,0:T(8,128)(2,1)S(1)} collective-permute-done((bf16[512,768]{1,0:T(8,128)(2,1)}, bf16[512,768]{1,0:T(8,128)(2,1)S(1)}, u32[]{:S(2)}, u32[]{:S(2)}) %collective-permute-start.20) | collective-permute-done | bytes 786464 | tf_op jit(solution)/shard_map/ppermute | solution.py:673
  99.8 88.5 %conditional.5 = (f32[8,128]{1,0:T(8,128)S(1)}, bf16[768,768]{1,0:T(8,128)(2,1)}, f32[2048,768]{1,0:T(8,128)}, f32[768]{0:T(1024)}, f32[768]{0:T(1024)}, /*index...) conditional(s32[]{:T(128)} %convert_element_type.14, () %tuple.39, ...), branch_computations={%region_2.3_spmd, %region_3.8_spmd} | conditional | flops 2414081 | bytes 73890032 | solution.py:658
  99.8 0.9 copy-done.21
  100.6 1.5 collective-permute-start.9
  102.1 18.1 %conditional = (f32[8,128]{1,0:T(8,128)S(1)}, f32[512,768]{1,0:T(8,128)}, f32[1,768]{1,0:T(1,128)}, bf16[512,768]{1,0:T(8,128)(2,1)}, f32[3,2,1024]{2,1,0:T(2,12...) conditional(s32[]{:T(128)} %convert_element_type.1, () %tuple.29, (f32[8,128]{1,0:T(8,128)S(1)}, ...), branch_computations={%region_4.4_spmd, %region_5.5_spmd} | conditional | bytes 17301728 | solution.py:658
  102.2 12.9 %attn_bwd.2 = (f32[8,128]{1,0:T(8,128)S(1)}, f32[512,768]{1,0:T(8,128)}, bf16[512,768]{1,0:T(8,128)(2,1)S(1)}, f32[1,768]{1,0:T(1,128)}, bf16[512,1152]{1,0:T(8,...) custom-call(f32[8,128]{1,0:T(8,128)S(1)} %get-tuple-element.131.token_ref, ...), custom_call_target="tpu_custom_call", output_to_operand_aliasing={{0}: (0, {})} | custom-call | tf_op jit(solution)/shard_map/cond/branch_1_fun/cond/branch_1_fun/attn_bwd/pallas_call | solution.py:52
  115.1 5.1 %grad_attn.1 = (f32[8,128]{1,0:T(8,128)S(1)}, bf16[768,768]{1,0:T(8,128)(2,1)}, bf16[768,768]{1,0:T(8,128)(2,1)}) custom-call(f32[8,128]{1,0:T(8,128)S(1)} %get-tuple-element.142.token_ref, bf16[512,768]{1,0:T(8,128)(2,1)S(1)} %copy-done.29, bf16[512,768]{1,0:T(8,128)(2,1)S(1)} %copy-done.30, ...), custom_call_target="tpu_custom_call", output_to_operand_aliasing={{0}: (0, {})} | custom-call | tf_op jit(solution)/shard_map/cond/branch_1_fun/cond/branch_1_fun/grad_attn/pallas_call | solution.py:52
  120.3 3.0 %collective-permute-done.10.refs_1_ = bf16[768,768]{1,0:T(8,128)(2,1)S(1)} collective-permute-done((bf16[768,768]{1,0:T(8,128)(2,1)}, bf16[768,768]{1,0:T(8,128)(2,1)S(1)}, u32[]{:S(2)}, u32[]{:S(2)}) %collective-permute-start.10) | collective-permute-done | bytes 1179680 | tf_op jit(solution)/shard_map/cond/branch_1_fun/ppermute | solution.py:670
  123.6 1.0 copy-done.9
  124.7 6.0 %all-to-all-start = ((bf16[8,96,768]{2,1,0:T(8,128)(2,1)}), bf16[8,96,768]{2,1,0:T(8,128)(2,1)S(1)}, u32[]{:S(2)}, u32[]{:S(2)}) async-start(bf16[8,96,768]{2,1,0:T(8,128)(2,1)} %bitcast.21), calls=%async_computation | async-start | bytes 2359296 | tf_op jit(solution)/shard_map/cond/branch_1_fun/all_to_all | solution.py:676
  130.7 52.9 %conditional.1 = (f32[8,128]{1,0:T(8,128)S(1)}, f32[2048,768]{1,0:T(8,128)}, f32[768]{0:T(1024)}, f32[768]{0:T(1024)}, f32[32,3]{1,0:T(8,128)}, /*index=5*/bf16[...) conditional(s32[]{:T(128)} %convert_element_type.1, () %tuple.28, (f32[8,128]{1,0:T(8,128)S(1)}, ...), branch_computations={%region_6.6_spmd, %region_7.7_spmd} | conditional | flops 2414080 | bytes 29455080 | solution.py:658
  130.7 1.1 collective-permute-start.2
  131.8 18.2 %collective-permute-done.2.refs_7_ = bf16[512,768]{1,0:T(8,128)(2,1)S(1)} collective-permute-done((bf16[512,768]{1,0:T(8,128)(2,1)S(1)}, bf16[512,768]{1,0:T(8,128)(2,1)S(1)}, u32[]{:S(2)}, u32[]{:S(2)}) %collective-permute-start.2) | collective-permute-done | bytes 786464 | tf_op jit(solution)/shard_map/cond/branch_1_fun/cond/branch_1_fun/ppermute | solution.py:673
  150.1 6.9 %grad_input.1 = (f32[8,128]{1,0:T(8,128)S(1)}, f32[2048,768]{1,0:T(8,128)}, f32[1024,768]{1,0:T(8,128)}, f32[1,768]{1,0:T(1,128)S(1)}) custom-call(f32[8,128]{1,0:T(8,128)S(1)} %get-tuple-element.162.token_ref, bf16[2048,768]{1,0:T(8,128)(2,1)} %get-tuple-element.163.refs_0_, ...), custom_call_target="tpu_custom_call", output_to_operand_aliasing={{0}: (0, {})} | custom-call | tf_op jit(solution)/shard_map/cond/branch_1_fun/cond/branch_1_fun/grad_input/pallas_call | solution.py:52
  157.0 1.1 collective-permute-start.8
  158.1 2.6 %copy.65 = s32[512,512]{0,1:T(8,128)} copy(s32[512,512]{1,0:T(8,128)} %get-tuple-element.415) | data formatting | bytes 2097152 | tf_op jit(solution)/shard_map
  160.7 0.7 slice.38
  161.4 0.7 slice.40
  162.1 1.2 slice.39
  163.4 0.7 pad_add_fusion
  164.9 0.9 collective-permute-done.3
  165.9 1.7 collective-permute-start.4
  167.6 2.0 collective-permute-done.4
  169.5 1.7 collective-permute-start.5
  171.2 2.0 collective-permute-done.5
  173.2 2.6 %collective-permute-start.6 = (f32[1632]{0:T(1024)S(1)}, f32[1632]{0:T(1024)S(1)}, u32[]{:S(2)}, u32[]{:S(2)}) collective-permute-start(f32[1632]{0:T(1024)S(1)} %add.20), channel_id=1, source_target_pairs={{0,4},{1,5},{2,6},{3,7},{4,0},{5,1},{6,2},{7,3},{8,12},{9,13},{10,... | collective-permute-start | bytes 19592 | tf_op jit(solution)/shard_map/cond/branch_1_fun/cond/branch_1_fun/ppermute | solution.py:778
  175.8 2.1 copy.113
  178.0 0.7 copy.62
  178.7 0.6 fusion.4
  179.3 4.2 %place.2 = (f32[8,128]{1,0:T(8,128)S(1)}, f32[2048,768]{1,0:T(8,128)}) custom-call(f32[8,128]{1,0:T(8,128)S(1)} %need.6.token_ref, f32[2048,768]{1,0:T(8,128)} %get-tuple-element.177.refs_0_, f32[1024,768]{1,0:T(8,128)} %collective-permute-done.7.refs_1_), custom_call_target="tpu_custom_call", output_to_operand_aliasing={{0}: (0, {}), {1}: (1, {})} | custom-call | tf_op jit(solution)/shard_map/cond/branch_1_fun/cond/branch_1_fun/place/pallas_call | solution.py:52
  183.5 1.4 copy.67
  184.9 3.4 %sum_parts.1 = (f32[8,128]{1,0:T(8,128)S(1)}, bf16[768,768]{1,0:T(8,128)(2,1)}) custom-call(f32[8,128]{1,0:T(8,128)S(1)} %get-tuple-element.221.token_ref, bf16[768,768]{1,0:T(8,128)(2,1)S(1)} %bitcast.20), custom_call_target="tpu_custom_call", output_to_operand_aliasing={{0}: (0, {})} | custom-call | tf_op jit(solution)/shard_map/cond/branch_1_fun/sum_parts/pallas_call | solution.py:52
  188.3 1.1 collective-permute-start.21
  189.4 5.7 %all-to-all-start.1 = ((bf16[8,96,768]{2,1,0:T(8,128)(2,1)}), bf16[8,96,768]{2,1,0:T(8,128)(2,1)S(1)}, u32[]{:S(2)}, u32[]{:S(2)}) async-start(bf16[8,96,768]{2,1,0:T(8,128)(2,1)} %bitcast.10), calls=%async_computation.1 | async-start | bytes 2359296 | tf_op jit(solution)/shard_map/all_to_all | solution.py:676
  195.0 9.2 %all-reduce.4.cloned.1.call-done = (bf16[768,768]{1,0:T(8,128)(2,1)}, bf16[768,768]{1,0:T(8,128)(2,1)}) async-done(((bf16[768,768]{1,0:T(8,128)(2,1)}, bf16[768,768]{1,0:T(8,128)(2,1)}), (bf16[768,768]{1,0:T(8,128)(2,1)}, bf16[768,768]{1,0:T(8,128)(2,1)})) %all-reduce.4.cloned.1.call-update) | async-done | bytes 2359312 | tf_op jit(solution)/shard_map/psum | solution.py:725
  204.2 1.3 copy-done.7
  205.4 1.3 copy-done.8
  206.7 2.5 %widen.1 = (f32[8,128]{1,0:T(8,128)S(1)}, f32[768,768]{1,0:T(8,128)}, f32[768,768]{1,0:T(8,128)}) custom-call(f32[8,128]{1,0:T(8,128)S(1)} %get-tuple-element.350.token_ref, bf16[768,768]{1,0:T(8,128)(2,1)S(1)} %copy-done.7, bf16[768,768]{1,0:T(8,128)(2,1)S(1)} %copy-done.8), custom_call_target="tpu_custom_call", output_to_operand_aliasing={{0}: (0, {})} | custom-call | tf_op jit(solution)/shard_map/widen/pallas_call | solution.py:52
  209.2 3.2 %mix.1 = (f32[8,128]{1,0:T(8,128)S(1)}, bf16[2048,768]{1,0:T(8,128)(2,1)}, bf16[1024,768]{1,0:T(8,128)(2,1)S(1)}) custom-call(f32[8,128]{1,0:T(8,128)S(1)} %get-tuple-element.353.token_ref, f32[512,768]{1,0:T(8,128)S(1)} %copy-done, f32[512,768]{1,0:T(8,128)S(1)} %copy-done.16, ...), custom_call_target="tpu_custom_call", output_to_operand_aliasing={{0}: (0, {})} | custom-call | tf_op jit(solution)/shard_map/mix/pallas_call | solution.py:52
  212.4 3.4 %collective-permute-done.22.refs_1_ = bf16[1024,768]{1,0:T(8,128)(2,1)S(1)} collective-permute-done((bf16[1024,768]{1,0:T(8,128)(2,1)S(1)}, bf16[1024,768]{1,0:T(8,128)(2,1)S(1)}, u32[]{:S(2)}, u32[]{:S(2)}) %collective-permute-start.22) | collective-permute-done | bytes 1572896 | tf_op jit(solution)/shard_map/ppermute | solution.py:670
  215.8 1.7 place.3
  217.5 9.2 %all-to-all-done.1 = bf16[8,96,768]{2,1,0:T(8,128)(2,1)S(1)} async-done(((bf16[8,96,768]{2,1,0:T(8,128)(2,1)}), bf16[8,96,768]{2,1,0:T(8,128)(2,1)S(1)}, u32[]{:S(2)}, u32[]{:S(2)}) %all-to-all-start.1) | async-done | bytes 1179680 | tf_op jit(solution)/shard_map/all_to_all | solution.py:676
  226.7 1.9 widen_attn.1
  (130 shorter events, 3.0 us)
Async XLA Ops:
  7.2 2.6 %copy-start.14 = (bf16[192,768]{1,0:T(8,128)(2,1)S(1)}, bf16[192,768]{1,0:T(8,128)(2,1)}, u32[]{:S(2)}) copy-start(bf16[192,768]{1,0:T(8,128)(2,1)} %refs_5_.3) | copy-start | bytes 884740
  7.2 5.3 %copy-start.37 = (bf16[768]{0:T(1024)(128)(2,1)S(1)}, bf16[768]{0:T(1024)(128)(2,1)}, u32[]{:S(2)}) copy-start(bf16[768]{0:T(1024)(128)(2,1)} %param.23) | copy-start | bytes 4612
  7.2 5.3 %copy-start.38 = (bf16[768]{0:T(1024)(128)(2,1)S(1)}, bf16[768]{0:T(1024)(128)(2,1)}, u32[]{:S(2)}) copy-start(bf16[768]{0:T(1024)(128)(2,1)} %param.20) | copy-start | bytes 4612
  7.2 197.0 %all-reduce.4.cloned.1.call-start = ((), (), s32[]{:S(2)}) async-start(), calls=%async_computation.2 | async-start | bytes 4718592 | tf_op jit(solution)/shard_map/psum | solution.py:725
  7.3 5.4 %copy-start.10 = (s32[4]{0:T(128)S(1)}, s32[4]{0:T(128)}, u32[]{:S(2)}) copy-start(s32[4]{0:T(128)} %refs_0_.5) | copy-start | bytes 52
  7.3 5.4 %copy-start.13 = (s32[512,512]{1,0:T(8,128)S(1)}, s32[512,512]{1,0:T(8,128)}, u32[]{:S(2)}) copy-start(s32[512,512]{1,0:T(8,128)} %refs_6_.1) | copy-start | bytes 3145732
  8.7 4.0 %collective-permute-start.11 = (bf16[784,768]{1,0:T(8,128)(2,1)S(1)}, bf16[784,768]{1,0:T(8,128)(2,1)S(1)}, u32[]{:S(2)}, u32[]{:S(2)}) collective-permute-start(bf16[784,768]{1,0:T(8,128)(2,1)S(1)} %fusion.3.refs_3_), channel_id=1, source_target_pairs={{0,8},{8,0},{1,9},{9,1},{2,10},{10,2},{3,11},{11,3},{4,12},{12,4},... | collective-permute-start | bytes 3612680 | tf_op jit(solution)/shard_map/ppermute | solution.py:670
  9.2 24.0 %collective-permute-start.16 = (bf16[768,768]{1,0:T(8,128)(2,1)}, bf16[768,768]{1,0:T(8,128)(2,1)S(1)}, u32[]{:S(2)}, u32[]{:S(2)}) collective-permute-start(bf16[768,768]{1,0:T(8,128)(2,1)} %refs_9_.3), channel_id=1, source_target_pairs={{0,8},{8,0},{1,9},{9,1},{2,10},{10,2},{3,11},{11,3},{4,12},{12,4},... | collective-permute-start | bytes 3538952 | tf_op jit(solution)/shard_map/ppermute | solution.py:670
  9.3 23.9 %collective-permute-start.17 = (bf16[768,768]{1,0:T(8,128)(2,1)}, bf16[768,768]{1,0:T(8,128)(2,1)S(1)}, u32[]{:S(2)}, u32[]{:S(2)}) collective-permute-start(bf16[768,768]{1,0:T(8,128)(2,1)} %refs_11_.3), channel_id=1, source_target_pairs={{0,8},{8,0},{1,9},{9,1},{2,10},{10,2},{3,11},{11,3},{4,12},{12,4},... | collective-permute-start | bytes 3538952 | tf_op jit(solution)/shard_map/ppermute | solution.py:670
  9.8 14.9 %collective-permute-start.12 = (bf16[192,768]{1,0:T(8,128)(2,1)S(1)}, bf16[192,768]{1,0:T(8,128)(2,1)S(1)}, u32[]{:S(2)}, u32[]{:S(2)}) collective-permute-start(bf16[192,768]{1,0:T(8,128)(2,1)S(1)} %copy-done.14), channel_id=1, source_target_pairs={{0,16},{16,0},{1,17},{17,1},{2,18},{18,2},{3,19},{19,3},{4,20},{20... | collective-permute-start | bytes 884744 | tf_op jit(solution)/shard_map/ppermute | solution.py:673
  12.3 20.8 %collective-permute-start.14 = (bf16[192,768]{1,0:T(8,128)(2,1)S(1)}, bf16[192,768]{1,0:T(8,128)(2,1)S(1)}, u32[]{:S(2)}, u32[]{:S(2)}) collective-permute-start(bf16[192,768]{1,0:T(8,128)(2,1)S(1)} %copy-done.14), channel_id=1, source_target_pairs={{0,8},{8,0},{1,9},{9,1},{2,10},{10,2},{3,11},{11,3},{4,12},{12,4},... | collective-permute-start | bytes 884744 | tf_op jit(solution)/shard_map/ppermute | solution.py:670
  12.7 11.9 %copy-start.11 = (bf16[2048,768]{1,0:T(8,128)(2,1)S(1)}, bf16[2048,768]{1,0:T(8,128)(2,1)}, u32[]{:S(2)}) copy-start(bf16[2048,768]{1,0:T(8,128)(2,1)} %refs_0_.7) | copy-start | bytes 9437188
  21.7 11.3 %copy-start.1 = (bf16[6,512,512]{2,1,0:T(8,128)(2,1)}, bf16[6,512,512]{2,1,0:T(8,128)(2,1)S(1)}, u32[]{:S(2)}) copy-start(bf16[6,512,512]{2,1,0:T(8,128)(2,1)S(1)} %get-tuple-element.332.refs_9_) | copy-start | bytes 9437188
  21.7 11.3 %copy-start.5 = (bf16[512,1152]{1,0:T(8,128)(2,1)}, bf16[512,1152]{1,0:T(8,128)(2,1)S(1)}, u32[]{:S(2)}) copy-start(bf16[512,1152]{1,0:T(8,128)(2,1)S(1)} %get-tuple-element.331.refs_8_) | copy-start | bytes 3538948
  21.7 13.1 %copy-start.12 = (bf16[1152,768]{1,0:T(8,128)(2,1)}, bf16[1152,768]{1,0:T(8,128)(2,1)S(1)}, u32[]{:S(2)}) copy-start(bf16[1152,768]{1,0:T(8,128)(2,1)S(1)} %get-tuple-element.308.refs_3_.refs_7_) | copy-start | bytes 5308420
  21.7 13.1 %copy-start.23 = (bf16[512,384]{1,0:T(8,128)(2,1)}, bf16[512,384]{1,0:T(8,128)(2,1)S(1)}, u32[]{:S(2)}) copy-start(bf16[512,384]{1,0:T(8,128)(2,1)S(1)} %get-tuple-element.311.refs_1_) | copy-start | bytes 1179652
  21.7 13.1 %collective-permute-start.13 = (bf16[512,384]{1,0:T(8,128)(2,1)S(1)}, bf16[512,384]{1,0:T(8,128)(2,1)S(1)}, u32[]{:S(2)}, u32[]{:S(2)}) collective-permute-start(bf16[512,384]{1,0:T(8,128)(2,1)S(1)} %get-tuple-element.311.refs_1_), channel_id=1, source_target_pairs={{0,16},{16,0},{1,17},{17,1},{2,18},{18,2},{3,19},{19,3},{4,20},{20... | collective-permute-start | bytes 1179656 | tf_op jit(solution)/shard_map/ppermute | solution.py:673
  24.6 8.5 %copy-start.3 = (bf16[192,768]{1,0:T(8,128)(2,1)}, bf16[192,768]{1,0:T(8,128)(2,1)S(1)}, u32[]{:S(2)}) copy-start(bf16[192,768]{1,0:T(8,128)(2,1)S(1)} %get-tuple-element.312.refs_5_) | copy-start | bytes 884740
  33.0 21.0 %copy-start.25 = (bf16[512,384]{1,0:T(8,128)(2,1)}, bf16[512,384]{1,0:T(8,128)(2,1)S(1)}, u32[]{:S(2)}) copy-start(bf16[512,384]{1,0:T(8,128)(2,1)S(1)} %get-tuple-element.314.refs_1_) | copy-start | bytes 1179652
  33.0 18.9 %collective-permute-start.18 = (bf16[512,384]{1,0:T(8,128)(2,1)S(1)}, bf16[512,384]{1,0:T(8,128)(2,1)S(1)}, u32[]{:S(2)}, u32[]{:S(2)}) collective-permute-start(bf16[512,384]{1,0:T(8,128)(2,1)S(1)} %get-tuple-element.314.refs_1_), channel_id=1, source_target_pairs={{0,16},{16,0},{1,17},{17,1},{2,18},{18,2},{3,19},{19,3},{4,20},{20... | collective-permute-start | bytes 1179656 | tf_op jit(solution)/shard_map/ppermute | solution.py:673
  33.1 1.6 collective-permute-start.15
  33.2 1.6 copy-start.18
  33.2 1.5 copy-start.19
  34.8 0.8 copy-start.32
  51.9 2.1 copy-start.4
  52.0 20.1 %collective-permute-start.19 = (bf16[512,768]{1,0:T(8,128)(2,1)}, bf16[512,768]{1,0:T(8,128)(2,1)S(1)}, u32[]{:S(2)}, u32[]{:S(2)}) collective-permute-start(bf16[512,768]{1,0:T(8,128)(2,1)} %get-tuple-element.326.refs_1_), channel_id=1, source_target_pairs={{0,16},{16,0},{1,17},{17,1},{2,18},{18,2},{3,19},{19,3},{4,20},{20... | collective-permute-start | bytes 2359304 | tf_op jit(solution)/shard_map/ppermute | solution.py:673
  71.4 0.9 copy-start.22
  72.3 3.1 %collective-permute-start = (bf16[768,768]{1,0:T(8,128)(2,1)}, bf16[768,768]{1,0:T(8,128)(2,1)S(1)}, u32[]{:S(2)}, u32[]{:S(2)}) collective-permute-start(bf16[768,768]{1,0:T(8,128)(2,1)} %get-tuple-element.128), channel_id=1, source_target_pairs={{0,8},{8,0},{1,9},{9,1},{2,10},{10,2},{3,11},{11,3},{4,12},{12,4},... | collective-permute-start | bytes 3538952 | tf_op jit(solution)/shard_map/cond/branch_1_fun/ppermute | solution.py:670
  72.3 4.7 %collective-permute-start.1 = (bf16[768,768]{1,0:T(8,128)(2,1)}, bf16[768,768]{1,0:T(8,128)(2,1)S(1)}, u32[]{:S(2)}, u32[]{:S(2)}) collective-permute-start(bf16[768,768]{1,0:T(8,128)(2,1)} %get-tuple-element.130), channel_id=1, source_target_pairs={{0,8},{8,0},{1,9},{9,1},{2,10},{10,2},{3,11},{11,3},{4,12},{12,4},... | collective-permute-start | bytes 3538952 | tf_op jit(solution)/shard_map/cond/branch_1_fun/ppermute | solution.py:670
  79.9 1.6 copy-start
  79.9 19.9 %collective-permute-start.20 = (bf16[512,768]{1,0:T(8,128)(2,1)}, bf16[512,768]{1,0:T(8,128)(2,1)S(1)}, u32[]{:S(2)}, u32[]{:S(2)}) collective-permute-start(bf16[512,768]{1,0:T(8,128)(2,1)} %copy-done.22), channel_id=1, source_target_pairs={{0,16},{16,0},{1,17},{17,1},{2,18},{18,2},{3,19},{19,3},{4,20},{20... | collective-permute-start | bytes 2359304 | tf_op jit(solution)/shard_map/ppermute | solution.py:673
  81.4 1.9 copy-start.2
  83.3 1.3 copy-start.6
  99.8 0.9 copy-start.21
  100.6 19.5 %collective-permute-start.9 = (bf16[512,768]{1,0:T(8,128)(2,1)}, bf16[512,768]{1,0:T(8,128)(2,1)}, u32[]{:S(2)}, u32[]{:S(2)}) collective-permute-start(bf16[512,768]{1,0:T(8,128)(2,1)} %get-tuple-element.204), channel_id=1, source_target_pairs={{0,16},{16,0},{1,17},{17,1},{2,18},{18,2},{3,19},{19,3},{4,20},{20... | collective-permute-start | bytes 2359304 | tf_op jit(solution)/shard_map/cond/branch_1_fun/ppermute | solution.py:673
  102.1 12.9 %copy-start.24 = (bf16[512,384]{1,0:T(8,128)(2,1)S(1)}, bf16[512,384]{1,0:T(8,128)(2,1)}, u32[]{:S(2)}) copy-start(bf16[512,384]{1,0:T(8,128)(2,1)} %get-tuple-element.149.refs_6_) | copy-start | bytes 1179652 | tf_op jit(solution)/shard_map/cond/branch_1_fun/cond
  102.1 12.9 %copy-start.26 = (bf16[512,384]{1,0:T(8,128)(2,1)S(1)}, bf16[512,384]{1,0:T(8,128)(2,1)}, u32[]{:S(2)}) copy-start(bf16[512,384]{1,0:T(8,128)(2,1)} %get-tuple-element.150.refs_7_) | copy-start | bytes 1179652 | tf_op jit(solution)/shard_map/cond/branch_1_fun/cond
  102.1 12.9 %copy-start.27 = (bf16[512,1152]{1,0:T(8,128)(2,1)S(1)}, bf16[512,1152]{1,0:T(8,128)(2,1)}, u32[]{:S(2)}) copy-start(bf16[512,1152]{1,0:T(8,128)(2,1)} %get-tuple-element.145.refs_2_) | copy-start | bytes 3538948 | tf_op jit(solution)/shard_map/cond/branch_1_fun/cond
  102.1 12.9 %copy-start.29 = (bf16[512,768]{1,0:T(8,128)(2,1)S(1)}, bf16[512,768]{1,0:T(8,128)(2,1)}, u32[]{:S(2)}) copy-start(bf16[512,768]{1,0:T(8,128)(2,1)} %get-tuple-element.143.refs_0_) | copy-start | bytes 2359300 | tf_op jit(solution)/shard_map/cond/branch_1_fun/cond
  102.1 12.9 %copy-start.30 = (bf16[512,768]{1,0:T(8,128)(2,1)S(1)}, bf16[512,768]{1,0:T(8,128)(2,1)}, u32[]{:S(2)}) copy-start(bf16[512,768]{1,0:T(8,128)(2,1)} %get-tuple-element.144.refs_1_) | copy-start | bytes 2359300 | tf_op jit(solution)/shard_map/cond/branch_1_fun/cond
  102.1 12.9 %copy-start.31 = (bf16[512,768]{1,0:T(8,128)(2,1)S(1)}, bf16[512,768]{1,0:T(8,128)(2,1)}, u32[]{:S(2)}) copy-start(bf16[512,768]{1,0:T(8,128)(2,1)} %get-tuple-element.147.refs_4_) | copy-start | bytes 2359300 | tf_op jit(solution)/shard_map/cond/branch_1_fun/cond
  120.2 3.1 %copy-start.20 = (bf16[768,768]{1,0:T(8,128)(2,1)S(1)}, bf16[768,768]{1,0:T(8,128)(2,1)}, u32[]{:S(2)}) copy-start(bf16[768,768]{1,0:T(8,128)(2,1)} %get-tuple-element.207.refs_0_) | copy-start | bytes 3538948 | tf_op jit(solution)/shard_map/cond
  120.2 3.1 %collective-permute-start.10 = (bf16[768,768]{1,0:T(8,128)(2,1)}, bf16[768,768]{1,0:T(8,128)(2,1)S(1)}, u32[]{:S(2)}, u32[]{:S(2)}) collective-permute-start(bf16[768,768]{1,0:T(8,128)(2,1)} %get-tuple-element.208), channel_id=1, source_target_pairs={{0,8},{8,0},{1,9},{9,1},{2,10},{10,2},{3,11},{11,3},{4,12},{12,4},... | collective-permute-start | bytes 3538952 | tf_op jit(solution)/shard_map/cond/branch_1_fun/ppermute | solution.py:670
  123.6 1.0 copy-start.9
  124.7 6.0 %copy-start.15 = (bf16[512,768]{1,0:T(8,128)(2,1)S(1)}, bf16[512,768]{1,0:T(8,128)(2,1)}, u32[]{:S(2)}) copy-start(bf16[512,768]{1,0:T(8,128)(2,1)} %get-tuple-element.210) | copy-start | bytes 2359300 | tf_op jit(solution)/shard_map/cond
  124.7 60.2 %all-to-all-start = ((bf16[8,96,768]{2,1,0:T(8,128)(2,1)}), bf16[8,96,768]{2,1,0:T(8,128)(2,1)S(1)}, u32[]{:S(2)}, u32[]{:S(2)}) async-start(bf16[8,96,768]{2,1,0:T(8,128)(2,1)} %bitcast.21), calls=%async_computation | async-start | bytes 2359296 | tf_op jit(solution)/shard_map/cond/branch_1_fun/all_to_all | solution.py:676
  130.7 19.4 %copy-start.17 = (f32[512,768]{1,0:T(8,128)S(1)}, f32[512,768]{1,0:T(8,128)}, u32[]{:S(2)}) copy-start(f32[512,768]{1,0:T(8,128)} %get-tuple-element.166.refs_3_) | copy-start | bytes 4718596 | tf_op jit(solution)/shard_map/cond/branch_1_fun/cond
  130.7 19.4 %collective-permute-start.2 = (bf16[512,768]{1,0:T(8,128)(2,1)S(1)}, bf16[512,768]{1,0:T(8,128)(2,1)S(1)}, u32[]{:S(2)}, u32[]{:S(2)}) collective-permute-start(bf16[512,768]{1,0:T(8,128)(2,1)S(1)} %get-tuple-element.168.refs_5_), channel_id=1, source_target_pairs={{0,16},{16,0},{1,17},{17,1},{2,18},{18,2},{3,19},{19,3},{4,20},{20... | collective-permute-start | bytes 2359304 | tf_op jit(solution)/shard_map/cond/branch_1_fun/cond/branch_1_fun/ppermute | solution.py:673
  157.0 6.4 %copy-start.33 = (f32[3,2,1024]{2,1,0:T(2,128)S(1)}, f32[3,2,1024]{2,1,0:T(2,128)}, u32[]{:S(2)}) copy-start(f32[3,2,1024]{2,1,0:T(2,128)} %get-tuple-element.175) | copy-start | bytes 73732 | tf_op jit(solution)/shard_map/cond/branch_1_fun/cond
  157.0 6.4 %copy-start.34 = (f32[3,2,1024]{2,1,0:T(2,128)S(1)}, f32[3,2,1024]{2,1,0:T(2,128)}, u32[]{:S(2)}) copy-start(f32[3,2,1024]{2,1,0:T(2,128)} %get-tuple-element.174) | copy-start | bytes 73732 | tf_op jit(solution)/shard_map/cond/branch_1_fun/cond
  157.0 22.3 %collective-permute-start.7 = (f32[1024,768]{1,0:T(8,128)}, f32[1024,768]{1,0:T(8,128)}, u32[]{:S(2)}, u32[]{:S(2)}) collective-permute-start(f32[1024,768]{1,0:T(8,128)} %get-tuple-element.178), channel_id=1, source_target_pairs={{0,8},{8,0},{1,9},{9,1},{2,10},{10,2},{3,11},{11,3},{4,12},{12,4},... | collective-permute-start | bytes 9437192 | tf_op jit(solution)/shard_map/cond/branch_1_fun/cond/branch_1_fun/ppermute | solution.py:670
  157.0 26.5 %collective-permute-start.8 = (bf16[512,768]{1,0:T(8,128)(2,1)}, bf16[512,768]{1,0:T(8,128)(2,1)}, u32[]{:S(2)}, u32[]{:S(2)}) collective-permute-start(bf16[512,768]{1,0:T(8,128)(2,1)} %get-tuple-element.450), channel_id=1, source_target_pairs={{0,16},{16,0},{1,17},{17,1},{2,18},{18,2},{3,19},{19,3},{4,20},{20... | collective-permute-start | bytes 2359304 | tf_op jit(solution)/shard_map/cond/branch_1_fun/cond/branch_1_fun/ppermute | solution.py:673
  158.1 6.4 %copy-start.35 = (f32[1,768]{1,0:T(1,128)S(1)}, f32[1,768]{1,0:T(1,128)}, u32[]{:S(2)}) copy-start(f32[1,768]{1,0:T(1,128)} %get-tuple-element.173) | copy-start | bytes 9220 | tf_op jit(solution)/shard_map/cond/branch_1_fun/cond
  158.1 6.4 %copy-start.36 = (f32[1,768]{1,0:T(1,128)S(1)}, f32[1,768]{1,0:T(1,128)}, u32[]{:S(2)}) copy-start(f32[1,768]{1,0:T(1,128)} %get-tuple-element.172) | copy-start | bytes 9220 | tf_op jit(solution)/shard_map/cond/branch_1_fun/cond
  164.6 1.2 collective-permute-start.3
  165.9 3.7 %collective-permute-start.4 = (f32[1632]{0:T(1024)S(1)}, f32[1632]{0:T(1024)S(1)}, u32[]{:S(2)}, u32[]{:S(2)}) collective-permute-start(f32[1632]{0:T(1024)S(1)} %maximum_add_fusion), channel_id=1, source_target_pairs={{0,1},{1,0},{2,3},{3,2},{4,5},{5,4},{6,7},{7,6},{8,9},{9,8},{10,11... | collective-permute-start | bytes 19592 | tf_op jit(solution)/shard_map/cond/branch_1_fun/cond/branch_1_fun/ppermute | solution.py:778
  169.5 3.7 %collective-permute-start.5 = (f32[1632]{0:T(1024)S(1)}, f32[1632]{0:T(1024)S(1)}, u32[]{:S(2)}, u32[]{:S(2)}) collective-permute-start(f32[1632]{0:T(1024)S(1)} %add.19), channel_id=1, source_target_pairs={{0,2},{1,3},{2,0},{3,1},{4,6},{5,7},{6,4},{7,5},{8,10},{9,11},{10,... | collective-permute-start | bytes 19592 | tf_op jit(solution)/shard_map/cond/branch_1_fun/cond/branch_1_fun/ppermute | solution.py:778
  173.2 4.7 %collective-permute-start.6 = (f32[1632]{0:T(1024)S(1)}, f32[1632]{0:T(1024)S(1)}, u32[]{:S(2)}, u32[]{:S(2)}) collective-permute-start(f32[1632]{0:T(1024)S(1)} %add.20), channel_id=1, source_target_pairs={{0,4},{1,5},{2,6},{3,7},{4,0},{5,1},{6,2},{7,3},{8,12},{9,13},{10,... | collective-permute-start | bytes 19592 | tf_op jit(solution)/shard_map/cond/branch_1_fun/cond/branch_1_fun/ppermute | solution.py:778
  188.3 20.9 %collective-permute-start.21 = (bf16[512,768]{1,0:T(8,128)(2,1)}, bf16[512,768]{1,0:T(8,128)(2,1)S(1)}, u32[]{:S(2)}, u32[]{:S(2)}) collective-permute-start(bf16[512,768]{1,0:T(8,128)(2,1)} %get-tuple-element.355.refs_3_), channel_id=1, source_target_pairs={{0,16},{16,0},{1,17},{17,1},{2,18},{18,2},{3,19},{19,3},{4,20},{20... | collective-permute-start | bytes 2359304 | tf_op jit(solution)/shard_map/ppermute | solution.py:673
  189.4 37.3 %all-to-all-start.1 = ((bf16[8,96,768]{2,1,0:T(8,128)(2,1)}), bf16[8,96,768]{2,1,0:T(8,128)(2,1)S(1)}, u32[]{:S(2)}, u32[]{:S(2)}) async-start(bf16[8,96,768]{2,1,0:T(8,128)(2,1)} %bitcast.10), calls=%async_computation.1 | async-start | bytes 2359296 | tf_op jit(solution)/shard_map/all_to_all | solution.py:676
  204.2 1.3 copy-start.7
  205.4 1.3 copy-start.8
  206.7 2.5 %copy-start.16 = (f32[512,768]{1,0:T(8,128)S(1)}, f32[512,768]{1,0:T(8,128)}, u32[]{:S(2)}) copy-start(f32[512,768]{1,0:T(8,128)} %get-tuple-element.336.refs_1_) | copy-start | bytes 4718596
  212.4 3.4 %collective-permute-start.22 = (bf16[1024,768]{1,0:T(8,128)(2,1)S(1)}, bf16[1024,768]{1,0:T(8,128)(2,1)S(1)}, u32[]{:S(2)}, u32[]{:S(2)}) collective-permute-start(bf16[1024,768]{1,0:T(8,128)(2,1)S(1)} %get-tuple-element.359), channel_id=1, source_target_pairs={{0,8},{8,0},{1,9},{9,1},{2,10},{10,2},{3,11},{11,3},{4,12},{12,4},... | collective-permute-start | bytes 4718600 | tf_op jit(solution)/shard_map/ppermute | solution.py:670
  (1 other events, 0.7 us)
Sparse Core Ops, SparseCore 0:
  80.0 124.1 all-reduce.3

commit v5 on v4

--- a/solution.py
+++ b/solution.py
@@ -779,20 +779,21 @@
             grad_gain_attn, grad_gain_ffn = small[:width], small[width : 2 * width]
             grad_table = small[2 * width :].reshape(heads, table_rows).T
             ids = need(ids, grad_gain_attn, grad_gain_ffn, grad_table)
-            (gsrc,), ids = place(ids, gsrc, from_core(gsrc_send))
-            ids = need(ids, *hoth)
-            return ids, gsrc, (grad_gain_attn, grad_gain_ffn, grad_table), sent, hoth
-
-        ids, gsrc, smalls, hsent, hoth = region(always, rows_back, ids)
+            gsrc_got = from_core(gsrc_send)
+            ids = need(ids, gsrc_got, *hoth)
+            return ids, gsrc, gsrc_got, (grad_gain_attn, grad_gain_ffn, grad_table), sent, hoth
+
+        ids, gsrc, gsrc_got, smalls, hsent, hoth = region(always, rows_back, ids)
         (gattn,), ids = sum_parts(ids, gattn, dp)
-        return ids, gattn, gsrc, smalls, hsent, hoth
-
-    ids, gattn, gsrc, smalls, hsent, hoth = region(always, attention_back, ids)
+        return ids, gattn, gsrc, gsrc_got, smalls, hsent, hoth
+
+    ids, gattn, gsrc, gsrc_got, smalls, hsent, hoth = region(always, attention_back, ids)
     grad_gain_attn, grad_gain_ffn, grad_table = smalls
     for doc in range(docs // 2, docs):
         (hsent[doc],), ids = gate(ids, hsent[doc])
         hoth.append(from_x(hsent[doc]))
     gattn = spread(gattn)
+    (gsrc,), ids = place(ids, gsrc, gsrc_got)
     (grad_w_back, grad_w_in), ids = widen(ids, gback, gin)
     (mixed, mixed_send), ids = mix(ids, middle, hsent, hoth, docs)
     mixed_got = from_core(mixed_send)

time: 236 us -> 236 us (level)
    all_to_all x2, waiting for transfers between devices: 9.18 us -> 4.38 us  [spread(): return lax.all_to_all(v, 'dp', 0, 0, tiled=True)]
    psum x1, waiting for transfers between devices: 9.15 us -> 13.8 us  [per_device(): gback, gin = lax.psum((gback, gin), 'dp')]
    cond x32 -> x28, local copies, waits for them, and re-layouts: 5.43 us -> 5.39 us
    unnamed x48 -> x50, local copies, waits for them, and re-layouts: 6.84 us -> 6.82 us
where the time goes in v5:
time: 236 us; the launch traced here: 235 us
  Pallas kernels  107 us (45%)
  waiting for transfers between devices  58.3 us (25%)
  starting transfers between devices  32.8 us (14%)
  local copies, waits for them, and re-layouts  19 us (8%)
  between operations  14.4 us (6%)
    pallas_call x30, Pallas kernels, call(): pl.pallas_call(body, grid=grid, in_specs=[anywhere] + list(in_specs), out...  107 us
    ppermute x9, waiting for transfers between devices, from_x(): return lax.ppermute(v, 'x', [(0, 1), (1, 0)])  22.8 us
    psum x1, waiting for transfers between devices, per_device(): gback, gin = lax.psum((gback, gin), 'dp')  13.8 us
    ppermute x9, starting transfers between devices, from_x(): return lax.ppermute(v, 'x', [(0, 1), (1, 0)])  13.4 us
    ppermute x11, waiting for transfers between devices, from_core(): return lax.ppermute(v, 'core', [(0, 1), (1, 0)])  13.1 us
    all_to_all x2, starting transfers between devices, spread(): return lax.all_to_all(v, 'dp', 0, 0, tiled=True)  11.5 us
    unnamed x50, local copies, waits for them, and re-layouts  6.82 us
    ppermute x3, starting transfers between devices, rows_back(): lax.ppermute(small, 'dp', [(i, i ^ 1 << s) for i in range(dp)])  5.84 us
  transfers between devices with their start and end apart: 26, of which 15 were waited for; matrix products, arithmetic and copies ran while one was open for 5% of the time, Pallas kernels for 44%

profile of v5, /device:TPU:0, one launch (start us, length us, event | category | flops | bytes accessed | tf_op | source)
XLA Modules:
  0.0 234.8 jit_solution(8379705318370433218)
XLA Ops:
  7.3 1.4 fusion.3.refs_3_
  8.7 0.5 collective-permute-start.11
  9.7 2.6 %collective-permute-start.12 = (bf16[192,768]{1,0:T(8,128)(2,1)}, bf16[192,768]{1,0:T(8,128)(2,1)S(1)}, u32[]{:S(2)}, u32[]{:S(2)}) collective-permute-start(bf16[192,768]{1,0:T(8,128)(2,1)} %refs_5_.3), channel_id=1, source_target_pairs={{0,16},{16,0},{1,17},{17,1},{2,18},{18,2},{3,19},{19,3},{4,20},{20... | collective-permute-start | bytes 884744 | tf_op jit(solution)/shard_map/ppermute | solution.py:673
  12.7 9.0 %attn_fwd.2 = (f32[8,128]{1,0:T(8,128)S(1)}, bf16[1152,768]{1,0:T(8,128)(2,1)S(1)}, f32[6,1024]{1,0:T(8,128)S(1)}, bf16[512,768]{1,0:T(8,128)(2,1)}, bf16[512,11...) custom-call(f32[8,128]{1,0:T(8,128)S(1)} %broadcast_43_token_ref.2.t, ...), custom_call_target="tpu_custom_call", output_to_operand_aliasing={{0}: (0, {})} | custom-call | tf_op jit(solution)/shard_map/attn_fwd/pallas_call | solution.py:52
  21.7 2.9 %collective-permute-start.13 = (bf16[512,384]{1,0:T(8,128)(2,1)S(1)}, bf16[512,384]{1,0:T(8,128)(2,1)S(1)}, u32[]{:S(2)}, u32[]{:S(2)}) collective-permute-start(bf16[512,384]{1,0:T(8,128)(2,1)S(1)} %get-tuple-element.313.refs_1_), channel_id=1, source_target_pairs={{0,16},{16,0},{1,17},{17,1},{2,18},{18,2},{3,19},{19,3},{4,20},{20... | collective-permute-start | bytes 1179656 | tf_op jit(solution)/shard_map/ppermute | solution.py:673
  24.7 8.2 %attn_fwd.3 = (f32[8,128]{1,0:T(8,128)S(1)}, bf16[512,768]{1,0:T(8,128)(2,1)}, bf16[512,1152]{1,0:T(8,128)(2,1)}, bf16[6,512,512]{2,1,0:T(8,128)(2,1)}, bf16[512,384]{1,0:T(8,128)(2,1)}) custom-call(f32[8,128]{1,0:T(8,128)S(1)} %get-tuple-element.309.token_ref, s32[4]{0:T(128)S(1)} %copy-done.10, ...), custom_call_target="tpu_custom_call", output_to_operand_aliasing={{0}: (0, {})} | custom-call | tf_op jit(solution)/shard_map/attn_fwd/pallas_call | solution.py:52
  33.2 1.5 collective-permute-done.15.refs_6_
  34.8 0.8 copy-done.31
  35.5 16.3 %ffn.2 = (f32[8,128]{1,0:T(8,128)S(1)}, f32[512,768]{1,0:T(8,128)}, bf16[512,768]{1,0:T(8,128)(2,1)}, bf16[512,768]{1,0:T(8,128)(2,1)}, bf16[768,768]{1,0:T(8,12...) custom-call(f32[8,128]{1,0:T(8,128)S(1)} %get-tuple-element.312.toke, ...), custom_call_target="tpu_custom_call", output_to_operand_aliasing={{0}: (0, {})} | custom-call | tf_op jit(solution)/shard_map/ffn/pallas_call | solution.py:52
  51.9 2.0 collective-permute-start.19
  54.0 17.5 %ffn.3 = (f32[8,128]{1,0:T(8,128)S(1)}, f32[512,768]{1,0:T(8,128)}, bf16[512,768]{1,0:T(8,128)(2,1)S(1)}, bf16[512,768]{1,0:T(8,128)(2,1)}, bf16[768,768]{1,0:T(...) custom-call(f32[8,128]{1,0:T(8,128)S(1)} %get-tuple-element.318.toke, ...), custom_call_target="tpu_custom_call", output_to_operand_aliasing={{0}: (0, {})} | custom-call | tf_op jit(solution)/shard_map/ffn/pallas_call | solution.py:52
  71.4 0.6 collective-permute-done.19.refs_0_.refs_2_
  72.3 7.4 %conditional.4 = ((f32[8,128]{1,0:T(8,128)S(1)}, bf16[768,768]{1,0:T(8,128)(2,1)}, bf16[768,768]{1,0:T(8,128)(2,1)})) conditional(s32[]{:T(128)} %convert_element_type.14, () %tuple.40, (bf16[768,768]{1,0:T(8,128)(2,1)}, bf16[768,768]{1,0:T(8,128)(2,1)}, f32[8,128]{1,0:T(8,128)S(1)}, bf16[768,768]{1,0:T(8,128)(2,1)S(1)}, ...), branch_computations={%region_0.1_spmd, %region_1.2_spmd} | conditional | bytes 9437272 | solution.py:658
  72.3 0.5 collective-permute-start.1
  72.8 2.5 %collective-permute-done.refs_1_ = bf16[768,768]{1,0:T(8,128)(2,1)S(1)} collective-permute-done((bf16[768,768]{1,0:T(8,128)(2,1)}, bf16[768,768]{1,0:T(8,128)(2,1)S(1)}, u32[]{:S(2)}, u32[]{:S(2)}) %collective-permute-start) | collective-permute-done | bytes 1179680 | tf_op jit(solution)/shard_map/cond/branch_1_fun/ppermute | solution.py:670
  75.4 1.7 collective-permute-done.1.refs_3_
  77.1 2.7 %sum_core.2 = (f32[8,128]{1,0:T(8,128)S(1)}, bf16[768,768]{1,0:T(8,128)(2,1)}, bf16[768,768]{1,0:T(8,128)(2,1)}) custom-call(f32[8,128]{1,0:T(8,128)S(1)} %get-tuple-element.126.token_ref, bf16[768,768]{1,0:T(8,128)(2,1)S(1)} %get-tuple-element.127.refs_0_, bf16[768,768]{1,0:T(8,128)(2,1)S(1)} %collective-permute-done.refs_1_, ...), custom_call_target="tpu_custom_call", output_to_operand_aliasing={{0}: (0, {})} | custom-call | tf_op jit(solution)/shard_map/cond/branch_1_fun/sum_core/pallas_call | solution.py:52
  79.8 1.6 collective-permute-start.20
  81.3 1.9 copy-done.2
  83.2 1.3 copy-done.6
  84.5 11.7 %attn_bwd.3 = (f32[8,128]{1,0:T(8,128)S(1)}, f32[512,768]{1,0:T(8,128)}, bf16[512,768]{1,0:T(8,128)(2,1)}, f32[1,768]{1,0:T(1,128)}, bf16[512,1152]{1,0:T(8,128)...) custom-call(f32[8,128]{1,0:T(8,128)S(1)} %get-tuple-element.331.token_ref, ...), custom_call_target="tpu_custom_call", output_to_operand_aliasing={{0}: (0, {})} | custom-call | tf_op jit(solution)/shard_map/attn_bwd/pallas_call | solution.py:52
  96.2 3.4 %collective-permute-done.20.refs_0_ = bf16[512,768]{1,0:T(8,128)(2,1)S(1)} collective-permute-done((bf16[512,768]{1,0:T(8,128)(2,1)}, bf16[512,768]{1,0:T(8,128)(2,1)S(1)}, u32[]{:S(2)}, u32[]{:S(2)}) %collective-permute-start.20) | collective-permute-done | bytes 786464 | tf_op jit(solution)/shard_map/ppermute | solution.py:673
  99.6 83.7 %conditional.5 = (f32[8,128]{1,0:T(8,128)S(1)}, bf16[768,768]{1,0:T(8,128)(2,1)}, f32[2048,768]{1,0:T(8,128)}, f32[1024,768]{1,0:T(8,128)}, f32[768]{0:T(1024)},...) conditional(s32[]{:T(128)} %convert_element_type.14, () %tuple.39, ...), branch_computations={%region_2.3_spmd, %region_3.8_spmd} | conditional | flops 2414081 | bytes 69171408 | solution.py:658
  99.6 1.5 collective-permute-start.9
  101.1 19.1 %conditional = (f32[8,128]{1,0:T(8,128)S(1)}, f32[512,768]{1,0:T(8,128)}, f32[1,768]{1,0:T(1,128)}, bf16[512,768]{1,0:T(8,128)(2,1)S(1)}, f32[3,2,1024]{2,1,0:T(...) conditional(s32[]{:T(128)} %convert_element_type.1, () %tuple.29, (f32[8,128]{1,0:T(8,128)S(1)}, ...), branch_computations={%region_4.4_spmd, %region_5.5_spmd} | conditional | bytes 18874592 | solution.py:658
  101.1 0.9 copy-done.22
  102.0 12.7 %attn_bwd.2 = (f32[8,128]{1,0:T(8,128)S(1)}, f32[512,768]{1,0:T(8,128)}, bf16[512,768]{1,0:T(8,128)(2,1)S(1)}, f32[1,768]{1,0:T(1,128)}, bf16[512,1152]{1,0:T(8,...) custom-call(f32[8,128]{1,0:T(8,128)S(1)} %get-tuple-element.131.token_ref, ...), custom_call_target="tpu_custom_call", output_to_operand_aliasing={{0}: (0, {})} | custom-call | tf_op jit(solution)/shard_map/cond/branch_1_fun/cond/branch_1_fun/attn_bwd/pallas_call | solution.py:52
  114.8 5.4 %grad_attn.1 = (f32[8,128]{1,0:T(8,128)S(1)}, bf16[768,768]{1,0:T(8,128)(2,1)}, bf16[768,768]{1,0:T(8,128)(2,1)S(1)}) custom-call(f32[8,128]{1,0:T(8,128)S(1)} %get-tuple-element.142.token_ref, bf16[512,768]{1,0:T(8,128)(2,1)S(1)} %copy-done.28, bf16[512,768]{1,0:T(8,128)(2,1)S(1)} %copy-done.29, ...), custom_call_target="tpu_custom_call", output_to_operand_aliasing={{0}: (0, {})} | custom-call | tf_op jit(solution)/shard_map/cond/branch_1_fun/cond/branch_1_fun/grad_attn/pallas_call | solution.py:52
  120.3 2.8 %collective-permute-done.10.refs_1_ = bf16[768,768]{1,0:T(8,128)(2,1)S(1)} collective-permute-done((bf16[768,768]{1,0:T(8,128)(2,1)S(1)}, bf16[768,768]{1,0:T(8,128)(2,1)S(1)}, u32[]{:S(2)}, u32[]{:S(2)}) %collective-permute-start.10) | collective-permute-done | bytes 1179680 | tf_op jit(solution)/shard_map/cond/branch_1_fun/ppermute | solution.py:670
  123.4 1.0 copy-done.9
  124.4 5.8 %all-to-all-start = ((bf16[8,96,768]{2,1,0:T(8,128)(2,1)}), bf16[8,96,768]{2,1,0:T(8,128)(2,1)S(1)}, u32[]{:S(2)}, u32[]{:S(2)}) async-start(bf16[8,96,768]{2,1,0:T(8,128)(2,1)} %bitcast.21), calls=%async_computation | async-start | bytes 2359296 | tf_op jit(solution)/shard_map/cond/branch_1_fun/all_to_all | solution.py:676
  130.3 48.2 %conditional.1 = (f32[8,128]{1,0:T(8,128)S(1)}, f32[2048,768]{1,0:T(8,128)}, f32[1024,768]{1,0:T(8,128)}, f32[768]{0:T(1024)}, f32[768]{0:T(1024)}, /*index=5*/f...) conditional(s32[]{:T(128)} %convert_element_type.1, () %tuple.28, ...), branch_computations={%region_6.6_spmd, %region_7.7_spmd} | conditional | flops 2414080 | bytes 29455088 | solution.py:658
  130.3 0.6 collective-permute-start.2
  130.9 18.7 %collective-permute-done.2.refs_7_ = bf16[512,768]{1,0:T(8,128)(2,1)S(1)} collective-permute-done((bf16[512,768]{1,0:T(8,128)(2,1)S(1)}, bf16[512,768]{1,0:T(8,128)(2,1)S(1)}, u32[]{:S(2)}, u32[]{:S(2)}) %collective-permute-start.2) | collective-permute-done | bytes 786464 | tf_op jit(solution)/shard_map/cond/branch_1_fun/cond/branch_1_fun/ppermute | solution.py:673
  149.6 6.9 %grad_input.1 = (f32[8,128]{1,0:T(8,128)S(1)}, f32[2048,768]{1,0:T(8,128)}, f32[1024,768]{1,0:T(8,128)}, f32[1,768]{1,0:T(1,128)S(1)}) custom-call(f32[8,128]{1,0:T(8,128)S(1)} %get-tuple-element.162.token_ref, bf16[2048,768]{1,0:T(8,128)(2,1)} %get-tuple-element.163.refs_0_, ...), custom_call_target="tpu_custom_call", output_to_operand_aliasing={{0}: (0, {})} | custom-call | tf_op jit(solution)/shard_map/cond/branch_1_fun/cond/branch_1_fun/grad_input/pallas_call | solution.py:52
  156.5 0.7 collective-permute-start.8
  157.2 2.6 %copy.65 = s32[512,512]{0,1:T(8,128)} copy(s32[512,512]{1,0:T(8,128)} %get-tuple-element.420) | data formatting | bytes 2097152 | tf_op jit(solution)/shard_map
  159.8 1.2 slice.39
  161.0 0.7 slice.40
  161.7 0.7 slice.38
  162.5 0.7 pad_add_fusion
  164.0 0.9 collective-permute-done.3
  165.0 1.6 collective-permute-start.4
  166.6 2.0 collective-permute-done.4
  168.6 1.6 collective-permute-start.5
  170.3 2.0 collective-permute-done.5
  172.3 2.5 %collective-permute-start.6 = (f32[1632]{0:T(1024)S(1)}, f32[1632]{0:T(1024)S(1)}, u32[]{:S(2)}, u32[]{:S(2)}) collective-permute-start(f32[1632]{0:T(1024)S(1)} %add.20), channel_id=1, source_target_pairs={{0,4},{1,5},{2,6},{3,7},{4,0},{5,1},{6,2},{7,3},{8,12},{9,13},{10,... | collective-permute-start | bytes 19592 | tf_op jit(solution)/shard_map/cond/branch_1_fun/cond/branch_1_fun/ppermute | solution.py:778
  174.9 2.1 copy.113
  177.2 0.7 copy.62
  177.9 0.6 fusion.4
  178.5 1.4 copy.67
  179.9 3.4 %sum_parts.1 = (f32[8,128]{1,0:T(8,128)S(1)}, bf16[768,768]{1,0:T(8,128)(2,1)}) custom-call(f32[8,128]{1,0:T(8,128)S(1)} %get-tuple-element.219.token_ref, bf16[768,768]{1,0:T(8,128)(2,1)S(1)} %bitcast.20), custom_call_target="tpu_custom_call", output_to_operand_aliasing={{0}: (0, {})} | custom-call | tf_op jit(solution)/shard_map/cond/branch_1_fun/sum_parts/pallas_call | solution.py:52
  183.3 1.4 collective-permute-start.21
  184.6 5.7 %all-to-all-start.1 = ((bf16[8,96,768]{2,1,0:T(8,128)(2,1)}), bf16[8,96,768]{2,1,0:T(8,128)(2,1)S(1)}, u32[]{:S(2)}, u32[]{:S(2)}) async-start(bf16[8,96,768]{2,1,0:T(8,128)(2,1)} %bitcast.23), calls=%async_computation.1 | async-start | bytes 2359296 | tf_op jit(solution)/shard_map/all_to_all | solution.py:676
  190.3 4.2 %place.2 = (f32[8,128]{1,0:T(8,128)S(1)}, f32[2048,768]{1,0:T(8,128)}) custom-call(f32[8,128]{1,0:T(8,128)S(1)} %get-tuple-element.352.token_ref, f32[2048,768]{1,0:T(8,128)} %get-tuple-element.353.refs_0_, f32[1024,768]{1,0:T(8,128)} %get-tuple-element.354.refs_1_), custom_call_target="tpu_custom_call", output_to_operand_aliasing={{0}: (0, {}), {1}: (1, {})} | custom-call | tf_op jit(solution)/shard_map/place/pallas_call | solution.py:52
  194.5 13.8 %all-reduce.4.cloned.1.call-done = (bf16[768,768]{1,0:T(8,128)(2,1)}, bf16[768,768]{1,0:T(8,128)(2,1)}) async-done(((bf16[768,768]{1,0:T(8,128)(2,1)}, bf16[768,768]{1,0:T(8,128)(2,1)}), (bf16[768,768]{1,0:T(8,128)(2,1)}, bf16[768,768]{1,0:T(8,128)(2,1)})) %all-reduce.4.cloned.1.call-update) | async-done | bytes 2359312 | tf_op jit(solution)/shard_map/psum | solution.py:725
  208.3 1.3 copy-done.7
  209.6 1.3 copy-done.8
  210.9 2.5 %widen.1 = (f32[8,128]{1,0:T(8,128)S(1)}, f32[768,768]{1,0:T(8,128)}, f32[768,768]{1,0:T(8,128)}) custom-call(f32[8,128]{1,0:T(8,128)S(1)} %get-tuple-element.355.token_ref, bf16[768,768]{1,0:T(8,128)(2,1)S(1)} %copy-done.7, bf16[768,768]{1,0:T(8,128)(2,1)S(1)} %copy-done.8), custom_call_target="tpu_custom_call", output_to_operand_aliasing={{0}: (0, {})} | custom-call | tf_op jit(solution)/shard_map/widen/pallas_call | solution.py:52
  213.4 3.2 %mix.1 = (f32[8,128]{1,0:T(8,128)S(1)}, bf16[2048,768]{1,0:T(8,128)(2,1)}, bf16[1024,768]{1,0:T(8,128)(2,1)S(1)}) custom-call(f32[8,128]{1,0:T(8,128)S(1)} %get-tuple-element.358.token_ref, f32[512,768]{1,0:T(8,128)S(1)} %copy-done, f32[512,768]{1,0:T(8,128)S(1)} %copy-done.15, ...), custom_call_target="tpu_custom_call", output_to_operand_aliasing={{0}: (0, {})} | custom-call | tf_op jit(solution)/shard_map/mix/pallas_call | solution.py:52
  216.6 3.4 %collective-permute-done.22.refs_1_ = bf16[1024,768]{1,0:T(8,128)(2,1)S(1)} collective-permute-done((bf16[1024,768]{1,0:T(8,128)(2,1)S(1)}, bf16[1024,768]{1,0:T(8,128)(2,1)S(1)}, u32[]{:S(2)}, u32[]{:S(2)}) %collective-permute-start.22) | collective-permute-done | bytes 1572896 | tf_op jit(solution)/shard_map/ppermute | solution.py:670
  220.0 1.7 place.3
  221.7 4.4 %all-to-all-done.1 = bf16[8,96,768]{2,1,0:T(8,128)(2,1)S(1)} async-done(((bf16[8,96,768]{2,1,0:T(8,128)(2,1)}), bf16[8,96,768]{2,1,0:T(8,128)(2,1)S(1)}, u32[]{:S(2)}, u32[]{:S(2)}) %all-to-all-start.1) | async-done | bytes 1179680 | tf_op jit(solution)/shard_map/all_to_all | solution.py:676
  226.1 1.9 widen_attn.1
  (128 shorter events, 3.0 us)
Async XLA Ops:
  7.2 5.3 %copy-start.36 = (bf16[768]{0:T(1024)(128)(2,1)S(1)}, bf16[768]{0:T(1024)(128)(2,1)}, u32[]{:S(2)}) copy-start(bf16[768]{0:T(1024)(128)(2,1)} %param.20) | copy-start | bytes 4612
  7.2 5.3 %copy-start.37 = (bf16[768]{0:T(1024)(128)(2,1)S(1)}, bf16[768]{0:T(1024)(128)(2,1)}, u32[]{:S(2)}) copy-start(bf16[768]{0:T(1024)(128)(2,1)} %param.23) | copy-start | bytes 4612
  7.2 201.1 %all-reduce.4.cloned.1.call-start = ((), (), s32[]{:S(2)}) async-start(), calls=%async_computation.2 | async-start | bytes 4718592 | tf_op jit(solution)/shard_map/psum | solution.py:725
  7.2 5.4 %copy-start.10 = (s32[4]{0:T(128)S(1)}, s32[4]{0:T(128)}, u32[]{:S(2)}) copy-start(s32[4]{0:T(128)} %refs_0_.5) | copy-start | bytes 52
  7.3 5.4 %copy-start.14 = (s32[512,512]{1,0:T(8,128)S(1)}, s32[512,512]{1,0:T(8,128)}, u32[]{:S(2)}) copy-start(s32[512,512]{1,0:T(8,128)} %refs_6_.1) | copy-start | bytes 3145732
  8.7 4.0 %collective-permute-start.11 = (bf16[784,768]{1,0:T(8,128)(2,1)S(1)}, bf16[784,768]{1,0:T(8,128)(2,1)S(1)}, u32[]{:S(2)}, u32[]{:S(2)}) collective-permute-start(bf16[784,768]{1,0:T(8,128)(2,1)S(1)} %fusion.3.refs_3_), channel_id=1, source_target_pairs={{0,8},{8,0},{1,9},{9,1},{2,10},{10,2},{3,11},{11,3},{4,12},{12,4},... | collective-permute-start | bytes 3612680 | tf_op jit(solution)/shard_map/ppermute | solution.py:670
  9.2 23.9 %collective-permute-start.16 = (bf16[768,768]{1,0:T(8,128)(2,1)}, bf16[768,768]{1,0:T(8,128)(2,1)S(1)}, u32[]{:S(2)}, u32[]{:S(2)}) collective-permute-start(bf16[768,768]{1,0:T(8,128)(2,1)} %refs_9_.3), channel_id=1, source_target_pairs={{0,8},{8,0},{1,9},{9,1},{2,10},{10,2},{3,11},{11,3},{4,12},{12,4},... | collective-permute-start | bytes 3538952 | tf_op jit(solution)/shard_map/ppermute | solution.py:670
  9.3 23.9 %collective-permute-start.17 = (bf16[768,768]{1,0:T(8,128)(2,1)}, bf16[768,768]{1,0:T(8,128)(2,1)S(1)}, u32[]{:S(2)}, u32[]{:S(2)}) collective-permute-start(bf16[768,768]{1,0:T(8,128)(2,1)} %refs_11_.3), channel_id=1, source_target_pairs={{0,8},{8,0},{1,9},{9,1},{2,10},{10,2},{3,11},{11,3},{4,12},{12,4},... | collective-permute-start | bytes 3538952 | tf_op jit(solution)/shard_map/ppermute | solution.py:670
  9.7 14.9 %collective-permute-start.12 = (bf16[192,768]{1,0:T(8,128)(2,1)}, bf16[192,768]{1,0:T(8,128)(2,1)S(1)}, u32[]{:S(2)}, u32[]{:S(2)}) collective-permute-start(bf16[192,768]{1,0:T(8,128)(2,1)} %refs_5_.3), channel_id=1, source_target_pairs={{0,16},{16,0},{1,17},{17,1},{2,18},{18,2},{3,19},{19,3},{4,20},{20... | collective-permute-start | bytes 884744 | tf_op jit(solution)/shard_map/ppermute | solution.py:673
  12.3 20.7 %collective-permute-start.14 = (bf16[192,768]{1,0:T(8,128)(2,1)}, bf16[192,768]{1,0:T(8,128)(2,1)S(1)}, u32[]{:S(2)}, u32[]{:S(2)}) collective-permute-start(bf16[192,768]{1,0:T(8,128)(2,1)} %refs_5_.3), channel_id=1, source_target_pairs={{0,8},{8,0},{1,9},{9,1},{2,10},{10,2},{3,11},{11,3},{4,12},{12,4},... | collective-permute-start | bytes 884744 | tf_op jit(solution)/shard_map/ppermute | solution.py:670
  12.7 12.0 %copy-start.11 = (bf16[2048,768]{1,0:T(8,128)(2,1)S(1)}, bf16[2048,768]{1,0:T(8,128)(2,1)}, u32[]{:S(2)}) copy-start(bf16[2048,768]{1,0:T(8,128)(2,1)} %refs_0_.7) | copy-start | bytes 9437188
  21.7 11.2 %copy-start.1 = (bf16[6,512,512]{2,1,0:T(8,128)(2,1)}, bf16[6,512,512]{2,1,0:T(8,128)(2,1)S(1)}, u32[]{:S(2)}) copy-start(bf16[6,512,512]{2,1,0:T(8,128)(2,1)S(1)} %get-tuple-element.334.refs_9_) | copy-start | bytes 9437188
  21.7 11.2 %copy-start.5 = (bf16[512,1152]{1,0:T(8,128)(2,1)}, bf16[512,1152]{1,0:T(8,128)(2,1)S(1)}, u32[]{:S(2)}) copy-start(bf16[512,1152]{1,0:T(8,128)(2,1)S(1)} %get-tuple-element.333.refs_8_) | copy-start | bytes 3538948
  21.7 11.2 %copy-start.24 = (bf16[512,384]{1,0:T(8,128)(2,1)}, bf16[512,384]{1,0:T(8,128)(2,1)S(1)}, u32[]{:S(2)}) copy-start(bf16[512,384]{1,0:T(8,128)(2,1)S(1)} %get-tuple-element.313.refs_1_) | copy-start | bytes 1179652
  21.7 13.0 %copy-start.13 = (bf16[1152,768]{1,0:T(8,128)(2,1)}, bf16[1152,768]{1,0:T(8,128)(2,1)S(1)}, u32[]{:S(2)}) copy-start(bf16[1152,768]{1,0:T(8,128)(2,1)S(1)} %get-tuple-element.310.refs_3_.refs_7_) | copy-start | bytes 5308420
  21.7 13.0 %collective-permute-start.13 = (bf16[512,384]{1,0:T(8,128)(2,1)S(1)}, bf16[512,384]{1,0:T(8,128)(2,1)S(1)}, u32[]{:S(2)}, u32[]{:S(2)}) collective-permute-start(bf16[512,384]{1,0:T(8,128)(2,1)S(1)} %get-tuple-element.313.refs_1_), channel_id=1, source_target_pairs={{0,16},{16,0},{1,17},{17,1},{2,18},{18,2},{3,19},{19,3},{4,20},{20... | collective-permute-start | bytes 1179656 | tf_op jit(solution)/shard_map/ppermute | solution.py:673
  24.7 8.4 %copy-start.3 = (bf16[192,768]{1,0:T(8,128)(2,1)}, bf16[192,768]{1,0:T(8,128)(2,1)S(1)}, u32[]{:S(2)}) copy-start(bf16[192,768]{1,0:T(8,128)(2,1)S(1)} %get-tuple-element.314.refs_5_) | copy-start | bytes 884740
  24.7 10.9 %copy-start.12 = (bf16[2048,768]{1,0:T(8,128)(2,1)S(1)}, bf16[2048,768]{1,0:T(8,128)(2,1)}, u32[]{:S(2)}) copy-start(bf16[2048,768]{1,0:T(8,128)(2,1)} %refs_4_.1) | copy-start | bytes 9437188
  32.9 18.9 %collective-permute-start.18 = (bf16[512,384]{1,0:T(8,128)(2,1)}, bf16[512,384]{1,0:T(8,128)(2,1)S(1)}, u32[]{:S(2)}, u32[]{:S(2)}) collective-permute-start(bf16[512,384]{1,0:T(8,128)(2,1)} %get-tuple-element.316.refs_1_), channel_id=1, source_target_pairs={{0,16},{16,0},{1,17},{17,1},{2,18},{18,2},{3,19},{19,3},{4,20},{20... | collective-permute-start | bytes 1179656 | tf_op jit(solution)/shard_map/ppermute | solution.py:673
  33.1 1.7 copy-start.20
  33.1 1.6 collective-permute-start.15
  33.1 1.6 copy-start.17
  33.2 1.6 copy-start.18
  34.7 0.8 copy-start.27
  34.7 0.8 copy-start.31
  51.8 2.1 copy-start.21
  51.8 2.1 copy-start.4
  51.9 20.2 %collective-permute-start.19 = (bf16[512,768]{1,0:T(8,128)(2,1)}, bf16[512,768]{1,0:T(8,128)(2,1)S(1)}, u32[]{:S(2)}, u32[]{:S(2)}) collective-permute-start(bf16[512,768]{1,0:T(8,128)(2,1)} %get-tuple-element.328.refs_1_), channel_id=1, source_target_pairs={{0,16},{16,0},{1,17},{17,1},{2,18},{18,2},{3,19},{19,3},{4,20},{20... | collective-permute-start | bytes 2359304 | tf_op jit(solution)/shard_map/ppermute | solution.py:673
  71.4 0.9 copy-start.23
  72.3 3.1 %collective-permute-start = (bf16[768,768]{1,0:T(8,128)(2,1)}, bf16[768,768]{1,0:T(8,128)(2,1)S(1)}, u32[]{:S(2)}, u32[]{:S(2)}) collective-permute-start(bf16[768,768]{1,0:T(8,128)(2,1)} %get-tuple-element.128), channel_id=1, source_target_pairs={{0,8},{8,0},{1,9},{9,1},{2,10},{10,2},{3,11},{11,3},{4,12},{12,4},... | collective-permute-start | bytes 3538952 | tf_op jit(solution)/shard_map/cond/branch_1_fun/ppermute | solution.py:670
  72.3 4.7 %collective-permute-start.1 = (bf16[768,768]{1,0:T(8,128)(2,1)}, bf16[768,768]{1,0:T(8,128)(2,1)S(1)}, u32[]{:S(2)}, u32[]{:S(2)}) collective-permute-start(bf16[768,768]{1,0:T(8,128)(2,1)} %get-tuple-element.130), channel_id=1, source_target_pairs={{0,8},{8,0},{1,9},{9,1},{2,10},{10,2},{3,11},{11,3},{4,12},{12,4},... | collective-permute-start | bytes 3538952 | tf_op jit(solution)/shard_map/cond/branch_1_fun/ppermute | solution.py:670
  79.7 1.6 copy-start
  79.8 19.9 %collective-permute-start.20 = (bf16[512,768]{1,0:T(8,128)(2,1)}, bf16[512,768]{1,0:T(8,128)(2,1)S(1)}, u32[]{:S(2)}, u32[]{:S(2)}) collective-permute-start(bf16[512,768]{1,0:T(8,128)(2,1)} %copy-done.23), channel_id=1, source_target_pairs={{0,16},{16,0},{1,17},{17,1},{2,18},{18,2},{3,19},{19,3},{4,20},{20... | collective-permute-start | bytes 2359304 | tf_op jit(solution)/shard_map/ppermute | solution.py:673
  81.3 1.9 copy-start.2
  83.2 1.3 copy-start.6
  99.6 20.6 %collective-permute-start.9 = (bf16[512,768]{1,0:T(8,128)(2,1)}, bf16[512,768]{1,0:T(8,128)(2,1)}, u32[]{:S(2)}, u32[]{:S(2)}) collective-permute-start(bf16[512,768]{1,0:T(8,128)(2,1)} %get-tuple-element.202), channel_id=1, source_target_pairs={{0,16},{16,0},{1,17},{17,1},{2,18},{18,2},{3,19},{19,3},{4,20},{20... | collective-permute-start | bytes 2359304 | tf_op jit(solution)/shard_map/cond/branch_1_fun/ppermute | solution.py:673
  101.1 0.9 copy-start.22
  102.0 12.7 %copy-start.25 = (bf16[512,384]{1,0:T(8,128)(2,1)S(1)}, bf16[512,384]{1,0:T(8,128)(2,1)}, u32[]{:S(2)}) copy-start(bf16[512,384]{1,0:T(8,128)(2,1)} %get-tuple-element.149.refs_6_) | copy-start | bytes 1179652 | tf_op jit(solution)/shard_map/cond/branch_1_fun/cond
  102.0 12.7 %copy-start.26 = (bf16[512,1152]{1,0:T(8,128)(2,1)S(1)}, bf16[512,1152]{1,0:T(8,128)(2,1)}, u32[]{:S(2)}) copy-start(bf16[512,1152]{1,0:T(8,128)(2,1)} %get-tuple-element.145.refs_2_) | copy-start | bytes 3538948 | tf_op jit(solution)/shard_map/cond/branch_1_fun/cond
  102.0 12.7 %copy-start.28 = (bf16[512,768]{1,0:T(8,128)(2,1)S(1)}, bf16[512,768]{1,0:T(8,128)(2,1)}, u32[]{:S(2)}) copy-start(bf16[512,768]{1,0:T(8,128)(2,1)} %get-tuple-element.143.refs_0_) | copy-start | bytes 2359300 | tf_op jit(solution)/shard_map/cond/branch_1_fun/cond
  102.0 12.7 %copy-start.29 = (bf16[512,768]{1,0:T(8,128)(2,1)S(1)}, bf16[512,768]{1,0:T(8,128)(2,1)}, u32[]{:S(2)}) copy-start(bf16[512,768]{1,0:T(8,128)(2,1)} %get-tuple-element.144.refs_1_) | copy-start | bytes 2359300 | tf_op jit(solution)/shard_map/cond/branch_1_fun/cond
  102.0 12.7 %copy-start.30 = (bf16[512,768]{1,0:T(8,128)(2,1)S(1)}, bf16[512,768]{1,0:T(8,128)(2,1)}, u32[]{:S(2)}) copy-start(bf16[512,768]{1,0:T(8,128)(2,1)} %get-tuple-element.147.refs_4_) | copy-start | bytes 2359300 | tf_op jit(solution)/shard_map/cond/branch_1_fun/cond
  120.2 2.9 %copy-start.19 = (bf16[768,768]{1,0:T(8,128)(2,1)S(1)}, bf16[768,768]{1,0:T(8,128)(2,1)}, u32[]{:S(2)}) copy-start(bf16[768,768]{1,0:T(8,128)(2,1)} %get-tuple-element.205.refs_0_) | copy-start | bytes 3538948 | tf_op jit(solution)/shard_map/cond
  120.2 2.9 %collective-permute-start.10 = (bf16[768,768]{1,0:T(8,128)(2,1)S(1)}, bf16[768,768]{1,0:T(8,128)(2,1)S(1)}, u32[]{:S(2)}, u32[]{:S(2)}) collective-permute-start(bf16[768,768]{1,0:T(8,128)(2,1)S(1)} %get-tuple-element.206), channel_id=1, source_target_pairs={{0,8},{8,0},{1,9},{9,1},{2,10},{10,2},{3,11},{11,3},{4,12},{12,4},... | collective-permute-start | bytes 3538952 | tf_op jit(solution)/shard_map/cond/branch_1_fun/ppermute | solution.py:670
  123.4 1.0 copy-start.9
  124.4 55.4 %all-to-all-start = ((bf16[8,96,768]{2,1,0:T(8,128)(2,1)}), bf16[8,96,768]{2,1,0:T(8,128)(2,1)S(1)}, u32[]{:S(2)}, u32[]{:S(2)}) async-start(bf16[8,96,768]{2,1,0:T(8,128)(2,1)} %bitcast.21), calls=%async_computation | async-start | bytes 2359296 | tf_op jit(solution)/shard_map/cond/branch_1_fun/all_to_all | solution.py:676
  130.3 19.4 %copy-start.16 = (f32[512,768]{1,0:T(8,128)S(1)}, f32[512,768]{1,0:T(8,128)}, u32[]{:S(2)}) copy-start(f32[512,768]{1,0:T(8,128)} %get-tuple-element.166.refs_3_) | copy-start | bytes 4718596 | tf_op jit(solution)/shard_map/cond/branch_1_fun/cond
  130.3 19.4 %collective-permute-start.2 = (bf16[512,768]{1,0:T(8,128)(2,1)S(1)}, bf16[512,768]{1,0:T(8,128)(2,1)S(1)}, u32[]{:S(2)}, u32[]{:S(2)}) collective-permute-start(bf16[512,768]{1,0:T(8,128)(2,1)S(1)} %get-tuple-element.168.refs_5_), channel_id=1, source_target_pairs={{0,16},{16,0},{1,17},{17,1},{2,18},{18,2},{3,19},{19,3},{4,20},{20... | collective-permute-start | bytes 2359304 | tf_op jit(solution)/shard_map/cond/branch_1_fun/cond/branch_1_fun/ppermute | solution.py:673
  156.5 5.9 %copy-start.32 = (f32[3,2,1024]{2,1,0:T(2,128)S(1)}, f32[3,2,1024]{2,1,0:T(2,128)}, u32[]{:S(2)}) copy-start(f32[3,2,1024]{2,1,0:T(2,128)} %get-tuple-element.175) | copy-start | bytes 73732 | tf_op jit(solution)/shard_map/cond/branch_1_fun/cond
  156.5 5.9 %copy-start.33 = (f32[3,2,1024]{2,1,0:T(2,128)S(1)}, f32[3,2,1024]{2,1,0:T(2,128)}, u32[]{:S(2)}) copy-start(f32[3,2,1024]{2,1,0:T(2,128)} %get-tuple-element.174) | copy-start | bytes 73732 | tf_op jit(solution)/shard_map/cond/branch_1_fun/cond
  156.5 22.0 %collective-permute-start.7 = (f32[1024,768]{1,0:T(8,128)}, f32[1024,768]{1,0:T(8,128)}, u32[]{:S(2)}, u32[]{:S(2)}) collective-permute-start(f32[1024,768]{1,0:T(8,128)} %get-tuple-element.177), channel_id=1, source_target_pairs={{0,8},{8,0},{1,9},{9,1},{2,10},{10,2},{3,11},{11,3},{4,12},{12,4},... | collective-permute-start | bytes 9437192 | tf_op jit(solution)/shard_map/cond/branch_1_fun/cond/branch_1_fun/ppermute | solution.py:670
  156.5 22.0 %collective-permute-start.8 = (bf16[512,768]{1,0:T(8,128)(2,1)}, bf16[512,768]{1,0:T(8,128)(2,1)}, u32[]{:S(2)}, u32[]{:S(2)}) collective-permute-start(bf16[512,768]{1,0:T(8,128)(2,1)} %get-tuple-element.457), channel_id=1, source_target_pairs={{0,16},{16,0},{1,17},{17,1},{2,18},{18,2},{3,19},{19,3},{4,20},{20... | collective-permute-start | bytes 2359304 | tf_op jit(solution)/shard_map/cond/branch_1_fun/cond/branch_1_fun/ppermute | solution.py:673
  157.2 6.5 %copy-start.34 = (f32[1,768]{1,0:T(1,128)S(1)}, f32[1,768]{1,0:T(1,128)}, u32[]{:S(2)}) copy-start(f32[1,768]{1,0:T(1,128)} %get-tuple-element.173) | copy-start | bytes 9220 | tf_op jit(solution)/shard_map/cond/branch_1_fun/cond
  157.2 6.5 %copy-start.35 = (f32[1,768]{1,0:T(1,128)S(1)}, f32[1,768]{1,0:T(1,128)}, u32[]{:S(2)}) copy-start(f32[1,768]{1,0:T(1,128)} %get-tuple-element.172) | copy-start | bytes 9220 | tf_op jit(solution)/shard_map/cond/branch_1_fun/cond
  163.7 1.2 collective-permute-start.3
  165.0 3.7 %collective-permute-start.4 = (f32[1632]{0:T(1024)S(1)}, f32[1632]{0:T(1024)S(1)}, u32[]{:S(2)}, u32[]{:S(2)}) collective-permute-start(f32[1632]{0:T(1024)S(1)} %maximum_add_fusion), channel_id=1, source_target_pairs={{0,1},{1,0},{2,3},{3,2},{4,5},{5,4},{6,7},{7,6},{8,9},{9,8},{10,11... | collective-permute-start | bytes 19592 | tf_op jit(solution)/shard_map/cond/branch_1_fun/cond/branch_1_fun/ppermute | solution.py:778
  168.6 3.7 %collective-permute-start.5 = (f32[1632]{0:T(1024)S(1)}, f32[1632]{0:T(1024)S(1)}, u32[]{:S(2)}, u32[]{:S(2)}) collective-permute-start(f32[1632]{0:T(1024)S(1)} %add.19), channel_id=1, source_target_pairs={{0,2},{1,3},{2,0},{3,1},{4,6},{5,7},{6,4},{7,5},{8,10},{9,11},{10,... | collective-permute-start | bytes 19592 | tf_op jit(solution)/shard_map/cond/branch_1_fun/cond/branch_1_fun/ppermute | solution.py:778
  172.3 4.8 %collective-permute-start.6 = (f32[1632]{0:T(1024)S(1)}, f32[1632]{0:T(1024)S(1)}, u32[]{:S(2)}, u32[]{:S(2)}) collective-permute-start(f32[1632]{0:T(1024)S(1)} %add.20), channel_id=1, source_target_pairs={{0,4},{1,5},{2,6},{3,7},{4,0},{5,1},{6,2},{7,3},{8,12},{9,13},{10,... | collective-permute-start | bytes 19592 | tf_op jit(solution)/shard_map/cond/branch_1_fun/cond/branch_1_fun/ppermute | solution.py:778
  183.3 30.1 %collective-permute-start.21 = (bf16[512,768]{1,0:T(8,128)(2,1)}, bf16[512,768]{1,0:T(8,128)(2,1)S(1)}, u32[]{:S(2)}, u32[]{:S(2)}) collective-permute-start(bf16[512,768]{1,0:T(8,128)(2,1)} %get-tuple-element.360.refs_3_), channel_id=1, source_target_pairs={{0,16},{16,0},{1,17},{17,1},{2,18},{18,2},{3,19},{19,3},{4,20},{20... | collective-permute-start | bytes 2359304 | tf_op jit(solution)/shard_map/ppermute | solution.py:673
  184.6 41.4 %all-to-all-start.1 = ((bf16[8,96,768]{2,1,0:T(8,128)(2,1)}), bf16[8,96,768]{2,1,0:T(8,128)(2,1)S(1)}, u32[]{:S(2)}, u32[]{:S(2)}) async-start(bf16[8,96,768]{2,1,0:T(8,128)(2,1)} %bitcast.23), calls=%async_computation.1 | async-start | bytes 2359296 | tf_op jit(solution)/shard_map/all_to_all | solution.py:676
  208.3 1.3 copy-start.7
  209.6 1.3 copy-start.8
  210.9 2.5 %copy-start.15 = (f32[512,768]{1,0:T(8,128)S(1)}, f32[512,768]{1,0:T(8,128)}, u32[]{:S(2)}) copy-start(f32[512,768]{1,0:T(8,128)} %get-tuple-element.338.refs_1_) | copy-start | bytes 4718596
  216.6 3.4 %collective-permute-start.22 = (bf16[1024,768]{1,0:T(8,128)(2,1)S(1)}, bf16[1024,768]{1,0:T(8,128)(2,1)S(1)}, u32[]{:S(2)}, u32[]{:S(2)}) collective-permute-start(bf16[1024,768]{1,0:T(8,128)(2,1)S(1)} %get-tuple-element.364), channel_id=1, source_target_pairs={{0,8},{8,0},{1,9},{9,1},{2,10},{10,2},{3,11},{11,3},{4,12},{12,4},... | collective-permute-start | bytes 4718600 | tf_op jit(solution)/shard_map/ppermute | solution.py:670
Sparse Core Ops, SparseCore 0:
  79.9 128.4 all-reduce.3

commit v6 on v4

--- a/solution.py
+++ b/solution.py
@@ -626,13 +626,18 @@
     )
 
 
-def sum_kernel(got_ref, out_ref):
+def sum_kernel(got_ref, out_ref, total_ref):
     rows = out_ref.shape[0]
     parts = got_ref.shape[0] // rows
-    total = got_ref[:rows, :].astype(F32)
-    for i in range(1, parts):
-        total = total + got_ref[i * rows : (i + 1) * rows, :].astype(F32)
-    out_ref[...] = total.astype(BF16)
+
+    @pl.when(pl.program_id(0) == 0)
+    def _():
+        total = got_ref[:rows, :].astype(F32)
+        for i in range(1, parts):
+            total = total + got_ref[i * rows : (i + 1) * rows, :].astype(F32)
+        total_ref[...] = total.astype(BF16)
+
+    out_ref[...] = total_ref[...]
 
 
 def sum_parts(token, got, dp):
@@ -650,6 +655,7 @@
         [shape_of((dp * rows, width), BF16)],
         [pl.BlockSpec((rows, width), lambda i: (i, 0))],
         grid=(dp,),
+        scratch=[pltpu.VMEM((rows, width), BF16)],
     )
 
 

time: 236 us -> 236 us (level)
  transfers between devices with their start and end apart: 26 -> 26, of which waited for: 15 -> 15; matrix products, arithmetic and copies ran while one was open for 5% -> 5% of each run, Pallas kernels for 44% -> 43%
where the time goes in v6:
time: 236 us; the launch traced here: 235 us
  Pallas kernels  107 us (45%)
  waiting for transfers between devices  58.5 us (25%)
  starting transfers between devices  33.6 us (14%)
  local copies, waits for them, and re-layouts  19 us (8%)
  between operations  14.3 us (6%)
    pallas_call x30, Pallas kernels, call(): pl.pallas_call(body, grid=grid, in_specs=[anywhere] + list(in_specs), out...  107 us
    ppermute x9, waiting for transfers between devices, from_x(): return lax.ppermute(v, 'x', [(0, 1), (1, 0)])  22.3 us
    ppermute x9, starting transfers between devices, from_x(): return lax.ppermute(v, 'x', [(0, 1), (1, 0)])  13.9 us
    ppermute x11, waiting for transfers between devices, from_core(): return lax.ppermute(v, 'core', [(0, 1), (1, 0)])  13.3 us
    all_to_all x2, starting transfers between devices, spread(): return lax.all_to_all(v, 'dp', 0, 0, tiled=True)  11.6 us
    psum x1, waiting for transfers between devices, per_device(): gback, gin = lax.psum((gback, gin), 'dp')  10.2 us
    all_to_all x2, waiting for transfers between devices, spread(): return lax.all_to_all(v, 'dp', 0, 0, tiled=True)  8.65 us
    unnamed x48, local copies, waits for them, and re-layouts  6.84 us
  transfers between devices with their start and end apart: 26, of which 15 were waited for; matrix products, arithmetic and copies ran while one was open for 5% of the time, Pallas kernels for 43%

profile of v6, /device:TPU:0, one launch (start us, length us, event | category | flops | bytes accessed | tf_op | source)
XLA Modules:
  0.0 235.4 jit_solution(7814927270614049038)
XLA Ops:
  7.3 1.4 fusion.3.refs_3_
  8.7 0.5 collective-permute-start.11
  9.8 2.6 %collective-permute-start.12 = (bf16[192,768]{1,0:T(8,128)(2,1)S(1)}, bf16[192,768]{1,0:T(8,128)(2,1)S(1)}, u32[]{:S(2)}, u32[]{:S(2)}) collective-permute-start(bf16[192,768]{1,0:T(8,128)(2,1)S(1)} %copy-done.14), channel_id=1, source_target_pairs={{0,16},{16,0},{1,17},{17,1},{2,18},{18,2},{3,19},{19,3},{4,20},{20... | collective-permute-start | bytes 884744 | tf_op jit(solution)/shard_map/ppermute | solution.py:679
  12.7 9.0 %attn_fwd.2 = (f32[8,128]{1,0:T(8,128)S(1)}, bf16[1152,768]{1,0:T(8,128)(2,1)S(1)}, f32[6,1024]{1,0:T(8,128)S(1)}, bf16[512,768]{1,0:T(8,128)(2,1)}, bf16[512,11...) custom-call(f32[8,128]{1,0:T(8,128)S(1)} %broadcast_39_token_ref.2.t, ...), custom_call_target="tpu_custom_call", output_to_operand_aliasing={{0}: (0, {})} | custom-call | tf_op jit(solution)/shard_map/attn_fwd/pallas_call | solution.py:52
  21.7 2.9 %collective-permute-start.13 = (bf16[512,384]{1,0:T(8,128)(2,1)S(1)}, bf16[512,384]{1,0:T(8,128)(2,1)S(1)}, u32[]{:S(2)}, u32[]{:S(2)}) collective-permute-start(bf16[512,384]{1,0:T(8,128)(2,1)S(1)} %get-tuple-element.311.refs_1_), channel_id=1, source_target_pairs={{0,16},{16,0},{1,17},{17,1},{2,18},{18,2},{3,19},{19,3},{4,20},{20... | collective-permute-start | bytes 1179656 | tf_op jit(solution)/shard_map/ppermute | solution.py:679
  24.6 8.4 %attn_fwd.3 = (f32[8,128]{1,0:T(8,128)S(1)}, bf16[512,768]{1,0:T(8,128)(2,1)}, bf16[512,1152]{1,0:T(8,128)(2,1)}, bf16[6,512,512]{2,1,0:T(8,128)(2,1)}, bf16[512,384]{1,0:T(8,128)(2,1)S(1)}) custom-call(f32[8,128]{1,0:T(8,128)S(1)} %get-tuple-element.307.token_ref, s32[4]{0:T(128)S(1)} %copy-done.10, ...), custom_call_target="tpu_custom_call", output_to_operand_aliasing={{0}: (0, {})} | custom-call | tf_op jit(solution)/shard_map/attn_fwd/pallas_call | solution.py:52
  33.3 1.5 collective-permute-done.15.refs_6_
  34.8 0.7 copy-done.28
  35.6 16.3 %ffn.2 = (f32[8,128]{1,0:T(8,128)S(1)}, f32[512,768]{1,0:T(8,128)}, bf16[512,768]{1,0:T(8,128)(2,1)}, bf16[512,768]{1,0:T(8,128)(2,1)}, bf16[768,768]{1,0:T(8,12...) custom-call(f32[8,128]{1,0:T(8,128)S(1)} %get-tuple-element.310.toke, ...), custom_call_target="tpu_custom_call", output_to_operand_aliasing={{0}: (0, {})} | custom-call | tf_op jit(solution)/shard_map/ffn/pallas_call | solution.py:52
  52.0 2.0 collective-permute-start.19
  54.0 17.4 %ffn.3 = (f32[8,128]{1,0:T(8,128)S(1)}, f32[512,768]{1,0:T(8,128)}, bf16[512,768]{1,0:T(8,128)(2,1)S(1)}, bf16[512,768]{1,0:T(8,128)(2,1)}, bf16[768,768]{1,0:T(...) custom-call(f32[8,128]{1,0:T(8,128)S(1)} %get-tuple-element.316.toke, ...), custom_call_target="tpu_custom_call", output_to_operand_aliasing={{0}: (0, {})} | custom-call | tf_op jit(solution)/shard_map/ffn/pallas_call | solution.py:52
  71.4 0.6 collective-permute-done.19.refs_0_.refs_2_
  72.3 7.6 %conditional.4 = ((f32[8,128]{1,0:T(8,128)S(1)}, bf16[768,768]{1,0:T(8,128)(2,1)}, bf16[768,768]{1,0:T(8,128)(2,1)})) conditional(s32[]{:T(128)} %convert_element_type.14, () %tuple.40, (bf16[768,768]{1,0:T(8,128)(2,1)}, bf16[768,768]{1,0:T(8,128)(2,1)}, f32[8,128]{1,0:T(8,128)S(1)}, bf16[768,768]{1,0:T(8,128)(2,1)}, bf16[768,768]{1,0:T(8,128)(2,1)}) %tuple.41), branch_computations={%region_0.1_spmd, %region_1.2_spmd} | conditional | bytes 9437272 | solution.py:664
  72.3 0.5 collective-permute-start.1
  72.8 2.5 %collective-permute-done.refs_1_ = bf16[768,768]{1,0:T(8,128)(2,1)S(1)} collective-permute-done((bf16[768,768]{1,0:T(8,128)(2,1)}, bf16[768,768]{1,0:T(8,128)(2,1)S(1)}, u32[]{:S(2)}, u32[]{:S(2)}) %collective-permute-start) | collective-permute-done | bytes 1179680 | tf_op jit(solution)/shard_map/cond/branch_1_fun/ppermute | solution.py:676
  75.3 1.7 collective-permute-done.1.refs_3_
  77.0 2.8 %sum_core.2 = (f32[8,128]{1,0:T(8,128)S(1)}, bf16[768,768]{1,0:T(8,128)(2,1)}, bf16[768,768]{1,0:T(8,128)(2,1)}) custom-call(f32[8,128]{1,0:T(8,128)S(1)} %get-tuple-element.126.token_ref, bf16[768,768]{1,0:T(8,128)(2,1)} %get-tuple-element.127.refs_0_, bf16[768,768]{1,0:T(8,128)(2,1)S(1)} %collective-permute-done.refs_1_, ...), custom_call_target="tpu_custom_call", output_to_operand_aliasing={{0}: (0, {})} | custom-call | tf_op jit(solution)/shard_map/cond/branch_1_fun/sum_core/pallas_call | solution.py:52
  79.9 1.5 collective-permute-start.20
  81.4 1.9 copy-done.2
  83.3 1.3 copy-done.6
  84.6 11.7 %attn_bwd.3 = (f32[8,128]{1,0:T(8,128)S(1)}, f32[512,768]{1,0:T(8,128)}, bf16[512,768]{1,0:T(8,128)(2,1)}, f32[1,768]{1,0:T(1,128)}, bf16[512,1152]{1,0:T(8,128)...) custom-call(f32[8,128]{1,0:T(8,128)S(1)} %get-tuple-element.329.token_ref, ...), custom_call_target="tpu_custom_call", output_to_operand_aliasing={{0}: (0, {})} | custom-call | tf_op jit(solution)/shard_map/attn_bwd/pallas_call | solution.py:52
  96.3 3.5 %collective-permute-done.20.refs_0_ = bf16[512,768]{1,0:T(8,128)(2,1)S(1)} collective-permute-done((bf16[512,768]{1,0:T(8,128)(2,1)}, bf16[512,768]{1,0:T(8,128)(2,1)S(1)}, u32[]{:S(2)}, u32[]{:S(2)}) %collective-permute-start.20) | collective-permute-done | bytes 786464 | tf_op jit(solution)/shard_map/ppermute | solution.py:679
  99.8 88.0 %conditional.5 = (f32[8,128]{1,0:T(8,128)S(1)}, bf16[768,768]{1,0:T(8,128)(2,1)}, f32[2048,768]{1,0:T(8,128)}, f32[768]{0:T(1024)}, f32[768]{0:T(1024)}, /*index...) conditional(s32[]{:T(128)} %convert_element_type.14, () %tuple.39, ...), branch_computations={%region_2.3_spmd, %region_3.8_spmd} | conditional | flops 2414081 | bytes 73890032 | solution.py:664
  99.8 0.9 copy-done.21
  100.6 1.5 collective-permute-start.9
  102.1 18.1 %conditional = (f32[8,128]{1,0:T(8,128)S(1)}, f32[512,768]{1,0:T(8,128)}, f32[1,768]{1,0:T(1,128)}, bf16[512,768]{1,0:T(8,128)(2,1)}, f32[3,2,1024]{2,1,0:T(2,12...) conditional(s32[]{:T(128)} %convert_element_type.1, () %tuple.29, (f32[8,128]{1,0:T(8,128)S(1)}, ...), branch_computations={%region_4.4_spmd, %region_5.5_spmd} | conditional | bytes 17301728 | solution.py:664
  102.2 12.9 %attn_bwd.2 = (f32[8,128]{1,0:T(8,128)S(1)}, f32[512,768]{1,0:T(8,128)}, bf16[512,768]{1,0:T(8,128)(2,1)S(1)}, f32[1,768]{1,0:T(1,128)}, bf16[512,1152]{1,0:T(8,...) custom-call(f32[8,128]{1,0:T(8,128)S(1)} %get-tuple-element.131.token_ref, ...), custom_call_target="tpu_custom_call", output_to_operand_aliasing={{0}: (0, {})} | custom-call | tf_op jit(solution)/shard_map/cond/branch_1_fun/cond/branch_1_fun/attn_bwd/pallas_call | solution.py:52
  115.1 5.1 %grad_attn.1 = (f32[8,128]{1,0:T(8,128)S(1)}, bf16[768,768]{1,0:T(8,128)(2,1)}, bf16[768,768]{1,0:T(8,128)(2,1)}) custom-call(f32[8,128]{1,0:T(8,128)S(1)} %get-tuple-element.142.token_ref, bf16[512,768]{1,0:T(8,128)(2,1)S(1)} %copy-done.29, bf16[512,768]{1,0:T(8,128)(2,1)S(1)} %copy-done.30, ...), custom_call_target="tpu_custom_call", output_to_operand_aliasing={{0}: (0, {})} | custom-call | tf_op jit(solution)/shard_map/cond/branch_1_fun/cond/branch_1_fun/grad_attn/pallas_call | solution.py:52
  120.3 3.0 %collective-permute-done.10.refs_1_ = bf16[768,768]{1,0:T(8,128)(2,1)S(1)} collective-permute-done((bf16[768,768]{1,0:T(8,128)(2,1)}, bf16[768,768]{1,0:T(8,128)(2,1)S(1)}, u32[]{:S(2)}, u32[]{:S(2)}) %collective-permute-start.10) | collective-permute-done | bytes 1179680 | tf_op jit(solution)/shard_map/cond/branch_1_fun/ppermute | solution.py:676
  123.6 1.0 copy-done.9
  124.7 6.0 %all-to-all-start = ((bf16[8,96,768]{2,1,0:T(8,128)(2,1)}), bf16[8,96,768]{2,1,0:T(8,128)(2,1)S(1)}, u32[]{:S(2)}, u32[]{:S(2)}) async-start(bf16[8,96,768]{2,1,0:T(8,128)(2,1)} %bitcast.21), calls=%async_computation | async-start | bytes 2359296 | tf_op jit(solution)/shard_map/cond/branch_1_fun/all_to_all | solution.py:682
  130.7 52.9 %conditional.1 = (f32[8,128]{1,0:T(8,128)S(1)}, f32[2048,768]{1,0:T(8,128)}, f32[768]{0:T(1024)}, f32[768]{0:T(1024)}, f32[32,3]{1,0:T(8,128)}, /*index=5*/bf16[...) conditional(s32[]{:T(128)} %convert_element_type.1, () %tuple.28, (f32[8,128]{1,0:T(8,128)S(1)}, ...), branch_computations={%region_6.6_spmd, %region_7.7_spmd} | conditional | flops 2414080 | bytes 29455080 | solution.py:664
  130.7 1.1 collective-permute-start.2
  131.8 18.2 %collective-permute-done.2.refs_7_ = bf16[512,768]{1,0:T(8,128)(2,1)S(1)} collective-permute-done((bf16[512,768]{1,0:T(8,128)(2,1)S(1)}, bf16[512,768]{1,0:T(8,128)(2,1)S(1)}, u32[]{:S(2)}, u32[]{:S(2)}) %collective-permute-start.2) | collective-permute-done | bytes 786464 | tf_op jit(solution)/shard_map/cond/branch_1_fun/cond/branch_1_fun/ppermute | solution.py:679
  150.1 6.9 %grad_input.1 = (f32[8,128]{1,0:T(8,128)S(1)}, f32[2048,768]{1,0:T(8,128)}, f32[1024,768]{1,0:T(8,128)}, f32[1,768]{1,0:T(1,128)S(1)}) custom-call(f32[8,128]{1,0:T(8,128)S(1)} %get-tuple-element.162.token_ref, bf16[2048,768]{1,0:T(8,128)(2,1)} %get-tuple-element.163.refs_0_, ...), custom_call_target="tpu_custom_call", output_to_operand_aliasing={{0}: (0, {})} | custom-call | tf_op jit(solution)/shard_map/cond/branch_1_fun/cond/branch_1_fun/grad_input/pallas_call | solution.py:52
  157.0 1.1 collective-permute-start.8
  158.1 2.6 %copy.65 = s32[512,512]{0,1:T(8,128)} copy(s32[512,512]{1,0:T(8,128)} %get-tuple-element.415) | data formatting | bytes 2097152 | tf_op jit(solution)/shard_map
  160.7 0.7 slice.38
  161.4 0.7 slice.40
  162.1 1.2 slice.39
  163.4 0.7 pad_add_fusion
  164.9 0.9 collective-permute-done.3
  165.9 1.7 collective-permute-start.4
  167.6 2.0 collective-permute-done.4
  169.5 1.7 collective-permute-start.5
  171.2 2.0 collective-permute-done.5
  173.2 2.6 %collective-permute-start.6 = (f32[1632]{0:T(1024)S(1)}, f32[1632]{0:T(1024)S(1)}, u32[]{:S(2)}, u32[]{:S(2)}) collective-permute-start(f32[1632]{0:T(1024)S(1)} %add.20), channel_id=1, source_target_pairs={{0,4},{1,5},{2,6},{3,7},{4,0},{5,1},{6,2},{7,3},{8,12},{9,13},{10,... | collective-permute-start | bytes 19592 | tf_op jit(solution)/shard_map/cond/branch_1_fun/cond/branch_1_fun/ppermute | solution.py:784
  175.8 2.1 copy.113
  178.0 0.7 copy.62
  178.7 0.6 fusion.4
  179.3 4.2 %place.2 = (f32[8,128]{1,0:T(8,128)S(1)}, f32[2048,768]{1,0:T(8,128)}) custom-call(f32[8,128]{1,0:T(8,128)S(1)} %need.6.token_ref, f32[2048,768]{1,0:T(8,128)} %get-tuple-element.177.refs_0_, f32[1024,768]{1,0:T(8,128)} %collective-permute-done.7.refs_1_), custom_call_target="tpu_custom_call", output_to_operand_aliasing={{0}: (0, {}), {1}: (1, {})} | custom-call | tf_op jit(solution)/shard_map/cond/branch_1_fun/cond/branch_1_fun/place/pallas_call | solution.py:52
  183.5 1.4 copy.67
  184.9 2.9 %sum_parts.1 = (f32[8,128]{1,0:T(8,128)S(1)}, bf16[768,768]{1,0:T(8,128)(2,1)}) custom-call(f32[8,128]{1,0:T(8,128)S(1)} %get-tuple-element.221.token_ref, bf16[768,768]{1,0:T(8,128)(2,1)S(1)} %bitcast.20), custom_call_target="tpu_custom_call", output_to_operand_aliasing={{0}: (0, {})} | custom-call | tf_op jit(solution)/shard_map/cond/branch_1_fun/sum_parts/pallas_call | solution.py:52
  187.8 1.1 collective-permute-start.21
  188.8 5.7 %all-to-all-start.1 = ((bf16[8,96,768]{2,1,0:T(8,128)(2,1)}), bf16[8,96,768]{2,1,0:T(8,128)(2,1)S(1)}, u32[]{:S(2)}, u32[]{:S(2)}) async-start(bf16[8,96,768]{2,1,0:T(8,128)(2,1)} %bitcast.10), calls=%async_computation.1 | async-start | bytes 2359296 | tf_op jit(solution)/shard_map/all_to_all | solution.py:682
  194.5 10.2 %all-reduce.4.cloned.1.call-done = (bf16[768,768]{1,0:T(8,128)(2,1)}, bf16[768,768]{1,0:T(8,128)(2,1)}) async-done(((bf16[768,768]{1,0:T(8,128)(2,1)}, bf16[768,768]{1,0:T(8,128)(2,1)}), (bf16[768,768]{1,0:T(8,128)(2,1)}, bf16[768,768]{1,0:T(8,128)(2,1)})) %all-reduce.4.cloned.1.call-update) | async-done | bytes 2359312 | tf_op jit(solution)/shard_map/psum | solution.py:731
  204.7 1.3 copy-done.7
  206.0 1.3 copy-done.8
  207.2 2.5 %widen.1 = (f32[8,128]{1,0:T(8,128)S(1)}, f32[768,768]{1,0:T(8,128)}, f32[768,768]{1,0:T(8,128)}) custom-call(f32[8,128]{1,0:T(8,128)S(1)} %get-tuple-element.350.token_ref, bf16[768,768]{1,0:T(8,128)(2,1)S(1)} %copy-done.7, bf16[768,768]{1,0:T(8,128)(2,1)S(1)} %copy-done.8), custom_call_target="tpu_custom_call", output_to_operand_aliasing={{0}: (0, {})} | custom-call | tf_op jit(solution)/shard_map/widen/pallas_call | solution.py:52
  209.8 3.2 %mix.1 = (f32[8,128]{1,0:T(8,128)S(1)}, bf16[2048,768]{1,0:T(8,128)(2,1)}, bf16[1024,768]{1,0:T(8,128)(2,1)S(1)}) custom-call(f32[8,128]{1,0:T(8,128)S(1)} %get-tuple-element.353.token_ref, f32[512,768]{1,0:T(8,128)S(1)} %copy-done, f32[512,768]{1,0:T(8,128)S(1)} %copy-done.16, ...), custom_call_target="tpu_custom_call", output_to_operand_aliasing={{0}: (0, {})} | custom-call | tf_op jit(solution)/shard_map/mix/pallas_call | solution.py:52
  213.0 3.4 %collective-permute-done.22.refs_1_ = bf16[1024,768]{1,0:T(8,128)(2,1)S(1)} collective-permute-done((bf16[1024,768]{1,0:T(8,128)(2,1)S(1)}, bf16[1024,768]{1,0:T(8,128)(2,1)S(1)}, u32[]{:S(2)}, u32[]{:S(2)}) %collective-permute-start.22) | collective-permute-done | bytes 1572896 | tf_op jit(solution)/shard_map/ppermute | solution.py:676
  216.4 1.7 place.3
  218.0 8.6 %all-to-all-done.1 = bf16[8,96,768]{2,1,0:T(8,128)(2,1)S(1)} async-done(((bf16[8,96,768]{2,1,0:T(8,128)(2,1)}), bf16[8,96,768]{2,1,0:T(8,128)(2,1)S(1)}, u32[]{:S(2)}, u32[]{:S(2)}) %all-to-all-start.1) | async-done | bytes 1179680 | tf_op jit(solution)/shard_map/all_to_all | solution.py:682
  226.7 1.9 widen_attn.1
  (130 shorter events, 3.0 us)
Async XLA Ops:
  7.2 2.6 %copy-start.14 = (bf16[192,768]{1,0:T(8,128)(2,1)S(1)}, bf16[192,768]{1,0:T(8,128)(2,1)}, u32[]{:S(2)}) copy-start(bf16[192,768]{1,0:T(8,128)(2,1)} %refs_5_.3) | copy-start | bytes 884740
  7.2 5.3 %copy-start.37 = (bf16[768]{0:T(1024)(128)(2,1)S(1)}, bf16[768]{0:T(1024)(128)(2,1)}, u32[]{:S(2)}) copy-start(bf16[768]{0:T(1024)(128)(2,1)} %param.23) | copy-start | bytes 4612
  7.2 5.3 %copy-start.38 = (bf16[768]{0:T(1024)(128)(2,1)S(1)}, bf16[768]{0:T(1024)(128)(2,1)}, u32[]{:S(2)}) copy-start(bf16[768]{0:T(1024)(128)(2,1)} %param.20) | copy-start | bytes 4612
  7.2 197.5 %all-reduce.4.cloned.1.call-start = ((), (), s32[]{:S(2)}) async-start(), calls=%async_computation.2 | async-start | bytes 4718592 | tf_op jit(solution)/shard_map/psum | solution.py:731
  7.3 5.4 %copy-start.10 = (s32[4]{0:T(128)S(1)}, s32[4]{0:T(128)}, u32[]{:S(2)}) copy-start(s32[4]{0:T(128)} %refs_0_.5) | copy-start | bytes 52
  7.3 5.4 %copy-start.13 = (s32[512,512]{1,0:T(8,128)S(1)}, s32[512,512]{1,0:T(8,128)}, u32[]{:S(2)}) copy-start(s32[512,512]{1,0:T(8,128)} %refs_6_.1) | copy-start | bytes 3145732
  8.7 4.0 %collective-permute-start.11 = (bf16[784,768]{1,0:T(8,128)(2,1)S(1)}, bf16[784,768]{1,0:T(8,128)(2,1)S(1)}, u32[]{:S(2)}, u32[]{:S(2)}) collective-permute-start(bf16[784,768]{1,0:T(8,128)(2,1)S(1)} %fusion.3.refs_3_), channel_id=1, source_target_pairs={{0,8},{8,0},{1,9},{9,1},{2,10},{10,2},{3,11},{11,3},{4,12},{12,4},... | collective-permute-start | bytes 3612680 | tf_op jit(solution)/shard_map/ppermute | solution.py:676
  9.2 24.0 %collective-permute-start.16 = (bf16[768,768]{1,0:T(8,128)(2,1)}, bf16[768,768]{1,0:T(8,128)(2,1)S(1)}, u32[]{:S(2)}, u32[]{:S(2)}) collective-permute-start(bf16[768,768]{1,0:T(8,128)(2,1)} %refs_9_.3), channel_id=1, source_target_pairs={{0,8},{8,0},{1,9},{9,1},{2,10},{10,2},{3,11},{11,3},{4,12},{12,4},... | collective-permute-start | bytes 3538952 | tf_op jit(solution)/shard_map/ppermute | solution.py:676
  9.3 23.9 %collective-permute-start.17 = (bf16[768,768]{1,0:T(8,128)(2,1)}, bf16[768,768]{1,0:T(8,128)(2,1)S(1)}, u32[]{:S(2)}, u32[]{:S(2)}) collective-permute-start(bf16[768,768]{1,0:T(8,128)(2,1)} %refs_11_.3), channel_id=1, source_target_pairs={{0,8},{8,0},{1,9},{9,1},{2,10},{10,2},{3,11},{11,3},{4,12},{12,4},... | collective-permute-start | bytes 3538952 | tf_op jit(solution)/shard_map/ppermute | solution.py:676
  9.8 14.9 %collective-permute-start.12 = (bf16[192,768]{1,0:T(8,128)(2,1)S(1)}, bf16[192,768]{1,0:T(8,128)(2,1)S(1)}, u32[]{:S(2)}, u32[]{:S(2)}) collective-permute-start(bf16[192,768]{1,0:T(8,128)(2,1)S(1)} %copy-done.14), channel_id=1, source_target_pairs={{0,16},{16,0},{1,17},{17,1},{2,18},{18,2},{3,19},{19,3},{4,20},{20... | collective-permute-start | bytes 884744 | tf_op jit(solution)/shard_map/ppermute | solution.py:679
  12.3 20.8 %collective-permute-start.14 = (bf16[192,768]{1,0:T(8,128)(2,1)S(1)}, bf16[192,768]{1,0:T(8,128)(2,1)S(1)}, u32[]{:S(2)}, u32[]{:S(2)}) collective-permute-start(bf16[192,768]{1,0:T(8,128)(2,1)S(1)} %copy-done.14), channel_id=1, source_target_pairs={{0,8},{8,0},{1,9},{9,1},{2,10},{10,2},{3,11},{11,3},{4,12},{12,4},... | collective-permute-start | bytes 884744 | tf_op jit(solution)/shard_map/ppermute | solution.py:676
  12.7 11.9 %copy-start.11 = (bf16[2048,768]{1,0:T(8,128)(2,1)S(1)}, bf16[2048,768]{1,0:T(8,128)(2,1)}, u32[]{:S(2)}) copy-start(bf16[2048,768]{1,0:T(8,128)(2,1)} %refs_0_.7) | copy-start | bytes 9437188
  21.7 11.3 %copy-start.1 = (bf16[6,512,512]{2,1,0:T(8,128)(2,1)}, bf16[6,512,512]{2,1,0:T(8,128)(2,1)S(1)}, u32[]{:S(2)}) copy-start(bf16[6,512,512]{2,1,0:T(8,128)(2,1)S(1)} %get-tuple-element.332.refs_9_) | copy-start | bytes 9437188
  21.7 11.3 %copy-start.5 = (bf16[512,1152]{1,0:T(8,128)(2,1)}, bf16[512,1152]{1,0:T(8,128)(2,1)S(1)}, u32[]{:S(2)}) copy-start(bf16[512,1152]{1,0:T(8,128)(2,1)S(1)} %get-tuple-element.331.refs_8_) | copy-start | bytes 3538948
  21.7 13.1 %copy-start.12 = (bf16[1152,768]{1,0:T(8,128)(2,1)}, bf16[1152,768]{1,0:T(8,128)(2,1)S(1)}, u32[]{:S(2)}) copy-start(bf16[1152,768]{1,0:T(8,128)(2,1)S(1)} %get-tuple-element.308.refs_3_.refs_7_) | copy-start | bytes 5308420
  21.7 13.1 %copy-start.23 = (bf16[512,384]{1,0:T(8,128)(2,1)}, bf16[512,384]{1,0:T(8,128)(2,1)S(1)}, u32[]{:S(2)}) copy-start(bf16[512,384]{1,0:T(8,128)(2,1)S(1)} %get-tuple-element.311.refs_1_) | copy-start | bytes 1179652
  21.7 13.1 %collective-permute-start.13 = (bf16[512,384]{1,0:T(8,128)(2,1)S(1)}, bf16[512,384]{1,0:T(8,128)(2,1)S(1)}, u32[]{:S(2)}, u32[]{:S(2)}) collective-permute-start(bf16[512,384]{1,0:T(8,128)(2,1)S(1)} %get-tuple-element.311.refs_1_), channel_id=1, source_target_pairs={{0,16},{16,0},{1,17},{17,1},{2,18},{18,2},{3,19},{19,3},{4,20},{20... | collective-permute-start | bytes 1179656 | tf_op jit(solution)/shard_map/ppermute | solution.py:679
  24.6 8.5 %copy-start.3 = (bf16[192,768]{1,0:T(8,128)(2,1)}, bf16[192,768]{1,0:T(8,128)(2,1)S(1)}, u32[]{:S(2)}) copy-start(bf16[192,768]{1,0:T(8,128)(2,1)S(1)} %get-tuple-element.312.refs_5_) | copy-start | bytes 884740
  33.0 21.0 %copy-start.25 = (bf16[512,384]{1,0:T(8,128)(2,1)}, bf16[512,384]{1,0:T(8,128)(2,1)S(1)}, u32[]{:S(2)}) copy-start(bf16[512,384]{1,0:T(8,128)(2,1)S(1)} %get-tuple-element.314.refs_1_) | copy-start | bytes 1179652
  33.0 18.9 %collective-permute-start.18 = (bf16[512,384]{1,0:T(8,128)(2,1)S(1)}, bf16[512,384]{1,0:T(8,128)(2,1)S(1)}, u32[]{:S(2)}, u32[]{:S(2)}) collective-permute-start(bf16[512,384]{1,0:T(8,128)(2,1)S(1)} %get-tuple-element.314.refs_1_), channel_id=1, source_target_pairs={{0,16},{16,0},{1,17},{17,1},{2,18},{18,2},{3,19},{19,3},{4,20},{20... | collective-permute-start | bytes 1179656 | tf_op jit(solution)/shard_map/ppermute | solution.py:679
  33.1 1.6 collective-permute-start.15
  33.2 1.6 copy-start.18
  33.2 1.5 copy-start.19
  34.8 0.8 copy-start.32
  51.9 2.1 copy-start.4
  52.0 20.1 %collective-permute-start.19 = (bf16[512,768]{1,0:T(8,128)(2,1)}, bf16[512,768]{1,0:T(8,128)(2,1)S(1)}, u32[]{:S(2)}, u32[]{:S(2)}) collective-permute-start(bf16[512,768]{1,0:T(8,128)(2,1)} %get-tuple-element.326.refs_1_), channel_id=1, source_target_pairs={{0,16},{16,0},{1,17},{17,1},{2,18},{18,2},{3,19},{19,3},{4,20},{20... | collective-permute-start | bytes 2359304 | tf_op jit(solution)/shard_map/ppermute | solution.py:679
  71.4 0.9 copy-start.22
  72.3 3.1 %collective-permute-start = (bf16[768,768]{1,0:T(8,128)(2,1)}, bf16[768,768]{1,0:T(8,128)(2,1)S(1)}, u32[]{:S(2)}, u32[]{:S(2)}) collective-permute-start(bf16[768,768]{1,0:T(8,128)(2,1)} %get-tuple-element.128), channel_id=1, source_target_pairs={{0,8},{8,0},{1,9},{9,1},{2,10},{10,2},{3,11},{11,3},{4,12},{12,4},... | collective-permute-start | bytes 3538952 | tf_op jit(solution)/shard_map/cond/branch_1_fun/ppermute | solution.py:676
  72.3 4.7 %collective-permute-start.1 = (bf16[768,768]{1,0:T(8,128)(2,1)}, bf16[768,768]{1,0:T(8,128)(2,1)S(1)}, u32[]{:S(2)}, u32[]{:S(2)}) collective-permute-start(bf16[768,768]{1,0:T(8,128)(2,1)} %get-tuple-element.130), channel_id=1, source_target_pairs={{0,8},{8,0},{1,9},{9,1},{2,10},{10,2},{3,11},{11,3},{4,12},{12,4},... | collective-permute-start | bytes 3538952 | tf_op jit(solution)/shard_map/cond/branch_1_fun/ppermute | solution.py:676
  79.9 1.6 copy-start
  79.9 19.9 %collective-permute-start.20 = (bf16[512,768]{1,0:T(8,128)(2,1)}, bf16[512,768]{1,0:T(8,128)(2,1)S(1)}, u32[]{:S(2)}, u32[]{:S(2)}) collective-permute-start(bf16[512,768]{1,0:T(8,128)(2,1)} %copy-done.22), channel_id=1, source_target_pairs={{0,16},{16,0},{1,17},{17,1},{2,18},{18,2},{3,19},{19,3},{4,20},{20... | collective-permute-start | bytes 2359304 | tf_op jit(solution)/shard_map/ppermute | solution.py:679
  81.4 1.9 copy-start.2
  83.3 1.3 copy-start.6
  99.8 0.9 copy-start.21
  100.6 19.5 %collective-permute-start.9 = (bf16[512,768]{1,0:T(8,128)(2,1)}, bf16[512,768]{1,0:T(8,128)(2,1)}, u32[]{:S(2)}, u32[]{:S(2)}) collective-permute-start(bf16[512,768]{1,0:T(8,128)(2,1)} %get-tuple-element.204), channel_id=1, source_target_pairs={{0,16},{16,0},{1,17},{17,1},{2,18},{18,2},{3,19},{19,3},{4,20},{20... | collective-permute-start | bytes 2359304 | tf_op jit(solution)/shard_map/cond/branch_1_fun/ppermute | solution.py:679
  102.1 12.9 %copy-start.24 = (bf16[512,384]{1,0:T(8,128)(2,1)S(1)}, bf16[512,384]{1,0:T(8,128)(2,1)}, u32[]{:S(2)}) copy-start(bf16[512,384]{1,0:T(8,128)(2,1)} %get-tuple-element.149.refs_6_) | copy-start | bytes 1179652 | tf_op jit(solution)/shard_map/cond/branch_1_fun/cond
  102.1 12.9 %copy-start.26 = (bf16[512,384]{1,0:T(8,128)(2,1)S(1)}, bf16[512,384]{1,0:T(8,128)(2,1)}, u32[]{:S(2)}) copy-start(bf16[512,384]{1,0:T(8,128)(2,1)} %get-tuple-element.150.refs_7_) | copy-start | bytes 1179652 | tf_op jit(solution)/shard_map/cond/branch_1_fun/cond
  102.1 12.9 %copy-start.27 = (bf16[512,1152]{1,0:T(8,128)(2,1)S(1)}, bf16[512,1152]{1,0:T(8,128)(2,1)}, u32[]{:S(2)}) copy-start(bf16[512,1152]{1,0:T(8,128)(2,1)} %get-tuple-element.145.refs_2_) | copy-start | bytes 3538948 | tf_op jit(solution)/shard_map/cond/branch_1_fun/cond
  102.1 12.9 %copy-start.29 = (bf16[512,768]{1,0:T(8,128)(2,1)S(1)}, bf16[512,768]{1,0:T(8,128)(2,1)}, u32[]{:S(2)}) copy-start(bf16[512,768]{1,0:T(8,128)(2,1)} %get-tuple-element.143.refs_0_) | copy-start | bytes 2359300 | tf_op jit(solution)/shard_map/cond/branch_1_fun/cond
  102.1 12.9 %copy-start.30 = (bf16[512,768]{1,0:T(8,128)(2,1)S(1)}, bf16[512,768]{1,0:T(8,128)(2,1)}, u32[]{:S(2)}) copy-start(bf16[512,768]{1,0:T(8,128)(2,1)} %get-tuple-element.144.refs_1_) | copy-start | bytes 2359300 | tf_op jit(solution)/shard_map/cond/branch_1_fun/cond
  102.1 12.9 %copy-start.31 = (bf16[512,768]{1,0:T(8,128)(2,1)S(1)}, bf16[512,768]{1,0:T(8,128)(2,1)}, u32[]{:S(2)}) copy-start(bf16[512,768]{1,0:T(8,128)(2,1)} %get-tuple-element.147.refs_4_) | copy-start | bytes 2359300 | tf_op jit(solution)/shard_map/cond/branch_1_fun/cond
  120.2 3.1 %copy-start.20 = (bf16[768,768]{1,0:T(8,128)(2,1)S(1)}, bf16[768,768]{1,0:T(8,128)(2,1)}, u32[]{:S(2)}) copy-start(bf16[768,768]{1,0:T(8,128)(2,1)} %get-tuple-element.207.refs_0_) | copy-start | bytes 3538948 | tf_op jit(solution)/shard_map/cond
  120.2 3.1 %collective-permute-start.10 = (bf16[768,768]{1,0:T(8,128)(2,1)}, bf16[768,768]{1,0:T(8,128)(2,1)S(1)}, u32[]{:S(2)}, u32[]{:S(2)}) collective-permute-start(bf16[768,768]{1,0:T(8,128)(2,1)} %get-tuple-element.208), channel_id=1, source_target_pairs={{0,8},{8,0},{1,9},{9,1},{2,10},{10,2},{3,11},{11,3},{4,12},{12,4},... | collective-permute-start | bytes 3538952 | tf_op jit(solution)/shard_map/cond/branch_1_fun/ppermute | solution.py:676
  123.6 1.0 copy-start.9
  124.7 6.0 %copy-start.15 = (bf16[512,768]{1,0:T(8,128)(2,1)S(1)}, bf16[512,768]{1,0:T(8,128)(2,1)}, u32[]{:S(2)}) copy-start(bf16[512,768]{1,0:T(8,128)(2,1)} %get-tuple-element.210) | copy-start | bytes 2359300 | tf_op jit(solution)/shard_map/cond
  124.7 60.2 %all-to-all-start = ((bf16[8,96,768]{2,1,0:T(8,128)(2,1)}), bf16[8,96,768]{2,1,0:T(8,128)(2,1)S(1)}, u32[]{:S(2)}, u32[]{:S(2)}) async-start(bf16[8,96,768]{2,1,0:T(8,128)(2,1)} %bitcast.21), calls=%async_computation | async-start | bytes 2359296 | tf_op jit(solution)/shard_map/cond/branch_1_fun/all_to_all | solution.py:682
  130.7 19.4 %copy-start.17 = (f32[512,768]{1,0:T(8,128)S(1)}, f32[512,768]{1,0:T(8,128)}, u32[]{:S(2)}) copy-start(f32[512,768]{1,0:T(8,128)} %get-tuple-element.166.refs_3_) | copy-start | bytes 4718596 | tf_op jit(solution)/shard_map/cond/branch_1_fun/cond
  130.7 19.4 %collective-permute-start.2 = (bf16[512,768]{1,0:T(8,128)(2,1)S(1)}, bf16[512,768]{1,0:T(8,128)(2,1)S(1)}, u32[]{:S(2)}, u32[]{:S(2)}) collective-permute-start(bf16[512,768]{1,0:T(8,128)(2,1)S(1)} %get-tuple-element.168.refs_5_), channel_id=1, source_target_pairs={{0,16},{16,0},{1,17},{17,1},{2,18},{18,2},{3,19},{19,3},{4,20},{20... | collective-permute-start | bytes 2359304 | tf_op jit(solution)/shard_map/cond/branch_1_fun/cond/branch_1_fun/ppermute | solution.py:679
  157.0 6.4 %copy-start.33 = (f32[3,2,1024]{2,1,0:T(2,128)S(1)}, f32[3,2,1024]{2,1,0:T(2,128)}, u32[]{:S(2)}) copy-start(f32[3,2,1024]{2,1,0:T(2,128)} %get-tuple-element.175) | copy-start | bytes 73732 | tf_op jit(solution)/shard_map/cond/branch_1_fun/cond
  157.0 6.4 %copy-start.34 = (f32[3,2,1024]{2,1,0:T(2,128)S(1)}, f32[3,2,1024]{2,1,0:T(2,128)}, u32[]{:S(2)}) copy-start(f32[3,2,1024]{2,1,0:T(2,128)} %get-tuple-element.174) | copy-start | bytes 73732 | tf_op jit(solution)/shard_map/cond/branch_1_fun/cond
  157.0 22.3 %collective-permute-start.7 = (f32[1024,768]{1,0:T(8,128)}, f32[1024,768]{1,0:T(8,128)}, u32[]{:S(2)}, u32[]{:S(2)}) collective-permute-start(f32[1024,768]{1,0:T(8,128)} %get-tuple-element.178), channel_id=1, source_target_pairs={{0,8},{8,0},{1,9},{9,1},{2,10},{10,2},{3,11},{11,3},{4,12},{12,4},... | collective-permute-start | bytes 9437192 | tf_op jit(solution)/shard_map/cond/branch_1_fun/cond/branch_1_fun/ppermute | solution.py:676
  157.0 26.5 %collective-permute-start.8 = (bf16[512,768]{1,0:T(8,128)(2,1)}, bf16[512,768]{1,0:T(8,128)(2,1)}, u32[]{:S(2)}, u32[]{:S(2)}) collective-permute-start(bf16[512,768]{1,0:T(8,128)(2,1)} %get-tuple-element.450), channel_id=1, source_target_pairs={{0,16},{16,0},{1,17},{17,1},{2,18},{18,2},{3,19},{19,3},{4,20},{20... | collective-permute-start | bytes 2359304 | tf_op jit(solution)/shard_map/cond/branch_1_fun/cond/branch_1_fun/ppermute | solution.py:679
  158.1 6.4 %copy-start.35 = (f32[1,768]{1,0:T(1,128)S(1)}, f32[1,768]{1,0:T(1,128)}, u32[]{:S(2)}) copy-start(f32[1,768]{1,0:T(1,128)} %get-tuple-element.173) | copy-start | bytes 9220 | tf_op jit(solution)/shard_map/cond/branch_1_fun/cond
  158.1 6.4 %copy-start.36 = (f32[1,768]{1,0:T(1,128)S(1)}, f32[1,768]{1,0:T(1,128)}, u32[]{:S(2)}) copy-start(f32[1,768]{1,0:T(1,128)} %get-tuple-element.172) | copy-start | bytes 9220 | tf_op jit(solution)/shard_map/cond/branch_1_fun/cond
  164.6 1.2 collective-permute-start.3
  165.9 3.7 %collective-permute-start.4 = (f32[1632]{0:T(1024)S(1)}, f32[1632]{0:T(1024)S(1)}, u32[]{:S(2)}, u32[]{:S(2)}) collective-permute-start(f32[1632]{0:T(1024)S(1)} %maximum_add_fusion), channel_id=1, source_target_pairs={{0,1},{1,0},{2,3},{3,2},{4,5},{5,4},{6,7},{7,6},{8,9},{9,8},{10,11... | collective-permute-start | bytes 19592 | tf_op jit(solution)/shard_map/cond/branch_1_fun/cond/branch_1_fun/ppermute | solution.py:784
  169.5 3.7 %collective-permute-start.5 = (f32[1632]{0:T(1024)S(1)}, f32[1632]{0:T(1024)S(1)}, u32[]{:S(2)}, u32[]{:S(2)}) collective-permute-start(f32[1632]{0:T(1024)S(1)} %add.19), channel_id=1, source_target_pairs={{0,2},{1,3},{2,0},{3,1},{4,6},{5,7},{6,4},{7,5},{8,10},{9,11},{10,... | collective-permute-start | bytes 19592 | tf_op jit(solution)/shard_map/cond/branch_1_fun/cond/branch_1_fun/ppermute | solution.py:784
  173.2 4.7 %collective-permute-start.6 = (f32[1632]{0:T(1024)S(1)}, f32[1632]{0:T(1024)S(1)}, u32[]{:S(2)}, u32[]{:S(2)}) collective-permute-start(f32[1632]{0:T(1024)S(1)} %add.20), channel_id=1, source_target_pairs={{0,4},{1,5},{2,6},{3,7},{4,0},{5,1},{6,2},{7,3},{8,12},{9,13},{10,... | collective-permute-start | bytes 19592 | tf_op jit(solution)/shard_map/cond/branch_1_fun/cond/branch_1_fun/ppermute | solution.py:784
  187.8 22.0 %collective-permute-start.21 = (bf16[512,768]{1,0:T(8,128)(2,1)}, bf16[512,768]{1,0:T(8,128)(2,1)S(1)}, u32[]{:S(2)}, u32[]{:S(2)}) collective-permute-start(bf16[512,768]{1,0:T(8,128)(2,1)} %get-tuple-element.355.refs_3_), channel_id=1, source_target_pairs={{0,16},{16,0},{1,17},{17,1},{2,18},{18,2},{3,19},{19,3},{4,20},{20... | collective-permute-start | bytes 2359304 | tf_op jit(solution)/shard_map/ppermute | solution.py:679
  188.8 37.9 %all-to-all-start.1 = ((bf16[8,96,768]{2,1,0:T(8,128)(2,1)}), bf16[8,96,768]{2,1,0:T(8,128)(2,1)S(1)}, u32[]{:S(2)}, u32[]{:S(2)}) async-start(bf16[8,96,768]{2,1,0:T(8,128)(2,1)} %bitcast.10), calls=%async_computation.1 | async-start | bytes 2359296 | tf_op jit(solution)/shard_map/all_to_all | solution.py:682
  204.7 1.3 copy-start.7
  206.0 1.3 copy-start.8
  207.2 2.5 %copy-start.16 = (f32[512,768]{1,0:T(8,128)S(1)}, f32[512,768]{1,0:T(8,128)}, u32[]{:S(2)}) copy-start(f32[512,768]{1,0:T(8,128)} %get-tuple-element.336.refs_1_) | copy-start | bytes 4718596
  213.0 3.4 %collective-permute-start.22 = (bf16[1024,768]{1,0:T(8,128)(2,1)S(1)}, bf16[1024,768]{1,0:T(8,128)(2,1)S(1)}, u32[]{:S(2)}, u32[]{:S(2)}) collective-permute-start(bf16[1024,768]{1,0:T(8,128)(2,1)S(1)} %get-tuple-element.359), channel_id=1, source_target_pairs={{0,8},{8,0},{1,9},{9,1},{2,10},{10,2},{3,11},{11,3},{4,12},{12,4},... | collective-permute-start | bytes 4718600 | tf_op jit(solution)/shard_map/ppermute | solution.py:676
  (1 other events, 0.7 us)
Sparse Core Ops, SparseCore 0:
  80.0 124.6 all-reduce.3
